TPU v7x, 32 devices: a whole 2x2x4 slice. The times are simulated.
32 devices in a mesh: tile: 16 (over z, x, core), head: 2 (over y).
Axes of the slice: x: 2, y: 2, z: 4, core: 2. Of those that a mesh axis runs over, the one named last changes fastest.
Arguments:
- attn_proj: bfloat16 [16, 3, 192, 3, 3072], P('tile', None, 'head')
- mlp_proj: bfloat16 [16, 3, 192, 6144], P('tile', None, 'head'), may hold values from -6 to 6
- stream: bfloat16 [16, 3, 192, 3072], P('tile', None, 'head'), may hold values from -6 to 6
- text_len: int32 [16], P('tile'), may hold values from 1 to 192, as said below
- q_gain: float32 [128], replicated
- k_gain: float32 [128], replicated
- w_out_attn: bfloat16 [3072, 3072], P('head', 'tile'), may hold values from -0.0625 to 0.0625
- w_out_mlp: bfloat16 [6144, 3072], P('head', 'tile'), may hold values from -0.0625 to 0.0625
- bias_out: float32 [3072], replicated, may hold values from -3 to 3
- gate_mod: float32 [16, 3072], P('tile'), may hold values from -4 to 4
- final_shift: float32 [16, 3072], P('tile'), may hold values from -3 to 3
- final_scale: float32 [16, 3072], P('tile'), may hold values from -3 to 3
- w_final: bfloat16 [3072, 64], replicated, may hold values from -0.109375 to 0.109375
- b_final: float32 [64], replicated, may hold values from -3 to 3
- latent: float32 [16, 2, 192, 64], P('tile', None, 'head'), may hold values from -6 to 6
- step_size: float32 [16], P('tile'), may hold values from -0.4 to -0.1
Outputs:
- hidden_out: bfloat16 [16, 3, 192, 3072], P('tile', None, 'head')
- latent_next: float32 [16, 2, 192, 64], P('tile', None, 'head')
Inputs may be any that keep to these rules, and one draw needn't show every extreme that they name: `text_len`: live text slots of each request; some request has all 192 text slots live in every draw.
All inputs are finite; a program needn't handle non-finite values.
Results may differ from a plain program's by a relative error of at most 0.0098.
Values may be sent and summed in bfloat16 or wider, within the bound.
No kernel may reach another device: no remote copies, remote signals or barrier semaphores. Data moves between devices by JAX's collectives and lax.ppermute only.
A program may use at most 128 MiB of HBM per device.

v0:
```python
import functools
import math

import jax
import jax.numpy as jnp
import numpy as np
from jax import lax
from jax.experimental import pallas as pl
from jax.experimental.pallas import tpu as pltpu
from jax.sharding import PartitionSpec as P

HEAD_DIM = 128
SLOTS = 192
GRID_W = 32


def rope_tables(positions):
    pairs_zero = HEAD_DIM // 16
    pairs_axis = (HEAD_DIM // 2 - pairs_zero) // 2
    freqs = 10000.0 ** (-jnp.arange(pairs_axis, dtype=jnp.float32) / pairs_axis)
    count = positions.shape[0]
    angles = [jnp.zeros((count, HEAD_DIM // 2), jnp.float32)]
    for block in range(1, 3):
        image_index = (block - 1) * SLOTS + positions
        rows = (image_index // GRID_W).astype(jnp.float32)
        columns = (image_index % GRID_W).astype(jnp.float32)
        angles.append(
            jnp.concatenate(
                [
                    jnp.zeros((count, pairs_zero), jnp.float32),
                    rows[:, None] * freqs[None, :],
                    columns[:, None] * freqs[None, :],
                ],
                axis=1,
            )
        )
    stacked = jnp.stack(angles)
    return (jnp.cos(stacked), jnp.sin(stacked))


def prepare(raw, gain, cosine, sine):
    normed = raw * lax.rsqrt(jnp.mean(raw * raw, axis=-1, keepdims=True) + 1e-06) * gain
    halves = normed.reshape(normed.shape[:-1] + (HEAD_DIM // 2, 2))
    first = halves[..., 0]
    second = halves[..., 1]
    cosine = cosine[None, :, :, None, :]
    sine = sine[None, :, :, None, :]
    rotated = jnp.stack([first * cosine - second * sine, first * sine + second * cosine], axis=-1)
    return rotated.reshape(raw.shape).astype(jnp.bfloat16)


def attend_head(inputs):
    queries, keys, values, live = inputs
    scores = jnp.einsum("qd,kd->qk", queries, keys, preferred_element_type=jnp.float32) / math.sqrt(
        HEAD_DIM
    )
    scores = jnp.where(live[None, :], scores, -jnp.inf)
    top = jnp.max(scores, axis=-1, keepdims=True)
    weights = jnp.exp(scores - top)
    total = jnp.sum(weights, axis=-1, keepdims=True)
    mixed = jnp.dot(weights.astype(jnp.bfloat16), values, preferred_element_type=jnp.float32)
    return (mixed / total).astype(jnp.bfloat16)


def attend_request(inputs):
    queries, keys, values, live = inputs
    count = queries.shape[1]
    broad_live = jnp.broadcast_to(live[None, :], (count, live.shape[0]))
    result = lax.map(
        attend_head,
        (
            jnp.moveaxis(queries, 1, 0),
            jnp.moveaxis(keys, 1, 0),
            jnp.moveaxis(values, 1, 0),
            broad_live,
        ),
    )
    return jnp.moveaxis(result, 0, 1)


def general(
    attn_proj,
    mlp_proj,
    stream,
    text_len,
    q_gain,
    k_gain,
    w_out_attn,
    w_out_mlp,
    bias_out,
    gate_mod,
    final_shift,
    final_scale,
    w_final,
    b_final,
    latent,
    step_size,
):
    requests = attn_proj.shape[0]
    own_slots = attn_proj.shape[2]
    width = attn_proj.shape[4]
    heads = width // HEAD_DIM
    start_slot = lax.axis_index("head") * own_slots
    positions = start_slot + jnp.arange(own_slots, dtype=jnp.int32)
    cosine, sine = rope_tables(positions)
    head_shape = (requests, 3, own_slots, heads, HEAD_DIM)
    queries = prepare(
        attn_proj[:, :, :, 0].astype(jnp.float32).reshape(head_shape), q_gain, cosine, sine
    )
    keys = prepare(
        attn_proj[:, :, :, 1].astype(jnp.float32).reshape(head_shape), k_gain, cosine, sine
    )
    packed = jnp.stack(
        [
            queries.reshape(requests, 3, own_slots, width),
            keys.reshape(requests, 3, own_slots, width),
            attn_proj[:, :, :, 2],
        ],
        axis=3,
    )
    units = mlp_proj[:, :, :, None, :]
    moved, hidden_units = (
        lax.all_to_all(packed, "head", split_axis=4, concat_axis=2, tiled=True),
        lax.all_to_all(units, "head", split_axis=4, concat_axis=2, tiled=True),
    )
    hidden_units = hidden_units[:, :, :, 0]
    tile_slots = moved.shape[2]
    local_width = moved.shape[4]
    local_heads = local_width // HEAD_DIM
    flat_shape = (requests, 3 * tile_slots, local_heads, HEAD_DIM)
    all_positions = jnp.arange(tile_slots, dtype=jnp.int32)
    text_live = all_positions[None, :] < text_len[:, None]
    image_live = jnp.ones_like(text_live)
    live = jnp.stack([text_live, image_live, image_live], axis=1).reshape(requests, 3 * tile_slots)
    attn_out = lax.map(
        attend_request,
        (
            moved[:, :, :, 0].reshape(flat_shape),
            moved[:, :, :, 1].reshape(flat_shape),
            moved[:, :, :, 2].reshape(flat_shape),
            live,
        ),
    )
    attn_out = attn_out.reshape(requests, 3, tile_slots, local_width)
    mlp_act = jax.nn.gelu(hidden_units.astype(jnp.float32), approximate=True).astype(jnp.bfloat16)
    term = jnp.einsum(
        "rbsk,kd->rbsd",
        attn_out,
        lax.all_gather(w_out_attn, "tile", axis=1, tiled=True),
        preferred_element_type=jnp.float32,
    )
    term = term + jnp.einsum(
        "rbsk,kd->rbsd",
        mlp_act,
        lax.all_gather(w_out_mlp, "tile", axis=1, tiled=True),
        preferred_element_type=jnp.float32,
    )
    proj = lax.psum_scatter(term, "head", scatter_dimension=2, tiled=True)
    updated = stream.astype(jnp.float32) + gate_mod[:, None, None, :] * (proj + bias_out)
    hidden_out = updated.astype(jnp.bfloat16)
    image = updated[:, 1:]
    center = image - jnp.mean(image, axis=-1, keepdims=True)
    variance = jnp.mean(center * center, axis=-1, keepdims=True)
    normed = center * lax.rsqrt(variance + 1e-06)
    modulated = (
        (1.0 + final_scale[:, None, None, :]) * normed + final_shift[:, None, None, :]
    ).astype(jnp.bfloat16)
    velocity = (
        jnp.einsum("rbsd,dc->rbsc", modulated, w_final, preferred_element_type=jnp.float32)
        + b_final
    )
    latent_next = latent + step_size[:, None, None, None] * velocity
    return (hidden_out, latent_next)


EPS = 1e-06
SCALE = math.log2(math.e) / math.sqrt(HEAD_DIM)
VMEM = 60 * 1024 * 1024
LESS = 34 * 1024 * 1024
NT = (((1,), (1,)), ((), ()))


def fits(sizes):
    return sizes["head"] == 2 and sizes["tile"] == 2 * len(PATH)


def tables_kernel(half_ref, len_ref, row_freq_ref, col_freq_ref, q_ref, k_ref, cq_ref, sq_ref, ck_ref, sk_ref, mask_ref, swap_ref):
    rows = cq_ref.shape[0]
    slots = rows // 6

    def place(axis, shape):
        index = lax.broadcasted_iota(jnp.int32, shape, axis)
        away = index >= rows // 2
        block = (index - jnp.where(away, rows // 2, 0)) // slots
        slot = index % slots + slots * jnp.where(away, 1 - half_ref[0], half_ref[0])
        return block, slot

    shape = (rows, HEAD_DIM)
    block, slot = place(0, shape)
    image = (block - 1) * SLOTS + slot
    angle = (image // GRID_W).astype(jnp.float32) * row_freq_ref[...]
    angle += (image % GRID_W).astype(jnp.float32) * col_freq_ref[...]
    angle = jnp.where(block == 0, 0.0, angle)
    cosine, sine = jnp.cos(angle), jnp.sin(angle)
    odd = lax.broadcasted_iota(jnp.int32, shape, 1) % 2 == 1
    for gain_ref, c_ref, s_ref in ((q_ref, cq_ref, sq_ref), (k_ref, ck_ref, sk_ref)):
        gain = jnp.broadcast_to(gain_ref[...], shape)
        partner = jnp.where(odd, pltpu.roll(gain, 1, 1), -pltpu.roll(gain, HEAD_DIM - 1, 1))
        c_ref[...] = cosine * gain
        s_ref[...] = sine * partner
    block, slot = place(1, (1, rows))
    mask_ref[...] = jnp.where((block > 0) | (slot < len_ref[0]), 0.0, -jnp.inf)
    square = (HEAD_DIM, HEAD_DIM)
    column = lax.broadcasted_iota(jnp.int32, square, 1)
    other = column + 1 - 2 * (column % 2)
    swap_ref[...] = jnp.where(lax.broadcasted_iota(jnp.int32, square, 0) == other, 1.0, 0.0).astype(jnp.bfloat16)


def make_tables(half, text_len, q_gain, k_gain, rows):
    pairs_zero = HEAD_DIM // 16
    pairs_axis = (HEAD_DIM // 2 - pairs_zero) // 2
    freqs = 10000.0 ** (-np.arange(pairs_axis, dtype=np.float32) / np.float32(pairs_axis))
    row_freq, col_freq = np.zeros((2, 1, HEAD_DIM // 2), np.float32)
    row_freq[0, pairs_zero : pairs_zero + pairs_axis] = freqs
    col_freq[0, pairs_zero + pairs_axis :] = freqs
    scalars = pl.BlockSpec(memory_space=pltpu.SMEM)
    table = jax.ShapeDtypeStruct((rows, HEAD_DIM), jnp.float32)
    return pl.pallas_call(
        tables_kernel,
        in_specs=[scalars, scalars] + [pl.BlockSpec(memory_space=pltpu.VMEM)] * 4,
        out_shape=[
            table,
            table,
            table,
            table,
            jax.ShapeDtypeStruct((1, rows), jnp.float32),
            jax.ShapeDtypeStruct((HEAD_DIM, HEAD_DIM), jnp.bfloat16),
        ],
        compiler_params=pltpu.CompilerParams(vmem_limit_bytes=VMEM),
        cost_estimate=pl.CostEstimate(flops=rows * HEAD_DIM * 8, bytes_accessed=rows * HEAD_DIM * 4, transcendentals=0),
        name="tables",
    )(
        half,
        text_len,
        np.repeat(row_freq, 2, axis=1),
        np.repeat(col_freq, 2, axis=1),
        q_gain[None, :],
        k_gain[None, :],
    )


def attend_kernel(half_ref, own_ref, far_ref, cq_ref, sq_ref, ck_ref, sk_ref, mask_ref, swap_ref, *refs):
    out_ref = refs[-1]
    rows = own_ref.shape[0] * own_ref.shape[2]

    def load(part):
        return jnp.concatenate(
            [own_ref[:, part].reshape(rows, HEAD_DIM), far_ref[:, part].reshape(rows, HEAD_DIM)], axis=0
        )

    def turn(raw, straight, crossed):
        wide = raw.astype(jnp.float32)
        scale = lax.rsqrt(jnp.mean(wide * wide, axis=-1, keepdims=True) + EPS)
        partner = jnp.dot(raw, swap_ref[...], preferred_element_type=jnp.float32)
        return ((wide * straight + partner * crossed) * scale).astype(jnp.bfloat16)

    queries = turn(load(0), cq_ref[...], sq_ref[...])
    keys = turn(load(1), ck_ref[...], sk_ref[...])
    scores = lax.dot_general(queries, keys, NT, preferred_element_type=jnp.float32)
    scores = scores * SCALE + mask_ref[...]
    weights = jnp.exp2(scores - jnp.max(scores, axis=-1, keepdims=True))
    total = jnp.sum(weights, axis=-1, keepdims=True)
    mixed = jnp.dot(weights.astype(jnp.bfloat16), load(2), preferred_element_type=jnp.float32)
    out_ref[...] = (mixed / total).astype(jnp.bfloat16)


def attend(half, own, far, tables, part, parts, into=None):
    blocks, kinds, slots, width = far.shape
    heads = width // HEAD_DIM
    count = heads // parts
    first = part * count
    rows = 2 * blocks * slots
    shape = (blocks, kinds, slots, HEAD_DIM)
    whole = pl.BlockSpec((rows, HEAD_DIM), lambda g, half: (0, 0))
    return pl.pallas_call(
        attend_kernel,
        grid_spec=pltpu.PrefetchScalarGridSpec(
            num_scalar_prefetch=1,
            grid=(count,),
            in_specs=[
                pl.BlockSpec(shape, lambda g, half: (0, 0, 0, half[0] * heads + first + g)),
                pl.BlockSpec(shape, lambda g, half: (0, 0, 0, first + g)),
                whole,
                whole,
                whole,
                whole,
                pl.BlockSpec((1, rows), lambda g, half: (0, 0)),
                pl.BlockSpec((HEAD_DIM, HEAD_DIM), lambda g, half: (0, 0)),
            ]
            + ([] if into is None else [pl.BlockSpec(memory_space=pl.ANY)]),
            out_specs=pl.BlockSpec((rows, HEAD_DIM), lambda g, half: (0, first + g)),
        ),
        out_shape=jax.ShapeDtypeStruct((rows, width), jnp.bfloat16),
        input_output_aliases={} if into is None else {9: 0},
        compiler_params=pltpu.CompilerParams(vmem_limit_bytes=VMEM),
        cost_estimate=pl.CostEstimate(
            flops=count * rows * rows * HEAD_DIM * 4,
            bytes_accessed=rows * width * 8,
            transcendentals=0,
        ),
        name="attend",
    )(half, own, far, *tables, *([] if into is None else [into]))


def gelu_kernel(part_ref, units_ref, *refs):
    refs[-1][...] = jax.nn.gelu(units_ref[0].astype(jnp.float32), approximate=True).astype(jnp.bfloat16)


def activate(part, units, width, into=None):
    blocks, slots, _ = units.shape
    first = 0 if into is None else blocks
    return pl.pallas_call(
        gelu_kernel,
        grid_spec=pltpu.PrefetchScalarGridSpec(
            num_scalar_prefetch=1,
            grid=(blocks,),
            in_specs=[pl.BlockSpec((1, slots, width), lambda b, part: (b, 0, part[0]))]
            + ([] if into is None else [pl.BlockSpec(memory_space=pl.ANY)]),
            out_specs=pl.BlockSpec((slots, width), lambda b, part: (first + b, 0)),
        ),
        out_shape=jax.ShapeDtypeStruct((2 * blocks * slots, width), jnp.bfloat16),
        input_output_aliases={} if into is None else {2: 0},
        compiler_params=pltpu.CompilerParams(vmem_limit_bytes=LESS),
        cost_estimate=pl.CostEstimate(
            flops=blocks * slots * width * 4, bytes_accessed=blocks * slots * width, transcendentals=0
        ),
        name="activate",
    )(part, units, *([] if into is None else [into]))


def project_kernel(layout, core_ref, attn_ref, act_ref, *refs):
    pieces, (own_ref, far_ref, w_ref, sems) = refs[:-4], refs[-4:]
    depth = attn_ref.shape[1]
    rows, columns = own_ref.shape
    core = core_ref[0]
    copies = []
    for (base, here, share), piece in zip(layout, pieces):
        start = base + (core if here else 1 - core) * share
        place = pl.ds(pl.multiple_of(start, 16), piece.shape[0])
        copies.append(pltpu.make_async_copy(piece, w_ref.at[place], sems.at[len(copies)]))
        copies[-1].start()
    pending = [base // (2 * share) * 2 * share for base, _, share in layout]
    for first in range(0, columns, 256):
        end = min(first + 256, columns)
        while pending and pending[0] < end:
            copies[-len(pending)].wait()
            pending.pop(0)
        total = lax.dot_general(attn_ref[...], w_ref[first:end, :depth], NT, preferred_element_type=jnp.float32)
        total += lax.dot_general(act_ref[...], w_ref[first:end, depth:], NT, preferred_element_type=jnp.float32)
        own_ref[:, first:end] = total[:rows]
        far_ref[:, first:end] = total[rows:].astype(jnp.bfloat16)


def project(core, attn, act, chips):
    share = sum(piece.shape[0] for here, _, piece in chips[0] if here)
    layout, flat = [], []
    for index, pieces in enumerate(chips):
        for here, first, piece in pieces:
            layout.append((2 * share * index + first, here, share))
            flat.append(piece)
    rows, depth = attn.shape[0] // 2, attn.shape[1] + act.shape[1]
    columns = 2 * share * len(chips)
    inside = pl.BlockSpec(memory_space=pltpu.VMEM)
    return pl.pallas_call(
        functools.partial(project_kernel, layout),
        in_specs=[pl.BlockSpec(memory_space=pltpu.SMEM), inside, inside]
        + [pl.BlockSpec(memory_space=pl.ANY)] * len(flat),
        out_specs=[inside, inside],
        out_shape=[
            jax.ShapeDtypeStruct((rows, columns), jnp.float32),
            jax.ShapeDtypeStruct((rows, columns), jnp.bfloat16),
        ],
        scratch_shapes=[
            pltpu.VMEM((columns, depth), jnp.bfloat16),
            pltpu.SemaphoreType.DMA((len(flat),)),
        ],
        compiler_params=pltpu.CompilerParams(vmem_limit_bytes=LESS),
        cost_estimate=pl.CostEstimate(
            flops=rows * columns * depth // 2, bytes_accessed=columns * depth // 4, transcendentals=0
        ),
        name="project",
    )(core, attn, act, *flat)


def finish_kernel(chunks, tile_ref, place_ref, step_ref, *refs):
    pairs = [refs[2 * i : 2 * i + 2] for i in range(chunks)]
    (
        stream_ref, bias_ref, gate_ref, scale_ref, shift_ref, w_ref, b_ref, latent_ref, hidden_ref, next_ref, proj_ref,
    ) = refs[2 * chunks :]
    places = len(PATH)
    chip = proj_ref.shape[1] // places
    mine = place_ref[places + tile_ref[0] // 2]
    behind = [0] + [distance for step in range(1, places // 2) for distance in (step, -step)] + [places // 2]
    for own_ref, far_ref in pairs:
        for first in range(0, own_ref.shape[1], chip):
            source = place_ref[(mine - behind.pop(0) + places) % places]
            target = pl.ds(pl.multiple_of(chip * source, 128), chip)
            part = slice(first, first + chip)
            proj_ref[:, target] = own_ref[:, part] + far_ref[:, part].astype(jnp.float32)
    updated = stream_ref[0].astype(jnp.float32) + gate_ref[...] * (proj_ref[...] + bias_ref[...])
    hidden_ref[0] = updated.astype(jnp.bfloat16)

    @pl.when(pl.program_id(0) > 0)
    def _():
        center = updated - jnp.mean(updated, axis=-1, keepdims=True)
        variance = jnp.mean(center * center, axis=-1, keepdims=True)
        normed = center * lax.rsqrt(variance + EPS)
        modulated = ((1.0 + scale_ref[...]) * normed + shift_ref[...]).astype(jnp.bfloat16)
        velocity = lax.dot_general(w_ref[...], modulated, NT, preferred_element_type=jnp.float32)
        next_ref[0] = latent_ref[0] + step_ref[0] * (velocity + b_ref[...])


def finish(tile, step, chunks, stream, bias, gate, scale, shift, w_final, b_final, latent):
    blocks, slots, width = stream.shape
    channels = w_final.shape[0]
    flat = [array for pair in chunks for array in pair]

    def whole(array):
        return pl.BlockSpec(array.shape, lambda b, *_: (0, 0))

    tokens = pl.BlockSpec((1, slots, width), lambda b, *_: (b, 0, 0))
    image = pl.BlockSpec((1, channels, slots), lambda b, *_: (jnp.maximum(b - 1, 0), 0, 0))
    return pl.pallas_call(
        functools.partial(finish_kernel, len(chunks)),
        grid_spec=pltpu.PrefetchScalarGridSpec(
            num_scalar_prefetch=3,
            grid=(blocks,),
            in_specs=[pl.BlockSpec((slots, array.shape[1]), lambda b, *_: (b, 0)) for array in flat]
            + [
                tokens,
                whole(bias),
                whole(gate),
                whole(scale),
                whole(shift),
                whole(w_final),
                whole(b_final),
                image,
            ],
            out_specs=[tokens, image],
            scratch_shapes=[pltpu.VMEM((slots, width), jnp.float32)],
        ),
        out_shape=[
            jax.ShapeDtypeStruct(stream.shape, jnp.bfloat16),
            jax.ShapeDtypeStruct(latent.shape, jnp.float32),
        ],
        compiler_params=pltpu.CompilerParams(vmem_limit_bytes=VMEM),
        cost_estimate=pl.CostEstimate(
            flops=blocks * slots * width * 160, bytes_accessed=blocks * slots * width * 10, transcendentals=0
        ),
        name="finish",
    )(tile, np.array(PATH + PLACE, np.int32), step, *flat, stream, bias, gate, scale, shift, w_final, b_final, latent)


PATH = (0, 1, 3, 5, 7, 6, 4, 2)
PLACE = tuple(PATH.index(chip) for chip in range(len(PATH)))


def hop(array, by):
    places = len(PATH)
    pairs = [(2 * PATH[i] + c, 2 * PATH[(i + by) % places] + c) for i in range(places) for c in range(2)]
    return lax.ppermute(array, "tile", pairs)


def both_cores(array, first=0):
    other = lax.ppermute(array, "tile", [(t, t ^ 1) for t in range(2 * len(PATH))])
    return [(True, first, array), (False, first, other)]


def paired(
    partners,
    attn_proj,
    mlp_proj,
    stream,
    text_len,
    q_gain,
    k_gain,
    w_out_attn,
    w_out_mlp,
    bias_out,
    gate_mod,
    final_shift,
    final_scale,
    w_final,
    b_final,
    latent,
    step_size,
):
    me = lax.axis_index("head")
    half = me[None].astype(jnp.int32)
    trade = functools.partial(lax.ppermute, axis_name="head", perm=[(0, 1), (1, 0)])

    tile = lax.axis_index("tile").astype(jnp.int32)
    core = (tile % 2)[None]
    own_attn = jnp.transpose(attn_proj[0], (0, 2, 1, 3))
    own_units = mlp_proj[0]
    slots = own_attn.shape[2]
    units = own_units.shape[2] // partners
    width = own_attn.shape[3] // partners
    sent_attn = lax.dynamic_slice_in_dim(own_attn, (1 - me) * width, width, axis=3)
    block = jnp.concatenate([w_out_attn.T, w_out_mlp.T], axis=1)

    onward, back = hop(block, 1), hop(block, -1)
    far_attn = trade(sent_attn)
    chips = [both_cores(block)]

    tables = make_tables(half, text_len, q_gain, k_gain, 6 * slots)
    act_near = activate(half, own_units, units)
    sent_units = lax.dynamic_slice_in_dim(own_units, (1 - me) * units, units, axis=2)

    onward, back, tables, act_near, sent_units, chips = lax.optimization_barrier(
        (onward, back, tables, act_near, sent_units, [[piece[2] for piece in chip] for chip in chips])
    )
    chips = [[(True, 0, chip[0]), (False, 0, chip[1])] for chip in chips]
    chips += [both_cores(onward), both_cores(back)]
    onward, back = hop(onward, 1), hop(back, -1)
    far_attn, sent_units = lax.optimization_barrier((far_attn, sent_units))
    far_units = trade(sent_units)
    attn = attend(half, own_attn, far_attn, tables, 0, 2)
    blocks = [piece[2] for chip in chips[1:] for piece in chip]
    attn, onward, back, blocks = lax.optimization_barrier((attn, onward, back, blocks))
    chips[1:] = [[(True, 0, blocks[i]), (False, 0, blocks[i + 1])] for i in (0, 2)]
    chips += [both_cores(onward), both_cores(back)]
    onward, back = hop(onward, 1), hop(back, -1)
    attn = attend(half, own_attn, far_attn, tables, 1, 2, attn)
    far_units, attn = lax.optimization_barrier((far_units, attn))
    act = activate(jnp.zeros_like(half), far_units, units, act_near)

    chunks = []

    def send(group):
        own, sent = project(core, attn, act, group)
        chunks.append((own, trade(sent)))
        return sent

    sent = send(chips[0:1])
    attn, sent = lax.optimization_barrier((attn, sent))
    sent = send(chips[1:3])
    onward, back, attn, sent, chunks[0] = lax.optimization_barrier((onward, back, attn, sent, chunks[0]))
    middle = block.shape[0] // 2
    last = hop(onward[:middle], 1), hop(back[middle:], -1)
    chips += [both_cores(onward), both_cores(back)]
    sent = send(chips[3:5])
    attn, sent, chunks[1] = lax.optimization_barrier((attn, sent, chunks[1]))
    sent = send(chips[5:7])
    onward, back, attn, sent, chunks[2] = lax.optimization_barrier((*last, attn, sent, chunks[2]))
    chips.append(both_cores(onward) + both_cores(back, middle))
    send(chips[7:8])

    hidden, following = finish(
        tile[None],
        step_size,
        chunks,
        stream[0],
        bias_out[None, :],
        gate_mod,
        final_scale,
        final_shift,
        w_final.T,
        b_final[:, None],
        jnp.transpose(latent[0], (0, 2, 1)),
    )
    return hidden[None], jnp.transpose(following, (0, 2, 1))[None]


def solution(mesh):
    placed = (
        P("tile", None, "head", None, None),
        P("tile", None, "head", None),
        P("tile", None, "head", None),
        P("tile"),
        P(),
        P(),
        P("head", "tile"),
        P("head", "tile"),
        P(),
        P("tile", None),
        P("tile", None),
        P("tile", None),
        P(),
        P(),
        P("tile", None, "head", None),
        P("tile"),
    )
    return jax.shard_map(
        functools.partial(paired, mesh.shape["head"]) if fits(mesh.shape) else general,
        mesh=mesh,
        in_specs=placed,
        out_specs=(P("tile", None, "head", None), P("tile", None, "head", None)),
        check_vma=False,
    )
```

profile of v0, /device:TPU:0, one launch (start us, length us, event | category | flops | bytes accessed | tf_op | source)
XLA Modules:
  0.0 180.1 jit_solution(10046959002230866613)
XLA Ops:
  0.6 2.8 %pad_maximum_fusion.refs_0_ = bf16[192,4608]{1,0:T(8,128)(2,1)} fusion(bf16[192,3072]{1,0:T(8,128)(2,1)} %bitcast.32, bf16[192,1536]{1,0:T(8,128)(2,1)} %bitcast.33), kind=kLoop, calls=%fused_computation.1 | loop fusion | flops 3538944 | bytes 3538944 | tf_op jit(solution)/shard_map/concatenate | solution.py:510
  3.4 2.9 %collective-permute-start.1 = (bf16[192,4608]{1,0:T(8,128)(2,1)}, bf16[192,4608]{1,0:T(8,128)(2,1)}, u32[]{:S(2)}, u32[]{:S(2)}) collective-permute-start(bf16[192,4608]{1,0:T(8,128)(2,1)} %pad_maximum_fusion.refs_0_), channel_id=1, source_target_pairs={{0,4},{2,6},{4,12},{6,14},{12,20},{14,22},{20,28},{22,30},{28,24},... | collective-permute-start | bytes 5308424 | tf_op jit(solution)/shard_map/ppermute | solution.py:471
  6.3 0.1 collective-permute-start.2
  6.4 0.0 collective-permute-start.3
  6.4 3.5 %dynamic-slice_bitcast_fusion = bf16[3,3,96,1536]{3,2,1,0:T(8,128)(2,1)} fusion(bf16[1,3,96,3,3072]{4,2,3,1,0:T(8,128)(2,1)} %param.19, s32[]{:T(128)S(6)} %select_n.13), kind=kLoop, calls=%fused_computation | loop fusion | bytes 5308420 | tf_op jit(solution)/shard_map/dynamic_slice | solution.py:509
  10.0 2.0 %collective-permute-start = (bf16[3,3,96,1536]{3,2,1,0:T(8,128)(2,1)}, bf16[3,3,96,1536]{3,2,1,0:T(8,128)(2,1)}, u32[]{:S(2)}, u32[]{:S(2)}) collective-permute-start(bf16[3,3,96,1536]{3,2,1,0:T(8,128)(2,1)} %dynamic-slice_bitcast_fusion), channel_id=1, source_target_pairs={{0,1},{1,0},{2,3},{3,2},{4,5},{5,4},{6,7},{7,6},{8,9},{9,8},{10,11... | collective-permute-start | bytes 7962632 | tf_op jit(solution)/shard_map/ppermute | solution.py:513
  12.6 3.2 %tables.1 = (f32[576,128]{1,0:T(8,128)}, f32[576,128]{1,0:T(8,128)}, f32[576,128]{1,0:T(8,128)}, f32[576,128]{1,0:T(8,128)}, f32[1,576]{1,0:T(1,128)}, /*index=5*/bf16[128,128]{1,0:T(8,128)(2,1)}) custom-call(s32[1]{0:T(128)} %bitcast.1.half_ref.part_ref, s32[1]{0:T(128)S(6)} %copy.26.len_ref, f32[1,128]{1,0:T(1,128)} %constant.39.clone.row_freq_ref, ...), custom_call_target="tpu_custom_call" | custom-call | flops 589824 | bytes 294912 | tf_op jit(solution)/shard_map/tables/pallas_call | solution.py:228
  15.9 2.0 %copy-done.1 = bf16[1,3,96,6144]{3,2,1,0:T(8,128)(2,1)S(1)} copy-done((bf16[1,3,96,6144]{3,2,1,0:T(8,128)(2,1)S(1)}, bf16[1,3,96,6144]{3,2,1,0:T(8,128)(2,1)}, u32[]{:S(2)}) %copy-start.1) | copy-done | bytes 3538968
  17.9 1.4 activate.2.refs_0_
  19.3 1.5 dynamic-slice_bitcast_fusion.1
  20.7 24.6 %collective-permute-done.1.refs_0_ = bf16[192,4608]{1,0:T(8,128)(2,1)} collective-permute-done((bf16[192,4608]{1,0:T(8,128)(2,1)}, bf16[192,4608]{1,0:T(8,128)(2,1)}, u32[]{:S(2)}, u32[]{:S(2)}) %collective-permute-start.1) | collective-permute-done | bytes 1769504 | tf_op jit(solution)/shard_map/ppermute | solution.py:471
  45.4 1.4 collective-permute-done.2.refs_2_
  46.7 0.0 collective-permute-done.3.refs_1_
  46.7 1.6 collective-permute-start.4
  48.3 0.4 collective-permute-start.5
  48.8 0.0 collective-permute-start.6
  48.8 0.5 collective-permute-start.7
  49.3 21.2 %collective-permute-done.far_ref = bf16[3,3,96,1536]{3,2,1,0:T(8,128)(2,1)} collective-permute-done((bf16[3,3,96,1536]{3,2,1,0:T(8,128)(2,1)}, bf16[3,3,96,1536]{3,2,1,0:T(8,128)(2,1)}, u32[]{:S(2)}, u32[]{:S(2)}) %collective-permute-start) | collective-permute-done | bytes 2654240 | tf_op jit(solution)/shard_map/ppermute | solution.py:513
  70.5 1.7 collective-permute-start.10
  72.2 9.3 %attend.2.refs_0_ = bf16[576,1536]{1,0:T(8,128)(2,1)} custom-call(s32[1]{0:T(128)} %bitcast.1.half_ref.part_ref, bf16[3,3,96,3072]{3,2,1,0:T(8,128)(2,1)} %bitcast.29, bf16[3,3,96,1536]{3,2,1,0:T(8,128)(2,1)} %collective-permute-done.far_ref, f32[576,128]{1,0:T(8,128)} %get-tuple-element.65.cq_ref, f32[576,128]{1,0:T(8,128)} %get-tuple-element.66.sq_ref, ...), custom_call_target="tpu_custom_call" | custom-call | flops 1019215872 | bytes 7077888 | tf_op jit(solution)/shard_map/attend/pallas_call | solution.py:285
  81.5 4.7 %collective-permute-done.4.refs_0_ = bf16[192,4608]{1,0:T(8,128)(2,1)} collective-permute-done((bf16[192,4608]{1,0:T(8,128)(2,1)}, bf16[192,4608]{1,0:T(8,128)(2,1)}, u32[]{:S(2)}, u32[]{:S(2)}) %collective-permute-start.4) | collective-permute-done | bytes 1769504 | tf_op jit(solution)/shard_map/ppermute | solution.py:471
  86.2 1.3 collective-permute-done.5.refs_2_
  87.5 0.0 collective-permute-done.7.refs_3_
  87.5 1.6 collective-permute-start.8
  89.1 0.4 collective-permute-start.9
  89.5 0.5 collective-permute-start.13
  90.1 9.3 %attend.3.attn_ref = bf16[576,1536]{1,0:T(8,128)(2,1)} custom-call(s32[1]{0:T(128)} %bitcast.1.half_ref.part_ref, bf16[3,3,96,3072]{3,2,1,0:T(8,128)(2,1)} %bitcast.30, bf16[3,3,96,1536]{3,2,1,0:T(8,128)(2,1)} %collective-permute-done.far_ref, f32[576,128]{1,0:T(8,128)} %get-tuple-element.65.cq_ref, ...), custom_call_target="tpu_custom_call", output_to_operand_aliasing={{}: (9, {})} | custom-call | flops 1019215872 | bytes 7077888 | tf_op jit(solution)/shard_map/attend/pallas_call | solution.py:285
  99.3 11.9 %collective-permute-done.10.units_ref = bf16[3,96,3072]{2,1,0:T(8,128)(2,1)} collective-permute-done((bf16[3,96,3072]{2,1,0:T(8,128)(2,1)}, bf16[3,96,3072]{2,1,0:T(8,128)(2,1)}, u32[]{:S(2)}, u32[]{:S(2)}) %collective-permute-start.10) | collective-permute-done | bytes 1769504 | tf_op jit(solution)/shard_map/ppermute | solution.py:527
  111.2 3.0 %activate.3.act_ref = bf16[576,3072]{1,0:T(8,128)(2,1)S(1)} custom-call(s32[1]{0:T(128)} %constant.38.clone.1.part_ref, bf16[3,96,3072]{2,1,0:T(8,128)(2,1)} %collective-permute-done.10.units_ref, bf16[576,3072]{1,0:T(8,128)(2,1)S(1)} %activate.2.refs_0_), custom_call_target="tpu_custom_call", output_to_operand_aliasing={{}: (2, {})} | custom-call | flops 3538944 | bytes 884736 | tf_op jit(solution)/shard_map/activate/pallas_call | solution.py:322
  114.2 5.0 %project.5 = (f32[288,384]{1,0:T(8,128)S(1)}, bf16[288,384]{1,0:T(8,128)(2,1)S(1)}) custom-call(s32[1]{0:T(128)} %bitcast.13.core_ref, bf16[576,1536]{1,0:T(8,128)(2,1)S(1)} %copy-done, bf16[576,3072]{1,0:T(8,128)(2,1)S(1)} %activate.3.act_ref, bf16[192,4608]{1,0:T(8,128)(2,1)} %pad_maximum_fusion.refs_0_, bf16[192,4608]{1,0:T(8,128)(2,1)} %collective-permute-done.3.refs_1_), custom_call_target="tpu_custom_call" | custom-call | flops 254803968 | bytes 442368 | tf_op jit(solution)/shard_map/project/pallas_call | solution.py:374
  119.2 0.8 copy-done.5
  119.9 1.6 collective-permute-start.11
  121.5 6.5 %project.6 = (f32[288,768]{1,0:T(8,128)S(1)}, bf16[288,768]{1,0:T(8,128)(2,1)S(1)}) custom-call(s32[1]{0:T(128)} %bitcast.13.core_ref, bf16[576,1536]{1,0:T(8,128)(2,1)S(1)} %copy-done, bf16[576,3072]{1,0:T(8,128)(2,1)S(1)} %activate.3.act_ref, bf16[192,4608]{1,0:T(8,128)(2,1)} %collective-permute-done.1.refs_0_, ...), custom_call_target="tpu_custom_call" | custom-call | flops 509607936 | bytes 884736 | tf_op jit(solution)/shard_map/project/pallas_call | solution.py:374
  128.1 0.0 collective-permute-done.11.refs_1_
  128.1 0.0 collective-permute-done.9.refs_2_
  128.1 0.7 copy-done.9
  128.8 0.5 collective-permute-start.18
  129.3 0.4 collective-permute-start.14
  129.8 1.2 slice.6
  131.0 1.2 slice.7
  132.2 1.6 collective-permute-start.15
  133.9 0.0 collective-permute-done.13.refs_3_
  133.9 0.5 collective-permute-start.16
  134.3 6.5 %project.7 = (f32[288,768]{1,0:T(8,128)S(1)}, bf16[288,768]{1,0:T(8,128)(2,1)S(1)}) custom-call(s32[1]{0:T(128)} %bitcast.13.core_ref, bf16[576,1536]{1,0:T(8,128)(2,1)S(1)} %copy-done, bf16[576,3072]{1,0:T(8,128)(2,1)S(1)} %activate.3.act_ref, bf16[192,4608]{1,0:T(8,128)(2,1)} %collective-permute-done.4.refs_0_, ...), custom_call_target="tpu_custom_call" | custom-call | flops 509607936 | bytes 884736 | tf_op jit(solution)/shard_map/project/pallas_call | solution.py:374
  140.9 0.9 copy-done.3
  141.8 0.0 collective-permute-done.14.refs_3_
  141.8 1.6 collective-permute-start.19
  143.4 0.0 collective-permute-done.17.refs_1_
  143.4 6.8 %project.8 = (f32[288,768]{1,0:T(8,128)S(1)}, bf16[288,768]{1,0:T(8,128)(2,1)}) custom-call(s32[1]{0:T(128)} %bitcast.13.core_ref, bf16[576,1536]{1,0:T(8,128)(2,1)S(1)} %copy-done, bf16[576,3072]{1,0:T(8,128)(2,1)S(1)} %activate.3.act_ref, bf16[192,4608]{1,0:T(8,128)(2,1)} %collective-permute-done.8.refs_0_, ...), custom_call_target="tpu_custom_call" | custom-call | flops 509607936 | bytes 884736 | tf_op jit(solution)/shard_map/project/pallas_call | solution.py:374
  150.2 3.0 %collective-permute-done.19.refs_5_ = bf16[288,768]{1,0:T(8,128)(2,1)S(1)} collective-permute-done((bf16[288,768]{1,0:T(8,128)(2,1)S(1)}, bf16[288,768]{1,0:T(8,128)(2,1)S(1)}, u32[]{:S(2)}, u32[]{:S(2)}) %collective-permute-start.19) | collective-permute-done | bytes 442400 | tf_op jit(solution)/shard_map/ppermute | solution.py:542
  153.2 0.4 collective-permute-done.15.refs_0_
  153.6 1.3 collective-permute-done.16.refs_2_
  154.9 0.5 collective-permute-start.22
  155.4 1.5 collective-permute-start.20
  156.9 0.4 collective-permute-done.21.refs_1_
  157.3 1.3 collective-permute-done.22.refs_3_
  158.5 4.4 %project.9 = (f32[288,384]{1,0:T(8,128)S(1)}, bf16[288,384]{1,0:T(8,128)(2,1)}) custom-call(s32[1]{0:T(128)} %bitcast.13.core_ref, bf16[576,1536]{1,0:T(8,128)(2,1)S(1)} %copy-done, bf16[576,3072]{1,0:T(8,128)(2,1)S(1)} %activate.3.act_ref, bf16[96,4608]{1,0:T(8,128)(2,1)S(1)} %collective-permute-done.15.refs_0_, ...), custom_call_target="tpu_custom_call" | custom-call | flops 254803968 | bytes 442368 | tf_op jit(solution)/shard_map/project/pallas_call | solution.py:374
  163.0 0.8 copy-done.6
  163.7 1.5 collective-permute-start.23
  165.3 0.7 copy.23.refs_16_
  166.6 2.1 %collective-permute-done.20.refs_7_ = bf16[288,768]{1,0:T(8,128)(2,1)} collective-permute-done((bf16[288,768]{1,0:T(8,128)(2,1)}, bf16[288,768]{1,0:T(8,128)(2,1)}, u32[]{:S(2)}, u32[]{:S(2)}) %collective-permute-start.20) | collective-permute-done | bytes 442400 | tf_op jit(solution)/shard_map/ppermute | solution.py:542
  168.7 3.7 %collective-permute-done.23.refs_9_ = bf16[288,384]{1,0:T(8,128)(2,1)S(1)} collective-permute-done((bf16[288,384]{1,0:T(8,128)(2,1)}, bf16[288,384]{1,0:T(8,128)(2,1)S(1)}, u32[]{:S(2)}, u32[]{:S(2)}) %collective-permute-start.23) | collective-permute-done | bytes 221216 | tf_op jit(solution)/shard_map/ppermute | solution.py:542
  172.4 0.7 copy-done.10
  173.1 6.8 %finish.1 = (bf16[3,96,3072]{2,1,0:T(8,128)(2,1)}, f32[2,64,96]{2,1,0:T(8,128)}) custom-call(s32[1]{0:T(128)} %bitcast.tile_ref, s32[16]{0:T(128)} %constant.41.clone.place_ref, f32[1]{0:T(128)S(6)} %copy.27.step_ref, f32[288,384]{1,0:T(8,128)} %copy-done.5, bf16[288,384]{1,0:T(8,128)(2,1)} %copy-done.9, f32[288,768]{1,0:T(8,128)} %copy-done.2, ...), custom_call_target="tpu_custom_call" | custom-call | flops 141557760 | bytes 8847360 | tf_op jit(solution)/shard_map/finish/pallas_call | solution.py:433
  (25 shorter events, 0.1 us)
Async XLA Ops:
  3.4 41.9 %collective-permute-start.1 = (bf16[192,4608]{1,0:T(8,128)(2,1)}, bf16[192,4608]{1,0:T(8,128)(2,1)}, u32[]{:S(2)}, u32[]{:S(2)}) collective-permute-start(bf16[192,4608]{1,0:T(8,128)(2,1)} %pad_maximum_fusion.refs_0_), channel_id=1, source_target_pairs={{0,4},{2,6},{4,12},{6,14},{12,20},{14,22},{20,28},{22,30},{28,24},... | collective-permute-start | bytes 5308424 | tf_op jit(solution)/shard_map/ppermute | solution.py:471
  6.3 40.4 %collective-permute-start.2 = (bf16[192,4608]{1,0:T(8,128)(2,1)}, bf16[192,4608]{1,0:T(8,128)(2,1)}, u32[]{:S(2)}, u32[]{:S(2)}) collective-permute-start(bf16[192,4608]{1,0:T(8,128)(2,1)} %pad_maximum_fusion.refs_0_), channel_id=1, source_target_pairs={{0,8},{2,10},{4,0},{6,2},{12,4},{14,6},{20,12},{22,14},{28,20},{30... | collective-permute-start | bytes 5308424 | tf_op jit(solution)/shard_map/ppermute | solution.py:471
  6.4 40.3 %collective-permute-start.3 = (bf16[192,4608]{1,0:T(8,128)(2,1)}, bf16[192,4608]{1,0:T(8,128)(2,1)}, u32[]{:S(2)}, u32[]{:S(2)}) collective-permute-start(bf16[192,4608]{1,0:T(8,128)(2,1)} %pad_maximum_fusion.refs_0_), channel_id=1, source_target_pairs={{0,2},{2,0},{4,6},{6,4},{8,10},{10,8},{12,14},{14,12},{16,18},{18,... | collective-permute-start | bytes 5308424 | tf_op jit(solution)/shard_map/ppermute | solution.py:475
  10.0 60.5 %collective-permute-start = (bf16[3,3,96,1536]{3,2,1,0:T(8,128)(2,1)}, bf16[3,3,96,1536]{3,2,1,0:T(8,128)(2,1)}, u32[]{:S(2)}, u32[]{:S(2)}) collective-permute-start(bf16[3,3,96,1536]{3,2,1,0:T(8,128)(2,1)} %dynamic-slice_bitcast_fusion), channel_id=1, source_target_pairs={{0,1},{1,0},{2,3},{3,2},{4,5},{5,4},{6,7},{7,6},{8,9},{9,8},{10,11... | collective-permute-start | bytes 7962632 | tf_op jit(solution)/shard_map/ppermute | solution.py:513
  15.9 2.0 %copy-start.1 = (bf16[1,3,96,6144]{3,2,1,0:T(8,128)(2,1)S(1)}, bf16[1,3,96,6144]{3,2,1,0:T(8,128)(2,1)}, u32[]{:S(2)}) copy-start(bf16[1,3,96,6144]{3,2,1,0:T(8,128)(2,1)} %param.20) | copy-start | bytes 10616836
  46.7 39.5 %collective-permute-start.4 = (bf16[192,4608]{1,0:T(8,128)(2,1)}, bf16[192,4608]{1,0:T(8,128)(2,1)}, u32[]{:S(2)}, u32[]{:S(2)}) collective-permute-start(bf16[192,4608]{1,0:T(8,128)(2,1)} %collective-permute-done.1.refs_0_), channel_id=1, source_target_pairs={{0,4},{2,6},{4,12},{6,14},{12,20},{14,22},{20,28},{22,30},{28,24},... | collective-permute-start | bytes 5308424 | tf_op jit(solution)/shard_map/ppermute | solution.py:471
  48.3 39.2 %collective-permute-start.5 = (bf16[192,4608]{1,0:T(8,128)(2,1)}, bf16[192,4608]{1,0:T(8,128)(2,1)}, u32[]{:S(2)}, u32[]{:S(2)}) collective-permute-start(bf16[192,4608]{1,0:T(8,128)(2,1)} %collective-permute-done.2.refs_2_), channel_id=1, source_target_pairs={{0,8},{2,10},{4,0},{6,2},{12,4},{14,6},{20,12},{22,14},{28,20},{30... | collective-permute-start | bytes 5308424 | tf_op jit(solution)/shard_map/ppermute | solution.py:471
  48.8 38.7 %collective-permute-start.6 = (bf16[192,4608]{1,0:T(8,128)(2,1)}, bf16[192,4608]{1,0:T(8,128)(2,1)}, u32[]{:S(2)}, u32[]{:S(2)}) collective-permute-start(bf16[192,4608]{1,0:T(8,128)(2,1)} %collective-permute-done.1.refs_0_), channel_id=1, source_target_pairs={{0,2},{2,0},{4,6},{6,4},{8,10},{10,8},{12,14},{14,12},{16,18},{18,... | collective-permute-start | bytes 5308424 | tf_op jit(solution)/shard_map/ppermute | solution.py:475
  48.8 38.7 %collective-permute-start.7 = (bf16[192,4608]{1,0:T(8,128)(2,1)}, bf16[192,4608]{1,0:T(8,128)(2,1)}, u32[]{:S(2)}, u32[]{:S(2)}) collective-permute-start(bf16[192,4608]{1,0:T(8,128)(2,1)} %collective-permute-done.2.refs_2_), channel_id=1, source_target_pairs={{0,2},{2,0},{4,6},{6,4},{8,10},{10,8},{12,14},{14,12},{16,18},{18,... | collective-permute-start | bytes 5308424 | tf_op jit(solution)/shard_map/ppermute | solution.py:475
  70.5 40.7 %collective-permute-start.10 = (bf16[3,96,3072]{2,1,0:T(8,128)(2,1)}, bf16[3,96,3072]{2,1,0:T(8,128)(2,1)}, u32[]{:S(2)}, u32[]{:S(2)}) collective-permute-start(bf16[3,96,3072]{2,1,0:T(8,128)(2,1)} %dynamic-slice_bitcast_fusion.1), channel_id=1, source_target_pairs={{0,1},{1,0},{2,3},{3,2},{4,5},{5,4},{6,7},{7,6},{8,9},{9,8},{10,11... | collective-permute-start | bytes 5308424 | tf_op jit(solution)/shard_map/ppermute | solution.py:527
  87.5 40.6 %collective-permute-start.8 = (bf16[192,4608]{1,0:T(8,128)(2,1)}, bf16[192,4608]{1,0:T(8,128)(2,1)}, u32[]{:S(2)}, u32[]{:S(2)}) collective-permute-start(bf16[192,4608]{1,0:T(8,128)(2,1)} %collective-permute-done.4.refs_0_), channel_id=1, source_target_pairs={{0,4},{2,6},{4,12},{6,14},{12,20},{14,22},{20,28},{22,30},{28,24},... | collective-permute-start | bytes 5308424 | tf_op jit(solution)/shard_map/ppermute | solution.py:471
  89.1 39.0 %collective-permute-start.9 = (bf16[192,4608]{1,0:T(8,128)(2,1)}, bf16[192,4608]{1,0:T(8,128)(2,1)}, u32[]{:S(2)}, u32[]{:S(2)}) collective-permute-start(bf16[192,4608]{1,0:T(8,128)(2,1)} %collective-permute-done.5.refs_2_), channel_id=1, source_target_pairs={{0,8},{2,10},{4,0},{6,2},{12,4},{14,6},{20,12},{22,14},{28,20},{30... | collective-permute-start | bytes 5308424 | tf_op jit(solution)/shard_map/ppermute | solution.py:471
  89.5 42.7 %collective-permute-start.12 = (bf16[192,4608]{1,0:T(8,128)(2,1)}, bf16[192,4608]{1,0:T(8,128)(2,1)}, u32[]{:S(2)}, u32[]{:S(2)}) collective-permute-start(bf16[192,4608]{1,0:T(8,128)(2,1)} %collective-permute-done.4.refs_0_), channel_id=1, source_target_pairs={{0,2},{2,0},{4,6},{6,4},{8,10},{10,8},{12,14},{14,12},{16,18},{18,... | collective-permute-start | bytes 5308424 | tf_op jit(solution)/shard_map/ppermute | solution.py:475
  89.5 44.3 %collective-permute-start.13 = (bf16[192,4608]{1,0:T(8,128)(2,1)}, bf16[192,4608]{1,0:T(8,128)(2,1)}, u32[]{:S(2)}, u32[]{:S(2)}) collective-permute-start(bf16[192,4608]{1,0:T(8,128)(2,1)} %collective-permute-done.5.refs_2_), channel_id=1, source_target_pairs={{0,2},{2,0},{4,6},{6,4},{8,10},{10,8},{12,14},{14,12},{16,18},{18,... | collective-permute-start | bytes 5308424 | tf_op jit(solution)/shard_map/ppermute | solution.py:475
  99.3 14.9 %copy-start = (bf16[576,1536]{1,0:T(8,128)(2,1)S(1)}, bf16[576,1536]{1,0:T(8,128)(2,1)}, u32[]{:S(2)}) copy-start(bf16[576,1536]{1,0:T(8,128)(2,1)} %attend.3.attn_ref) | copy-start | bytes 5308420
  119.2 0.8 copy-start.5
  119.9 8.2 %collective-permute-start.11 = (bf16[288,384]{1,0:T(8,128)(2,1)S(1)}, bf16[288,384]{1,0:T(8,128)(2,1)S(1)}, u32[]{:S(2)}, u32[]{:S(2)}) collective-permute-start(bf16[288,384]{1,0:T(8,128)(2,1)S(1)} %get-tuple-element.82), channel_id=1, source_target_pairs={{0,1},{1,0},{2,3},{3,2},{4,5},{5,4},{6,7},{7,6},{8,9},{9,8},{10,11... | collective-permute-start | bytes 663560 | tf_op jit(solution)/shard_map/ppermute | solution.py:542
  128.1 4.1 %copy-start.2 = (f32[288,768]{1,0:T(8,128)}, f32[288,768]{1,0:T(8,128)S(1)}, u32[]{:S(2)}) copy-start(f32[288,768]{1,0:T(8,128)S(1)} %get-tuple-element.95.refs_2_) | copy-start | bytes 2654212
  128.1 0.7 copy-start.9
  128.8 14.6 %collective-permute-start.17 = (bf16[192,4608]{1,0:T(8,128)(2,1)}, bf16[192,4608]{1,0:T(8,128)(2,1)S(1)}, u32[]{:S(2)}, u32[]{:S(2)}) collective-permute-start(bf16[192,4608]{1,0:T(8,128)(2,1)} %collective-permute-done.8.refs_0_), channel_id=1, source_target_pairs={{0,2},{2,0},{4,6},{6,4},{8,10},{10,8},{12,14},{14,12},{16,18},{18,... | collective-permute-start | bytes 5308424 | tf_op jit(solution)/shard_map/ppermute | solution.py:475
  128.8 14.6 %collective-permute-start.18 = (bf16[192,4608]{1,0:T(8,128)(2,1)}, bf16[192,4608]{1,0:T(8,128)(2,1)S(1)}, u32[]{:S(2)}, u32[]{:S(2)}) collective-permute-start(bf16[192,4608]{1,0:T(8,128)(2,1)} %collective-permute-done.9.refs_2_), channel_id=1, source_target_pairs={{0,2},{2,0},{4,6},{6,4},{8,10},{10,8},{12,14},{14,12},{16,18},{18,... | collective-permute-start | bytes 5308424 | tf_op jit(solution)/shard_map/ppermute | solution.py:475
  129.3 12.5 %collective-permute-start.14 = (bf16[288,768]{1,0:T(8,128)(2,1)S(1)}, bf16[288,768]{1,0:T(8,128)(2,1)S(1)}, u32[]{:S(2)}, u32[]{:S(2)}) collective-permute-start(bf16[288,768]{1,0:T(8,128)(2,1)S(1)} %get-tuple-element.88), channel_id=1, source_target_pairs={{0,1},{1,0},{2,3},{3,2},{4,5},{5,4},{6,7},{7,6},{8,9},{9,8},{10,11... | collective-permute-start | bytes 1327112 | tf_op jit(solution)/shard_map/ppermute | solution.py:542
  132.2 21.3 %collective-permute-start.15 = (bf16[96,4608]{1,0:T(8,128)(2,1)S(1)}, bf16[96,4608]{1,0:T(8,128)(2,1)S(1)}, u32[]{:S(2)}, u32[]{:S(2)}) collective-permute-start(bf16[96,4608]{1,0:T(8,128)(2,1)S(1)} %slice.6), channel_id=1, source_target_pairs={{0,4},{2,6},{4,12},{6,14},{12,20},{14,22},{20,28},{22,30},{28,24},... | collective-permute-start | bytes 2654216 | tf_op jit(solution)/shard_map/ppermute | solution.py:471
  133.9 21.0 %collective-permute-start.16 = (bf16[96,4608]{1,0:T(8,128)(2,1)S(1)}, bf16[96,4608]{1,0:T(8,128)(2,1)S(1)}, u32[]{:S(2)}, u32[]{:S(2)}) collective-permute-start(bf16[96,4608]{1,0:T(8,128)(2,1)S(1)} %slice.7), channel_id=1, source_target_pairs={{0,8},{2,10},{4,0},{6,2},{12,4},{14,6},{20,12},{22,14},{28,20},{30... | collective-permute-start | bytes 2654216 | tf_op jit(solution)/shard_map/ppermute | solution.py:471
  140.9 0.9 copy-start.3
  141.8 8.4 %copy-start.7 = (bf16[288,768]{1,0:T(8,128)(2,1)}, bf16[288,768]{1,0:T(8,128)(2,1)S(1)}, u32[]{:S(2)}) copy-start(bf16[288,768]{1,0:T(8,128)(2,1)S(1)} %collective-permute-done.14.refs_3_) | copy-start | bytes 1327108
  141.8 11.4 %collective-permute-start.19 = (bf16[288,768]{1,0:T(8,128)(2,1)S(1)}, bf16[288,768]{1,0:T(8,128)(2,1)S(1)}, u32[]{:S(2)}, u32[]{:S(2)}) collective-permute-start(bf16[288,768]{1,0:T(8,128)(2,1)S(1)} %get-tuple-element.93), channel_id=1, source_target_pairs={{0,1},{1,0},{2,3},{3,2},{4,5},{5,4},{6,7},{7,6},{8,9},{9,8},{10,11... | collective-permute-start | bytes 1327112 | tf_op jit(solution)/shard_map/ppermute | solution.py:542
  150.2 12.7 %copy-start.4 = (f32[288,768]{1,0:T(8,128)}, f32[288,768]{1,0:T(8,128)S(1)}, u32[]{:S(2)}) copy-start(f32[288,768]{1,0:T(8,128)S(1)} %get-tuple-element.104.refs_6_) | copy-start | bytes 2654212
  153.2 9.7 %copy-start.8 = (bf16[288,768]{1,0:T(8,128)(2,1)}, bf16[288,768]{1,0:T(8,128)(2,1)S(1)}, u32[]{:S(2)}) copy-start(bf16[288,768]{1,0:T(8,128)(2,1)S(1)} %collective-permute-done.19.refs_5_) | copy-start | bytes 1327108
  154.9 10.4 %copy-start.11 = (f32[64]{0:T(128)S(1)}, f32[64]{0:T(128)}, u32[]{:S(2)}) copy-start(f32[64]{0:T(128)} %param.32) | copy-start | bytes 772
  154.9 2.4 %collective-permute-start.21 = (bf16[96,4608]{1,0:T(8,128)(2,1)S(1)}, bf16[96,4608]{1,0:T(8,128)(2,1)S(1)}, u32[]{:S(2)}, u32[]{:S(2)}) collective-permute-start(bf16[96,4608]{1,0:T(8,128)(2,1)S(1)} %collective-permute-done.15.refs_0_), channel_id=1, source_target_pairs={{0,2},{2,0},{4,6},{6,4},{8,10},{10,8},{12,14},{14,12},{16,18},{18,... | collective-permute-start | bytes 2654216 | tf_op jit(solution)/shard_map/ppermute | solution.py:475
  154.9 3.7 %collective-permute-start.22 = (bf16[96,4608]{1,0:T(8,128)(2,1)S(1)}, bf16[96,4608]{1,0:T(8,128)(2,1)S(1)}, u32[]{:S(2)}, u32[]{:S(2)}) collective-permute-start(bf16[96,4608]{1,0:T(8,128)(2,1)S(1)} %collective-permute-done.16.refs_2_), channel_id=1, source_target_pairs={{0,2},{2,0},{4,6},{6,4},{8,10},{10,8},{12,14},{14,12},{16,18},{18,... | collective-permute-start | bytes 2654216 | tf_op jit(solution)/shard_map/ppermute | solution.py:475
  155.4 13.4 %collective-permute-start.20 = (bf16[288,768]{1,0:T(8,128)(2,1)}, bf16[288,768]{1,0:T(8,128)(2,1)}, u32[]{:S(2)}, u32[]{:S(2)}) collective-permute-start(bf16[288,768]{1,0:T(8,128)(2,1)} %get-tuple-element.100), channel_id=1, source_target_pairs={{0,1},{1,0},{2,3},{3,2},{4,5},{5,4},{6,7},{7,6},{8,9},{9,8},{10,11... | collective-permute-start | bytes 1327112 | tf_op jit(solution)/shard_map/ppermute | solution.py:542
  163.0 0.8 copy-start.6
  163.7 8.6 %collective-permute-start.23 = (bf16[288,384]{1,0:T(8,128)(2,1)}, bf16[288,384]{1,0:T(8,128)(2,1)S(1)}, u32[]{:S(2)}, u32[]{:S(2)}) collective-permute-start(bf16[288,384]{1,0:T(8,128)(2,1)} %get-tuple-element.109), channel_id=1, source_target_pairs={{0,1},{1,0},{2,3},{3,2},{4,5},{5,4},{6,7},{7,6},{8,9},{9,8},{10,11... | collective-permute-start | bytes 663560 | tf_op jit(solution)/shard_map/ppermute | solution.py:542
  172.4 0.7 copy-start.10
where the time goes:
time: 181 us; the launch traced here: 180 us
  waiting for transfers between devices  77.2 us (43%)
  Pallas kernels  62.2 us (34%)
  starting transfers between devices  21.6 us (12%)
  local copies, waits for them, and re-layouts  14 us (8%)
  other arithmetic  2.78 us (2%)
  between operations  2.3 us (1%)
    ppermute x8, waiting for transfers between devices, hop(): return lax.ppermute(array, 'tile', pairs)  33.6 us
    pallas_call x5, Pallas kernels, project(): pl.pallas_call(functools.partial(project_kernel, layout), in_specs=[pl.Bl...  29.2 us
    ppermute x1, waiting for transfers between devices, paired(): far_attn = trade(sent_attn)  21.2 us
    pallas_call x2, Pallas kernels, attend(): pl.pallas_call(attend_kernel, grid_spec=pltpu.PrefetchScalarGridSpec(num_...  18.5 us
    ppermute x1, waiting for transfers between devices, paired(): far_units = trade(sent_units)  11.9 us
    ppermute x8, starting transfers between devices, hop(): return lax.ppermute(array, 'tile', pairs)  9.16 us
    ppermute x5, waiting for transfers between devices, send(): chunks.append((own, trade(sent)))  8.78 us
    pallas_call x1, Pallas kernels, finish(): pl.pallas_call(functools.partial(finish_kernel, len(chunks)), grid_spec=p...  6.84 us
  transfers between devices with their start and end apart: 24, of which 13 were waited for; matrix products, arithmetic and copies ran while one was open for 5% of the time, Pallas kernels for 31%

commit v1 on v0

--- a/solution.py
+++ b/solution.py
@@ -338,10 +338,11 @@
     )(part, units, *([] if into is None else [into]))
 
 
-def project_kernel(layout, core_ref, attn_ref, act_ref, *refs):
-    pieces, (own_ref, far_ref, w_ref, sems) = refs[:-4], refs[-4:]
+def project_kernel(layout, sides, core_ref, attn_ref, act_ref, *refs):
+    pieces, outs, (w_ref, sems) = refs[: len(layout)], refs[len(layout) : -2], refs[-2:]
     depth = attn_ref.shape[1]
-    rows, columns = own_ref.shape
+    rows, columns = outs[0].shape
+    taken = pl.ds(rows * sides[0], rows * len(sides))
     core = core_ref[0]
     copies = []
     for (base, here, share), piece in zip(layout, pieces):
@@ -355,13 +356,13 @@
         while pending and pending[0] < end:
             copies[-len(pending)].wait()
             pending.pop(0)
-        total = lax.dot_general(attn_ref[...], w_ref[first:end, :depth], NT, preferred_element_type=jnp.float32)
-        total += lax.dot_general(act_ref[...], w_ref[first:end, depth:], NT, preferred_element_type=jnp.float32)
-        own_ref[:, first:end] = total[:rows]
-        far_ref[:, first:end] = total[rows:].astype(jnp.bfloat16)
-
-
-def project(core, attn, act, chips):
+        total = lax.dot_general(attn_ref[taken], w_ref[first:end, :depth], NT, preferred_element_type=jnp.float32)
+        total += lax.dot_general(act_ref[taken], w_ref[first:end, depth:], NT, preferred_element_type=jnp.float32)
+        for index, out_ref in enumerate(outs):
+            out_ref[:, first:end] = total[rows * index : rows * (index + 1)].astype(out_ref.dtype)
+
+
+def project(core, attn, act, chips, sides=(0, 1)):
     share = sum(piece.shape[0] for here, _, piece in chips[0] if here)
     layout, flat = [], []
     for index, pieces in enumerate(chips):
@@ -372,14 +373,11 @@
     columns = 2 * share * len(chips)
     inside = pl.BlockSpec(memory_space=pltpu.VMEM)
     return pl.pallas_call(
-        functools.partial(project_kernel, layout),
+        functools.partial(project_kernel, layout, sides),
         in_specs=[pl.BlockSpec(memory_space=pltpu.SMEM), inside, inside]
         + [pl.BlockSpec(memory_space=pl.ANY)] * len(flat),
-        out_specs=[inside, inside],
-        out_shape=[
-            jax.ShapeDtypeStruct((rows, columns), jnp.float32),
-            jax.ShapeDtypeStruct((rows, columns), jnp.bfloat16),
-        ],
+        out_specs=[inside] * len(sides),
+        out_shape=[jax.ShapeDtypeStruct((rows, columns), jnp.bfloat16)] * len(sides),
         scratch_shapes=[
             pltpu.VMEM((columns, depth), jnp.bfloat16),
             pltpu.SemaphoreType.DMA((len(flat),)),
@@ -406,7 +404,7 @@
             source = place_ref[(mine - behind.pop(0) + places) % places]
             target = pl.ds(pl.multiple_of(chip * source, 128), chip)
             part = slice(first, first + chip)
-            proj_ref[:, target] = own_ref[:, part] + far_ref[:, part].astype(jnp.float32)
+            proj_ref[:, target] = own_ref[:, part].astype(jnp.float32) + far_ref[:, part].astype(jnp.float32)
     updated = stream_ref[0].astype(jnp.float32) + gate_ref[...] * (proj_ref[...] + bias_ref[...])
     hidden_ref[0] = updated.astype(jnp.bfloat16)
 
@@ -542,10 +540,11 @@
         chunks.append((own, trade(sent)))
         return sent
 
-    sent = send(chips[0:1])
+    (sent,) = project(core, attn, act, chips[0:1], (1,))
+    chunks.append([None, trade(sent)])
     attn, sent = lax.optimization_barrier((attn, sent))
     sent = send(chips[1:3])
-    onward, back, attn, sent, chunks[0] = lax.optimization_barrier((onward, back, attn, sent, chunks[0]))
+    onward, back, attn, sent, chunks[0][1] = lax.optimization_barrier((onward, back, attn, sent, chunks[0][1]))
     middle = block.shape[0] // 2
     last = hop(onward[:middle], 1), hop(back[middle:], -1)
     chips += [both_cores(onward), both_cores(back)]
@@ -554,7 +553,9 @@
     sent = send(chips[5:7])
     onward, back, attn, sent, chunks[2] = lax.optimization_barrier((*last, attn, sent, chunks[2]))
     chips.append(both_cores(onward) + both_cores(back, middle))
-    send(chips[7:8])
+    sent = send(chips[7:8])
+    attn, sent = lax.optimization_barrier((attn, sent))
+    (chunks[0][0],) = project(core, attn, act, chips[0:1], (0,))
 
     hidden, following = finish(
         tile[None],

time: 181 us -> 179 us (0.989)
  starting transfers between devices: 21.6 us -> 19.6 us
    ppermute x5 -> x4, starting transfers between devices: 6.65 us -> 3.03 us  [send(): chunks.append((own, trade(sent)))]
    ppermute x5 -> x4, waiting for transfers between devices: 8.78 us -> 5.21 us  [send(): chunks.append((own, trade(sent)))]
    pallas_call x5 -> x6, Pallas kernels: 29.2 us -> 31.4 us  [project(): pl.pallas_call(functools.partial(project_kernel, layout, sides), in_specs...]
  transfers between devices with their start and end apart: 24 -> 24, of which waited for: 13 -> 13; matrix products, arithmetic and copies ran while one was open for 5% -> 5% of each run, Pallas kernels for 31% -> 32%
where the time goes in v1:
time: 179 us; the launch traced here: 178 us
  waiting for transfers between devices  76 us (42%)
  Pallas kernels  64 us (36%)
  starting transfers between devices  19.6 us (11%)
  local copies, waits for them, and re-layouts  13.8 us (8%)
  other arithmetic  2.76 us (2%)
  between operations  2.31 us (1%)
    ppermute x8, waiting for transfers between devices, hop(): return lax.ppermute(array, 'tile', pairs)  35.1 us
    pallas_call x6, Pallas kernels, project(): pl.pallas_call(functools.partial(project_kernel, layout, sides), in_specs...  31.4 us
    ppermute x1, waiting for transfers between devices, paired(): far_attn = trade(sent_attn)  21.2 us
    pallas_call x2, Pallas kernels, attend(): pl.pallas_call(attend_kernel, grid_spec=pltpu.PrefetchScalarGridSpec(num_...  18.5 us
    ppermute x1, waiting for transfers between devices, paired(): far_units = trade(sent_units)  11.8 us
    ppermute x8, starting transfers between devices, hop(): return lax.ppermute(array, 'tile', pairs)  9.16 us
    pallas_call x1, Pallas kernels, finish(): pl.pallas_call(functools.partial(finish_kernel, len(chunks)), grid_spec=p...  6.48 us
    unnamed x24, local copies, waits for them, and re-layouts  5.65 us
  transfers between devices with their start and end apart: 24, of which 13 were waited for; matrix products, arithmetic and copies ran while one was open for 5% of the time, Pallas kernels for 32%

profile of v1, /device:TPU:0, one launch (start us, length us, event | category | flops | bytes accessed | tf_op | source)
XLA Modules:
  0.0 178.5 jit_solution(455555826775971469)
XLA Ops:
  0.6 2.8 %pad_maximum_fusion.refs_0_ = bf16[192,4608]{1,0:T(8,128)(2,1)} fusion(bf16[192,3072]{1,0:T(8,128)(2,1)} %bitcast.32, bf16[192,1536]{1,0:T(8,128)(2,1)} %bitcast.33), kind=kLoop, calls=%fused_computation.1 | loop fusion | flops 3538944 | bytes 3538944 | tf_op jit(solution)/shard_map/concatenate | solution.py:508
  3.4 2.9 %collective-permute-start.1 = (bf16[192,4608]{1,0:T(8,128)(2,1)}, bf16[192,4608]{1,0:T(8,128)(2,1)}, u32[]{:S(2)}, u32[]{:S(2)}) collective-permute-start(bf16[192,4608]{1,0:T(8,128)(2,1)} %pad_maximum_fusion.refs_0_), channel_id=1, source_target_pairs={{0,4},{2,6},{4,12},{6,14},{12,20},{14,22},{20,28},{22,30},{28,24},... | collective-permute-start | bytes 5308424 | tf_op jit(solution)/shard_map/ppermute | solution.py:469
  6.3 0.1 collective-permute-start.2
  6.4 0.0 collective-permute-start.3
  6.4 3.5 %dynamic-slice_bitcast_fusion = bf16[3,3,96,1536]{3,2,1,0:T(8,128)(2,1)} fusion(bf16[1,3,96,3,3072]{4,2,3,1,0:T(8,128)(2,1)} %param.19, s32[]{:T(128)S(6)} %select_n.14), kind=kLoop, calls=%fused_computation | loop fusion | bytes 5308420 | tf_op jit(solution)/shard_map/dynamic_slice | solution.py:507
  9.9 2.0 %collective-permute-start = (bf16[3,3,96,1536]{3,2,1,0:T(8,128)(2,1)}, bf16[3,3,96,1536]{3,2,1,0:T(8,128)(2,1)}, u32[]{:S(2)}, u32[]{:S(2)}) collective-permute-start(bf16[3,3,96,1536]{3,2,1,0:T(8,128)(2,1)} %dynamic-slice_bitcast_fusion), channel_id=1, source_target_pairs={{0,1},{1,0},{2,3},{3,2},{4,5},{5,4},{6,7},{7,6},{8,9},{9,8},{10,11... | collective-permute-start | bytes 7962632 | tf_op jit(solution)/shard_map/ppermute | solution.py:511
  12.5 3.3 %tables.1 = (f32[576,128]{1,0:T(8,128)}, f32[576,128]{1,0:T(8,128)}, f32[576,128]{1,0:T(8,128)}, f32[576,128]{1,0:T(8,128)}, f32[1,576]{1,0:T(1,128)}, /*index=5*/bf16[128,128]{1,0:T(8,128)(2,1)}) custom-call(s32[1]{0:T(128)} %bitcast.2.half_ref.part_ref, s32[1]{0:T(128)S(6)} %copy.26.len_ref, f32[1,128]{1,0:T(1,128)} %constant.39.clone.row_freq_ref, ...), custom_call_target="tpu_custom_call" | custom-call | flops 589824 | bytes 294912 | tf_op jit(solution)/shard_map/tables/pallas_call | solution.py:228
  15.8 2.0 %copy-done.2 = bf16[1,3,96,6144]{3,2,1,0:T(8,128)(2,1)S(1)} copy-done((bf16[1,3,96,6144]{3,2,1,0:T(8,128)(2,1)S(1)}, bf16[1,3,96,6144]{3,2,1,0:T(8,128)(2,1)}, u32[]{:S(2)}) %copy-start.2) | copy-done | bytes 3538968
  17.8 1.4 activate.2.refs_0_
  19.2 1.5 dynamic-slice_bitcast_fusion.1
  20.7 24.7 %collective-permute-done.1.refs_0_ = bf16[192,4608]{1,0:T(8,128)(2,1)} collective-permute-done((bf16[192,4608]{1,0:T(8,128)(2,1)}, bf16[192,4608]{1,0:T(8,128)(2,1)}, u32[]{:S(2)}, u32[]{:S(2)}) %collective-permute-start.1) | collective-permute-done | bytes 1769504 | tf_op jit(solution)/shard_map/ppermute | solution.py:469
  45.3 1.4 collective-permute-done.2.refs_2_
  46.7 0.0 collective-permute-done.3.refs_1_
  46.7 1.6 collective-permute-start.4
  48.3 0.4 collective-permute-start.5
  48.7 0.5 collective-permute-start.7
  49.3 21.2 %collective-permute-done.far_ref = bf16[3,3,96,1536]{3,2,1,0:T(8,128)(2,1)} collective-permute-done((bf16[3,3,96,1536]{3,2,1,0:T(8,128)(2,1)}, bf16[3,3,96,1536]{3,2,1,0:T(8,128)(2,1)}, u32[]{:S(2)}, u32[]{:S(2)}) %collective-permute-start) | collective-permute-done | bytes 2654240 | tf_op jit(solution)/shard_map/ppermute | solution.py:511
  70.4 1.7 collective-permute-start.10
  72.2 9.3 %attend.2.refs_0_ = bf16[576,1536]{1,0:T(8,128)(2,1)} custom-call(s32[1]{0:T(128)} %bitcast.2.half_ref.part_ref, bf16[3,3,96,3072]{3,2,1,0:T(8,128)(2,1)} %bitcast.29, bf16[3,3,96,1536]{3,2,1,0:T(8,128)(2,1)} %collective-permute-done.far_ref, f32[576,128]{1,0:T(8,128)} %get-tuple-element.63.cq_ref, f32[576,128]{1,0:T(8,128)} %get-tuple-element.64.sq_ref, ...), custom_call_target="tpu_custom_call" | custom-call | flops 1019215872 | bytes 7077888 | tf_op jit(solution)/shard_map/attend/pallas_call | solution.py:285
  81.4 4.7 %collective-permute-done.4.refs_0_ = bf16[192,4608]{1,0:T(8,128)(2,1)} collective-permute-done((bf16[192,4608]{1,0:T(8,128)(2,1)}, bf16[192,4608]{1,0:T(8,128)(2,1)}, u32[]{:S(2)}, u32[]{:S(2)}) %collective-permute-start.4) | collective-permute-done | bytes 1769504 | tf_op jit(solution)/shard_map/ppermute | solution.py:469
  86.2 1.3 collective-permute-done.5.refs_2_
  87.5 0.0 collective-permute-done.6.refs_1_
  87.5 0.0 collective-permute-done.7.refs_3_
  87.5 1.6 collective-permute-start.8
  89.1 0.4 collective-permute-start.9
  89.5 0.5 collective-permute-start.15
  90.0 9.3 %attend.3.attn_ref = bf16[576,1536]{1,0:T(8,128)(2,1)} custom-call(s32[1]{0:T(128)} %bitcast.2.half_ref.part_ref, bf16[3,3,96,3072]{3,2,1,0:T(8,128)(2,1)} %bitcast.30, bf16[3,3,96,1536]{3,2,1,0:T(8,128)(2,1)} %collective-permute-done.far_ref, f32[576,128]{1,0:T(8,128)} %get-tuple-element.63.cq_ref, ...), custom_call_target="tpu_custom_call", output_to_operand_aliasing={{}: (9, {})} | custom-call | flops 1019215872 | bytes 7077888 | tf_op jit(solution)/shard_map/attend/pallas_call | solution.py:285
  99.3 11.8 %collective-permute-done.10.units_ref = bf16[3,96,3072]{2,1,0:T(8,128)(2,1)} collective-permute-done((bf16[3,96,3072]{2,1,0:T(8,128)(2,1)}, bf16[3,96,3072]{2,1,0:T(8,128)(2,1)}, u32[]{:S(2)}, u32[]{:S(2)}) %collective-permute-start.10) | collective-permute-done | bytes 1769504 | tf_op jit(solution)/shard_map/ppermute | solution.py:525
  111.1 3.0 %activate.3.act_ref = bf16[576,3072]{1,0:T(8,128)(2,1)S(1)} custom-call(s32[1]{0:T(128)} %constant.38.clone.1.part_ref, bf16[3,96,3072]{2,1,0:T(8,128)(2,1)} %collective-permute-done.10.units_ref, bf16[576,3072]{1,0:T(8,128)(2,1)S(1)} %activate.2.refs_0_), custom_call_target="tpu_custom_call", output_to_operand_aliasing={{}: (2, {})} | custom-call | flops 3538944 | bytes 884736 | tf_op jit(solution)/shard_map/activate/pallas_call | solution.py:322
  114.1 3.6 %project.6 = bf16[288,384]{1,0:T(8,128)(2,1)S(1)} custom-call(s32[1]{0:T(128)} %bitcast.1.core_ref, bf16[576,1536]{1,0:T(8,128)(2,1)S(1)} %copy-done, bf16[576,3072]{1,0:T(8,128)(2,1)S(1)} %activate.3.act_ref, bf16[192,4608]{1,0:T(8,128)(2,1)} %pad_maximum_fusion.refs_0_, bf16[192,4608]{1,0:T(8,128)(2,1)} %collective-permute-done.3.refs_1_), custom_call_target="tpu_custom_call" | custom-call | flops 254803968 | bytes 442368 | tf_op jit(solution)/shard_map/project/pallas_call | solution.py:375
  117.7 1.7 collective-permute-start.11
  119.4 6.5 %project.7 = (bf16[288,768]{1,0:T(8,128)(2,1)S(1)}, bf16[288,768]{1,0:T(8,128)(2,1)S(1)}) custom-call(s32[1]{0:T(128)} %bitcast.1.core_ref, bf16[576,1536]{1,0:T(8,128)(2,1)S(1)} %copy-done, bf16[576,3072]{1,0:T(8,128)(2,1)S(1)} %activate.3.act_ref, bf16[192,4608]{1,0:T(8,128)(2,1)} %collective-permute-done.1.refs_0_, ...), custom_call_target="tpu_custom_call" | custom-call | flops 509607936 | bytes 884736 | tf_op jit(solution)/shard_map/project/pallas_call | solution.py:375
  125.9 0.0 collective-permute-done.11.refs_1_
  126.0 1.1 collective-permute-done.9.refs_2_
  127.1 0.5 collective-permute-start.18
  127.6 1.5 collective-permute-start.16
  129.1 1.2 slice.6
  130.3 1.2 slice.7
  131.6 1.6 collective-permute-start.12
  133.2 0.0 collective-permute-done.15.refs_3_
  133.2 0.5 collective-permute-start.13
  133.7 6.5 %project.8 = (bf16[288,768]{1,0:T(8,128)(2,1)S(1)}, bf16[288,768]{1,0:T(8,128)(2,1)S(1)}) custom-call(s32[1]{0:T(128)} %bitcast.1.core_ref, bf16[576,1536]{1,0:T(8,128)(2,1)S(1)} %copy-done, bf16[576,3072]{1,0:T(8,128)(2,1)S(1)} %activate.3.act_ref, bf16[192,4608]{1,0:T(8,128)(2,1)} %collective-permute-done.4.refs_0_, ...), custom_call_target="tpu_custom_call" | custom-call | flops 509607936 | bytes 884736 | tf_op jit(solution)/shard_map/project/pallas_call | solution.py:375
  140.2 0.8 copy-done.5
  141.0 0.0 collective-permute-done.16.refs_3_
  141.0 0.5 collective-permute-start.19
  141.5 6.8 %project.9 = (bf16[288,768]{1,0:T(8,128)(2,1)S(1)}, bf16[288,768]{1,0:T(8,128)(2,1)}) custom-call(s32[1]{0:T(128)} %bitcast.1.core_ref, bf16[576,1536]{1,0:T(8,128)(2,1)S(1)} %copy-done, bf16[576,3072]{1,0:T(8,128)(2,1)S(1)} %activate.3.act_ref, bf16[192,4608]{1,0:T(8,128)(2,1)} %collective-permute-done.8.refs_0_, ...), custom_call_target="tpu_custom_call" | custom-call | flops 509607936 | bytes 884736 | tf_op jit(solution)/shard_map/project/pallas_call | solution.py:375
  148.3 3.9 %collective-permute-done.19.refs_5_ = bf16[288,768]{1,0:T(8,128)(2,1)S(1)} collective-permute-done((bf16[288,768]{1,0:T(8,128)(2,1)S(1)}, bf16[288,768]{1,0:T(8,128)(2,1)S(1)}, u32[]{:S(2)}, u32[]{:S(2)}) %collective-permute-start.19) | collective-permute-done | bytes 442400 | tf_op jit(solution)/shard_map/ppermute | solution.py:540
  152.3 0.6 collective-permute-done.12.refs_0_
  152.9 1.3 collective-permute-done.13.refs_2_
  154.2 0.0 collective-permute-start.20
  154.2 0.5 collective-permute-start.21
  154.7 0.5 collective-permute-start.22
  155.2 1.4 collective-permute-done.20.refs_1_
  156.6 1.3 collective-permute-done.21.refs_3_
  157.9 4.4 %project.10 = (bf16[288,384]{1,0:T(8,128)(2,1)S(1)}, bf16[288,384]{1,0:T(8,128)(2,1)}) custom-call(s32[1]{0:T(128)} %bitcast.1.core_ref, bf16[576,1536]{1,0:T(8,128)(2,1)S(1)} %copy-done, bf16[576,3072]{1,0:T(8,128)(2,1)S(1)} %activate.3.act_ref, bf16[96,4608]{1,0:T(8,128)(2,1)S(1)} %collective-permute-done.12.refs_0_, ...), custom_call_target="tpu_custom_call" | custom-call | flops 254803968 | bytes 442368 | tf_op jit(solution)/shard_map/project/pallas_call | solution.py:375
  162.3 0.7 copy-done.7
  163.0 0.5 collective-permute-start.23
  163.5 0.7 copy.23.refs_16_
  164.8 0.0 copy-start.1
  164.8 1.5 copy-done.1
  166.3 3.6 %project.11.refs_0_ = bf16[288,384]{1,0:T(8,128)(2,1)S(1)} custom-call(s32[1]{0:T(128)} %bitcast.1.core_ref, bf16[576,1536]{1,0:T(8,128)(2,1)S(1)} %copy-done.1, bf16[576,3072]{1,0:T(8,128)(2,1)S(1)} %activate.3.act_ref, bf16[192,4608]{1,0:T(8,128)(2,1)} %pad_maximum_fusion.refs_0_, bf16[192,4608]{1,0:T(8,128)(2,1)} %collective-permute-done.3.refs_1_), custom_call_target="tpu_custom_call" | custom-call | flops 254803968 | bytes 442368 | tf_op jit(solution)/shard_map/project/pallas_call | solution.py:375
  169.9 0.7 copy-done.3
  170.6 1.3 collective-permute-done.23.refs_9_
  171.9 6.5 %finish.1 = (bf16[3,96,3072]{2,1,0:T(8,128)(2,1)}, f32[2,64,96]{2,1,0:T(8,128)}) custom-call(s32[1]{0:T(128)} %bitcast.tile_ref, s32[16]{0:T(128)} %constant.41.clone.place_ref, f32[1]{0:T(128)S(6)} %copy.27.step_ref, bf16[288,384]{1,0:T(8,128)(2,1)} %copy-done.3, bf16[288,384]{1,0:T(8,128)(2,1)} %copy-done.10, bf16[288,768]{1,0:T(8,128)(2,1)} %copy-done.4, ...), custom_call_target="tpu_custom_call" | custom-call | flops 141557760 | bytes 8847360 | tf_op jit(solution)/shard_map/finish/pallas_call | solution.py:431
  (26 shorter events, 0.1 us)
Async XLA Ops:
  3.4 41.9 %collective-permute-start.1 = (bf16[192,4608]{1,0:T(8,128)(2,1)}, bf16[192,4608]{1,0:T(8,128)(2,1)}, u32[]{:S(2)}, u32[]{:S(2)}) collective-permute-start(bf16[192,4608]{1,0:T(8,128)(2,1)} %pad_maximum_fusion.refs_0_), channel_id=1, source_target_pairs={{0,4},{2,6},{4,12},{6,14},{12,20},{14,22},{20,28},{22,30},{28,24},... | collective-permute-start | bytes 5308424 | tf_op jit(solution)/shard_map/ppermute | solution.py:469
  6.3 40.4 %collective-permute-start.2 = (bf16[192,4608]{1,0:T(8,128)(2,1)}, bf16[192,4608]{1,0:T(8,128)(2,1)}, u32[]{:S(2)}, u32[]{:S(2)}) collective-permute-start(bf16[192,4608]{1,0:T(8,128)(2,1)} %pad_maximum_fusion.refs_0_), channel_id=1, source_target_pairs={{0,8},{2,10},{4,0},{6,2},{12,4},{14,6},{20,12},{22,14},{28,20},{30... | collective-permute-start | bytes 5308424 | tf_op jit(solution)/shard_map/ppermute | solution.py:469
  6.4 40.3 %collective-permute-start.3 = (bf16[192,4608]{1,0:T(8,128)(2,1)}, bf16[192,4608]{1,0:T(8,128)(2,1)}, u32[]{:S(2)}, u32[]{:S(2)}) collective-permute-start(bf16[192,4608]{1,0:T(8,128)(2,1)} %pad_maximum_fusion.refs_0_), channel_id=1, source_target_pairs={{0,2},{2,0},{4,6},{6,4},{8,10},{10,8},{12,14},{14,12},{16,18},{18,... | collective-permute-start | bytes 5308424 | tf_op jit(solution)/shard_map/ppermute | solution.py:473
  9.9 60.5 %collective-permute-start = (bf16[3,3,96,1536]{3,2,1,0:T(8,128)(2,1)}, bf16[3,3,96,1536]{3,2,1,0:T(8,128)(2,1)}, u32[]{:S(2)}, u32[]{:S(2)}) collective-permute-start(bf16[3,3,96,1536]{3,2,1,0:T(8,128)(2,1)} %dynamic-slice_bitcast_fusion), channel_id=1, source_target_pairs={{0,1},{1,0},{2,3},{3,2},{4,5},{5,4},{6,7},{7,6},{8,9},{9,8},{10,11... | collective-permute-start | bytes 7962632 | tf_op jit(solution)/shard_map/ppermute | solution.py:511
  15.8 2.0 %copy-start.2 = (bf16[1,3,96,6144]{3,2,1,0:T(8,128)(2,1)S(1)}, bf16[1,3,96,6144]{3,2,1,0:T(8,128)(2,1)}, u32[]{:S(2)}) copy-start(bf16[1,3,96,6144]{3,2,1,0:T(8,128)(2,1)} %param.20) | copy-start | bytes 10616836
  46.7 39.5 %collective-permute-start.4 = (bf16[192,4608]{1,0:T(8,128)(2,1)}, bf16[192,4608]{1,0:T(8,128)(2,1)}, u32[]{:S(2)}, u32[]{:S(2)}) collective-permute-start(bf16[192,4608]{1,0:T(8,128)(2,1)} %collective-permute-done.1.refs_0_), channel_id=1, source_target_pairs={{0,4},{2,6},{4,12},{6,14},{12,20},{14,22},{20,28},{22,30},{28,24},... | collective-permute-start | bytes 5308424 | tf_op jit(solution)/shard_map/ppermute | solution.py:469
  48.3 39.2 %collective-permute-start.5 = (bf16[192,4608]{1,0:T(8,128)(2,1)}, bf16[192,4608]{1,0:T(8,128)(2,1)}, u32[]{:S(2)}, u32[]{:S(2)}) collective-permute-start(bf16[192,4608]{1,0:T(8,128)(2,1)} %collective-permute-done.2.refs_2_), channel_id=1, source_target_pairs={{0,8},{2,10},{4,0},{6,2},{12,4},{14,6},{20,12},{22,14},{28,20},{30... | collective-permute-start | bytes 5308424 | tf_op jit(solution)/shard_map/ppermute | solution.py:469
  48.7 38.7 %collective-permute-start.6 = (bf16[192,4608]{1,0:T(8,128)(2,1)}, bf16[192,4608]{1,0:T(8,128)(2,1)}, u32[]{:S(2)}, u32[]{:S(2)}) collective-permute-start(bf16[192,4608]{1,0:T(8,128)(2,1)} %collective-permute-done.1.refs_0_), channel_id=1, source_target_pairs={{0,2},{2,0},{4,6},{6,4},{8,10},{10,8},{12,14},{14,12},{16,18},{18,... | collective-permute-start | bytes 5308424 | tf_op jit(solution)/shard_map/ppermute | solution.py:473
  48.7 38.7 %collective-permute-start.7 = (bf16[192,4608]{1,0:T(8,128)(2,1)}, bf16[192,4608]{1,0:T(8,128)(2,1)}, u32[]{:S(2)}, u32[]{:S(2)}) collective-permute-start(bf16[192,4608]{1,0:T(8,128)(2,1)} %collective-permute-done.2.refs_2_), channel_id=1, source_target_pairs={{0,2},{2,0},{4,6},{6,4},{8,10},{10,8},{12,14},{14,12},{16,18},{18,... | collective-permute-start | bytes 5308424 | tf_op jit(solution)/shard_map/ppermute | solution.py:473
  70.4 40.7 %collective-permute-start.10 = (bf16[3,96,3072]{2,1,0:T(8,128)(2,1)}, bf16[3,96,3072]{2,1,0:T(8,128)(2,1)}, u32[]{:S(2)}, u32[]{:S(2)}) collective-permute-start(bf16[3,96,3072]{2,1,0:T(8,128)(2,1)} %dynamic-slice_bitcast_fusion.1), channel_id=1, source_target_pairs={{0,1},{1,0},{2,3},{3,2},{4,5},{5,4},{6,7},{7,6},{8,9},{9,8},{10,11... | collective-permute-start | bytes 5308424 | tf_op jit(solution)/shard_map/ppermute | solution.py:525
  87.5 38.5 %collective-permute-start.8 = (bf16[192,4608]{1,0:T(8,128)(2,1)}, bf16[192,4608]{1,0:T(8,128)(2,1)}, u32[]{:S(2)}, u32[]{:S(2)}) collective-permute-start(bf16[192,4608]{1,0:T(8,128)(2,1)} %collective-permute-done.4.refs_0_), channel_id=1, source_target_pairs={{0,4},{2,6},{4,12},{6,14},{12,20},{14,22},{20,28},{22,30},{28,24},... | collective-permute-start | bytes 5308424 | tf_op jit(solution)/shard_map/ppermute | solution.py:469
  89.1 38.0 %collective-permute-start.9 = (bf16[192,4608]{1,0:T(8,128)(2,1)}, bf16[192,4608]{1,0:T(8,128)(2,1)}, u32[]{:S(2)}, u32[]{:S(2)}) collective-permute-start(bf16[192,4608]{1,0:T(8,128)(2,1)} %collective-permute-done.5.refs_2_), channel_id=1, source_target_pairs={{0,8},{2,10},{4,0},{6,2},{12,4},{14,6},{20,12},{22,14},{28,20},{30... | collective-permute-start | bytes 5308424 | tf_op jit(solution)/shard_map/ppermute | solution.py:469
  89.5 42.0 %collective-permute-start.14 = (bf16[192,4608]{1,0:T(8,128)(2,1)}, bf16[192,4608]{1,0:T(8,128)(2,1)}, u32[]{:S(2)}, u32[]{:S(2)}) collective-permute-start(bf16[192,4608]{1,0:T(8,128)(2,1)} %collective-permute-done.4.refs_0_), channel_id=1, source_target_pairs={{0,2},{2,0},{4,6},{6,4},{8,10},{10,8},{12,14},{14,12},{16,18},{18,... | collective-permute-start | bytes 5308424 | tf_op jit(solution)/shard_map/ppermute | solution.py:473
  89.5 43.7 %collective-permute-start.15 = (bf16[192,4608]{1,0:T(8,128)(2,1)}, bf16[192,4608]{1,0:T(8,128)(2,1)}, u32[]{:S(2)}, u32[]{:S(2)}) collective-permute-start(bf16[192,4608]{1,0:T(8,128)(2,1)} %collective-permute-done.5.refs_2_), channel_id=1, source_target_pairs={{0,2},{2,0},{4,6},{6,4},{8,10},{10,8},{12,14},{14,12},{16,18},{18,... | collective-permute-start | bytes 5308424 | tf_op jit(solution)/shard_map/ppermute | solution.py:473
  99.3 14.8 %copy-start = (bf16[576,1536]{1,0:T(8,128)(2,1)S(1)}, bf16[576,1536]{1,0:T(8,128)(2,1)}, u32[]{:S(2)}) copy-start(bf16[576,1536]{1,0:T(8,128)(2,1)} %attend.3.attn_ref) | copy-start | bytes 5308420
  117.7 8.2 %collective-permute-start.11 = (bf16[288,384]{1,0:T(8,128)(2,1)S(1)}, bf16[288,384]{1,0:T(8,128)(2,1)S(1)}, u32[]{:S(2)}, u32[]{:S(2)}) collective-permute-start(bf16[288,384]{1,0:T(8,128)(2,1)S(1)} %project.6), channel_id=1, source_target_pairs={{0,1},{1,0},{2,3},{3,2},{4,5},{5,4},{6,7},{7,6},{8,9},{9,8},{10,11... | collective-permute-start | bytes 663560 | tf_op jit(solution)/shard_map/ppermute | solution.py:544
  125.9 5.6 %copy-start.4 = (bf16[288,768]{1,0:T(8,128)(2,1)}, bf16[288,768]{1,0:T(8,128)(2,1)S(1)}, u32[]{:S(2)}) copy-start(bf16[288,768]{1,0:T(8,128)(2,1)S(1)} %get-tuple-element.100.refs_2_) | copy-start | bytes 1327108
  125.9 1.1 copy-start.10
  127.1 14.4 %collective-permute-start.17 = (bf16[192,4608]{1,0:T(8,128)(2,1)}, bf16[192,4608]{1,0:T(8,128)(2,1)S(1)}, u32[]{:S(2)}, u32[]{:S(2)}) collective-permute-start(bf16[192,4608]{1,0:T(8,128)(2,1)} %collective-permute-done.8.refs_0_), channel_id=1, source_target_pairs={{0,2},{2,0},{4,6},{6,4},{8,10},{10,8},{12,14},{14,12},{16,18},{18,... | collective-permute-start | bytes 5308424 | tf_op jit(solution)/shard_map/ppermute | solution.py:473
  127.1 14.4 %collective-permute-start.18 = (bf16[192,4608]{1,0:T(8,128)(2,1)}, bf16[192,4608]{1,0:T(8,128)(2,1)S(1)}, u32[]{:S(2)}, u32[]{:S(2)}) collective-permute-start(bf16[192,4608]{1,0:T(8,128)(2,1)} %collective-permute-done.9.refs_2_), channel_id=1, source_target_pairs={{0,2},{2,0},{4,6},{6,4},{8,10},{10,8},{12,14},{14,12},{16,18},{18,... | collective-permute-start | bytes 5308424 | tf_op jit(solution)/shard_map/ppermute | solution.py:473
  127.6 13.4 %collective-permute-start.16 = (bf16[288,768]{1,0:T(8,128)(2,1)S(1)}, bf16[288,768]{1,0:T(8,128)(2,1)S(1)}, u32[]{:S(2)}, u32[]{:S(2)}) collective-permute-start(bf16[288,768]{1,0:T(8,128)(2,1)S(1)} %get-tuple-element.85), channel_id=1, source_target_pairs={{0,1},{1,0},{2,3},{3,2},{4,5},{5,4},{6,7},{7,6},{8,9},{9,8},{10,11... | collective-permute-start | bytes 1327112 | tf_op jit(solution)/shard_map/ppermute | solution.py:540
  131.6 21.3 %collective-permute-start.12 = (bf16[96,4608]{1,0:T(8,128)(2,1)S(1)}, bf16[96,4608]{1,0:T(8,128)(2,1)S(1)}, u32[]{:S(2)}, u32[]{:S(2)}) collective-permute-start(bf16[96,4608]{1,0:T(8,128)(2,1)S(1)} %slice.6), channel_id=1, source_target_pairs={{0,4},{2,6},{4,12},{6,14},{12,20},{14,22},{20,28},{22,30},{28,24},... | collective-permute-start | bytes 2654216 | tf_op jit(solution)/shard_map/ppermute | solution.py:469
  133.2 21.0 %collective-permute-start.13 = (bf16[96,4608]{1,0:T(8,128)(2,1)S(1)}, bf16[96,4608]{1,0:T(8,128)(2,1)S(1)}, u32[]{:S(2)}, u32[]{:S(2)}) collective-permute-start(bf16[96,4608]{1,0:T(8,128)(2,1)S(1)} %slice.7), channel_id=1, source_target_pairs={{0,8},{2,10},{4,0},{6,2},{12,4},{14,6},{20,12},{22,14},{28,20},{30... | collective-permute-start | bytes 2654216 | tf_op jit(solution)/shard_map/ppermute | solution.py:469
  140.2 0.8 copy-start.5
  141.0 7.3 %copy-start.8 = (bf16[288,768]{1,0:T(8,128)(2,1)}, bf16[288,768]{1,0:T(8,128)(2,1)S(1)}, u32[]{:S(2)}) copy-start(bf16[288,768]{1,0:T(8,128)(2,1)S(1)} %collective-permute-done.16.refs_3_) | copy-start | bytes 1327108
  141.0 11.2 %collective-permute-start.19 = (bf16[288,768]{1,0:T(8,128)(2,1)S(1)}, bf16[288,768]{1,0:T(8,128)(2,1)S(1)}, u32[]{:S(2)}, u32[]{:S(2)}) collective-permute-start(bf16[288,768]{1,0:T(8,128)(2,1)S(1)} %get-tuple-element.89), channel_id=1, source_target_pairs={{0,1},{1,0},{2,3},{3,2},{4,5},{5,4},{6,7},{7,6},{8,9},{9,8},{10,11... | collective-permute-start | bytes 1327112 | tf_op jit(solution)/shard_map/ppermute | solution.py:540
  148.3 14.0 %copy-start.6 = (bf16[288,768]{1,0:T(8,128)(2,1)}, bf16[288,768]{1,0:T(8,128)(2,1)S(1)}, u32[]{:S(2)}) copy-start(bf16[288,768]{1,0:T(8,128)(2,1)S(1)} %get-tuple-element.104.refs_6_) | copy-start | bytes 1327108
  152.3 10.0 %copy-start.9 = (bf16[288,768]{1,0:T(8,128)(2,1)}, bf16[288,768]{1,0:T(8,128)(2,1)S(1)}, u32[]{:S(2)}) copy-start(bf16[288,768]{1,0:T(8,128)(2,1)S(1)} %collective-permute-done.19.refs_5_) | copy-start | bytes 1327108
  154.2 9.3 %copy-start.11 = (f32[64]{0:T(128)S(1)}, f32[64]{0:T(128)}, u32[]{:S(2)}) copy-start(f32[64]{0:T(128)} %param.32) | copy-start | bytes 772
  154.2 2.4 %collective-permute-start.20 = (bf16[96,4608]{1,0:T(8,128)(2,1)S(1)}, bf16[96,4608]{1,0:T(8,128)(2,1)S(1)}, u32[]{:S(2)}, u32[]{:S(2)}) collective-permute-start(bf16[96,4608]{1,0:T(8,128)(2,1)S(1)} %collective-permute-done.12.refs_0_), channel_id=1, source_target_pairs={{0,2},{2,0},{4,6},{6,4},{8,10},{10,8},{12,14},{14,12},{16,18},{18,... | collective-permute-start | bytes 2654216 | tf_op jit(solution)/shard_map/ppermute | solution.py:473
  154.2 3.7 %collective-permute-start.21 = (bf16[96,4608]{1,0:T(8,128)(2,1)S(1)}, bf16[96,4608]{1,0:T(8,128)(2,1)S(1)}, u32[]{:S(2)}, u32[]{:S(2)}) collective-permute-start(bf16[96,4608]{1,0:T(8,128)(2,1)S(1)} %collective-permute-done.13.refs_2_), channel_id=1, source_target_pairs={{0,2},{2,0},{4,6},{6,4},{8,10},{10,8},{12,14},{14,12},{16,18},{18,... | collective-permute-start | bytes 2654216 | tf_op jit(solution)/shard_map/ppermute | solution.py:473
  154.7 15.9 %collective-permute-start.22 = (bf16[288,768]{1,0:T(8,128)(2,1)}, bf16[288,768]{1,0:T(8,128)(2,1)}, u32[]{:S(2)}, u32[]{:S(2)}) collective-permute-start(bf16[288,768]{1,0:T(8,128)(2,1)} %get-tuple-element.92), channel_id=1, source_target_pairs={{0,1},{1,0},{2,3},{3,2},{4,5},{5,4},{6,7},{7,6},{8,9},{9,8},{10,11... | collective-permute-start | bytes 1327112 | tf_op jit(solution)/shard_map/ppermute | solution.py:540
  162.3 0.7 copy-start.7
  163.0 8.9 %collective-permute-start.23 = (bf16[288,384]{1,0:T(8,128)(2,1)}, bf16[288,384]{1,0:T(8,128)(2,1)}, u32[]{:S(2)}, u32[]{:S(2)}) collective-permute-start(bf16[288,384]{1,0:T(8,128)(2,1)} %get-tuple-element.97), channel_id=1, source_target_pairs={{0,1},{1,0},{2,3},{3,2},{4,5},{5,4},{6,7},{7,6},{8,9},{9,8},{10,11... | collective-permute-start | bytes 663560 | tf_op jit(solution)/shard_map/ppermute | solution.py:540
  164.8 1.5 copy-start.1
  169.9 0.7 copy-start.3

commit v2 on v1

--- a/solution.py
+++ b/solution.py
@@ -176,6 +176,7 @@
 EPS = 1e-06
 SCALE = math.log2(math.e) / math.sqrt(HEAD_DIM)
 VMEM = 60 * 1024 * 1024
+LIGHT = 24 * 1024 * 1024
 LESS = 34 * 1024 * 1024
 NT = (((1,), (1,)), ((), ()))
 
@@ -451,7 +452,7 @@
             jax.ShapeDtypeStruct(stream.shape, jnp.bfloat16),
             jax.ShapeDtypeStruct(latent.shape, jnp.float32),
         ],
-        compiler_params=pltpu.CompilerParams(vmem_limit_bytes=VMEM),
+        compiler_params=pltpu.CompilerParams(vmem_limit_bytes=LIGHT),
         cost_estimate=pl.CostEstimate(
             flops=blocks * slots * width * 160, bytes_accessed=blocks * slots * width * 10, transcendentals=0
         ),

time: 179 us -> 178 us (level)
    unnamed x24 -> x54, local copies, waits for them, and re-layouts: 5.65 us -> 5.73 us
  transfers between devices with their start and end apart: 24 -> 24, of which waited for: 13 -> 13; matrix products, arithmetic and copies ran while one was open for 5% -> 5% of each run, Pallas kernels for 32% -> 33%
where the time goes in v2:
time: 178 us; the launch traced here: 177 us
  waiting for transfers between devices  75.7 us (43%)
  Pallas kernels  63 us (35%)
  starting transfers between devices  19.6 us (11%)
  local copies, waits for them, and re-layouts  13.8 us (8%)
  other arithmetic  2.78 us (2%)
  between operations  2.35 us (1%)
    ppermute x8, waiting for transfers between devices, hop(): return lax.ppermute(array, 'tile', pairs)  34.7 us
    pallas_call x6, Pallas kernels, project(): pl.pallas_call(functools.partial(project_kernel, layout, sides), in_specs...  31.5 us
    ppermute x1, waiting for transfers between devices, paired(): far_attn = trade(sent_attn)  21.1 us
    pallas_call x2, Pallas kernels, attend(): pl.pallas_call(attend_kernel, grid_spec=pltpu.PrefetchScalarGridSpec(num_...  18.5 us
    ppermute x1, waiting for transfers between devices, paired(): far_units = trade(sent_units)  11.7 us
    ppermute x8, starting transfers between devices, hop(): return lax.ppermute(array, 'tile', pairs)  9.16 us
    unnamed x54, local copies, waits for them, and re-layouts  5.73 us
    ppermute x4, waiting for transfers between devices, send(): chunks.append((own, trade(sent)))  5.56 us
  transfers between devices with their start and end apart: 24, of which 13 were waited for; matrix products, arithmetic and copies ran while one was open for 5% of the time, Pallas kernels for 33%

profile of v2, /device:TPU:0, one launch (start us, length us, event | category | flops | bytes accessed | tf_op | source)
XLA Modules:
  0.0 177.2 jit_solution(10788725659135294024)
XLA Ops:
  0.6 2.8 %pad_maximum_fusion.refs_0_ = bf16[192,4608]{1,0:T(8,128)(2,1)} fusion(bf16[192,3072]{1,0:T(8,128)(2,1)} %bitcast.35, bf16[192,1536]{1,0:T(8,128)(2,1)} %bitcast.36), kind=kLoop, calls=%fused_computation.1 | loop fusion | flops 3538944 | bytes 3538944 | tf_op jit(solution)/shard_map/concatenate | solution.py:509
  3.4 2.9 %collective-permute-start.1 = (bf16[192,4608]{1,0:T(8,128)(2,1)}, bf16[192,4608]{1,0:T(8,128)(2,1)}, u32[]{:S(2)}, u32[]{:S(2)}) collective-permute-start(bf16[192,4608]{1,0:T(8,128)(2,1)} %pad_maximum_fusion.refs_0_), channel_id=1, source_target_pairs={{0,4},{2,6},{4,12},{6,14},{12,20},{14,22},{20,28},{22,30},{28,24},... | collective-permute-start | bytes 5308424 | tf_op jit(solution)/shard_map/ppermute | solution.py:470
  6.4 0.1 collective-permute-start.2
  6.4 3.4 %dynamic-slice_bitcast_fusion = bf16[3,3,96,1536]{3,2,1,0:T(8,128)(2,1)} fusion(bf16[1,3,96,3,3072]{4,2,3,1,0:T(8,128)(2,1)} %param.19, s32[]{:T(128)S(6)} %select_n.14), kind=kLoop, calls=%fused_computation | loop fusion | bytes 5308420 | tf_op jit(solution)/shard_map/dynamic_slice | solution.py:508
  9.8 2.0 %collective-permute-start = (bf16[3,3,96,1536]{3,2,1,0:T(8,128)(2,1)}, bf16[3,3,96,1536]{3,2,1,0:T(8,128)(2,1)}, u32[]{:S(2)}, u32[]{:S(2)}) collective-permute-start(bf16[3,3,96,1536]{3,2,1,0:T(8,128)(2,1)} %dynamic-slice_bitcast_fusion), channel_id=1, source_target_pairs={{0,1},{1,0},{2,3},{3,2},{4,5},{5,4},{6,7},{7,6},{8,9},{9,8},{10,11... | collective-permute-start | bytes 7962632 | tf_op jit(solution)/shard_map/ppermute | solution.py:512
  12.5 3.3 %tables.1 = (f32[576,128]{1,0:T(8,128)}, f32[576,128]{1,0:T(8,128)}, f32[576,128]{1,0:T(8,128)}, f32[576,128]{1,0:T(8,128)}, f32[1,576]{1,0:T(1,128)}, /*index=5*/bf16[128,128]{1,0:T(8,128)(2,1)}) custom-call(s32[1]{0:T(128)} %bitcast.2.half_ref.part_ref, s32[1]{0:T(128)S(6)} %copy.26.len_ref, f32[1,128]{1,0:T(1,128)} %constant.39.clone.row_freq_ref, ...), custom_call_target="tpu_custom_call" | custom-call | flops 589824 | bytes 294912 | tf_op jit(solution)/shard_map/tables/pallas_call | solution.py:229
  15.8 2.0 %copy-done.2 = bf16[1,3,96,6144]{3,2,1,0:T(8,128)(2,1)S(1)} copy-done((bf16[1,3,96,6144]{3,2,1,0:T(8,128)(2,1)S(1)}, bf16[1,3,96,6144]{3,2,1,0:T(8,128)(2,1)}, u32[]{:S(2)}) %copy-start.2) | copy-done | bytes 3538968
  17.8 1.4 activate.2.refs_0_
  19.2 1.5 dynamic-slice_bitcast_fusion.1
  20.7 24.7 %collective-permute-done.1.refs_0_ = bf16[192,4608]{1,0:T(8,128)(2,1)} collective-permute-done((bf16[192,4608]{1,0:T(8,128)(2,1)}, bf16[192,4608]{1,0:T(8,128)(2,1)}, u32[]{:S(2)}, u32[]{:S(2)}) %collective-permute-start.1) | collective-permute-done | bytes 1769504 | tf_op jit(solution)/shard_map/ppermute | solution.py:470
  45.4 1.4 collective-permute-done.2.refs_2_
  46.7 1.6 collective-permute-start.4
  48.3 0.4 collective-permute-start.5
  48.8 0.5 collective-permute-start.7
  49.3 21.1 %collective-permute-done.far_ref = bf16[3,3,96,1536]{3,2,1,0:T(8,128)(2,1)} collective-permute-done((bf16[3,3,96,1536]{3,2,1,0:T(8,128)(2,1)}, bf16[3,3,96,1536]{3,2,1,0:T(8,128)(2,1)}, u32[]{:S(2)}, u32[]{:S(2)}) %collective-permute-start) | collective-permute-done | bytes 2654240 | tf_op jit(solution)/shard_map/ppermute | solution.py:512
  70.4 1.7 collective-permute-start.10
  72.1 9.3 %attend.2.refs_0_ = bf16[576,1536]{1,0:T(8,128)(2,1)} custom-call(s32[1]{0:T(128)} %bitcast.2.half_ref.part_ref, bf16[3,3,96,3072]{3,2,1,0:T(8,128)(2,1)} %bitcast.33, bf16[3,3,96,1536]{3,2,1,0:T(8,128)(2,1)} %collective-permute-done.far_ref, f32[576,128]{1,0:T(8,128)} %get-tuple-element.63.cq_ref, f32[576,128]{1,0:T(8,128)} %get-tuple-element.64.sq_ref, ...), custom_call_target="tpu_custom_call" | custom-call | flops 1019215872 | bytes 7077888 | tf_op jit(solution)/shard_map/attend/pallas_call | solution.py:286
  81.4 4.8 %collective-permute-done.4.refs_0_ = bf16[192,4608]{1,0:T(8,128)(2,1)} collective-permute-done((bf16[192,4608]{1,0:T(8,128)(2,1)}, bf16[192,4608]{1,0:T(8,128)(2,1)}, u32[]{:S(2)}, u32[]{:S(2)}) %collective-permute-start.4) | collective-permute-done | bytes 1769504 | tf_op jit(solution)/shard_map/ppermute | solution.py:470
  86.2 1.3 collective-permute-done.5.refs_2_
  87.5 1.6 collective-permute-start.8
  89.1 0.4 collective-permute-start.9
  89.5 0.5 collective-permute-start.15
  90.1 9.3 %attend.3.attn_ref = bf16[576,1536]{1,0:T(8,128)(2,1)} custom-call(s32[1]{0:T(128)} %bitcast.2.half_ref.part_ref, bf16[3,3,96,3072]{3,2,1,0:T(8,128)(2,1)} %bitcast.34, bf16[3,3,96,1536]{3,2,1,0:T(8,128)(2,1)} %collective-permute-done.far_ref, f32[576,128]{1,0:T(8,128)} %get-tuple-element.63.cq_ref, ...), custom_call_target="tpu_custom_call", output_to_operand_aliasing={{}: (9, {})} | custom-call | flops 1019215872 | bytes 7077888 | tf_op jit(solution)/shard_map/attend/pallas_call | solution.py:286
  99.3 11.7 %collective-permute-done.10.units_ref = bf16[3,96,3072]{2,1,0:T(8,128)(2,1)} collective-permute-done((bf16[3,96,3072]{2,1,0:T(8,128)(2,1)}, bf16[3,96,3072]{2,1,0:T(8,128)(2,1)}, u32[]{:S(2)}, u32[]{:S(2)}) %collective-permute-start.10) | collective-permute-done | bytes 1769504 | tf_op jit(solution)/shard_map/ppermute | solution.py:526
  111.1 3.0 %activate.3.act_ref = bf16[576,3072]{1,0:T(8,128)(2,1)S(1)} custom-call(s32[1]{0:T(128)} %constant.38.clone.1.part_ref, bf16[3,96,3072]{2,1,0:T(8,128)(2,1)} %collective-permute-done.10.units_ref, bf16[576,3072]{1,0:T(8,128)(2,1)S(1)} %activate.2.refs_0_), custom_call_target="tpu_custom_call", output_to_operand_aliasing={{}: (2, {})} | custom-call | flops 3538944 | bytes 884736 | tf_op jit(solution)/shard_map/activate/pallas_call | solution.py:323
  114.0 3.6 %project.6 = bf16[288,384]{1,0:T(8,128)(2,1)S(1)} custom-call(s32[1]{0:T(128)} %bitcast.1.core_ref, bf16[576,1536]{1,0:T(8,128)(2,1)S(1)} %copy-done, bf16[576,3072]{1,0:T(8,128)(2,1)S(1)} %activate.3.act_ref, bf16[192,4608]{1,0:T(8,128)(2,1)} %pad_maximum_fusion.refs_0_, bf16[192,4608]{1,0:T(8,128)(2,1)} %collective-permute-done.3.refs_1_), custom_call_target="tpu_custom_call" | custom-call | flops 254803968 | bytes 442368 | tf_op jit(solution)/shard_map/project/pallas_call | solution.py:376
  117.6 1.7 collective-permute-start.11
  119.3 6.5 %project.7 = (bf16[288,768]{1,0:T(8,128)(2,1)S(1)}, bf16[288,768]{1,0:T(8,128)(2,1)S(1)}) custom-call(s32[1]{0:T(128)} %bitcast.1.core_ref, bf16[576,1536]{1,0:T(8,128)(2,1)S(1)} %copy-done, bf16[576,3072]{1,0:T(8,128)(2,1)S(1)} %activate.3.act_ref, bf16[192,4608]{1,0:T(8,128)(2,1)} %collective-permute-done.1.refs_0_, ...), custom_call_target="tpu_custom_call" | custom-call | flops 509607936 | bytes 884736 | tf_op jit(solution)/shard_map/project/pallas_call | solution.py:376
  125.9 0.7 copy-done.15
  126.6 0.5 collective-permute-done.9.refs_2_
  127.1 0.5 collective-permute-start.18
  127.6 1.5 collective-permute-start.16
  129.1 1.2 slice.6
  130.3 1.2 slice.7
  131.6 1.6 collective-permute-start.12
  133.2 0.5 collective-permute-start.13
  133.7 6.5 %project.8 = (bf16[288,768]{1,0:T(8,128)(2,1)S(1)}, bf16[288,768]{1,0:T(8,128)(2,1)S(1)}) custom-call(s32[1]{0:T(128)} %bitcast.1.core_ref, bf16[576,1536]{1,0:T(8,128)(2,1)S(1)} %copy-done, bf16[576,3072]{1,0:T(8,128)(2,1)S(1)} %activate.3.act_ref, bf16[192,4608]{1,0:T(8,128)(2,1)} %collective-permute-done.4.refs_0_, ...), custom_call_target="tpu_custom_call" | custom-call | flops 509607936 | bytes 884736 | tf_op jit(solution)/shard_map/project/pallas_call | solution.py:376
  140.2 0.7 copy-done.8
  141.0 0.5 collective-permute-start.19
  141.5 6.8 %project.9 = (bf16[288,768]{1,0:T(8,128)(2,1)S(1)}, bf16[288,768]{1,0:T(8,128)(2,1)}) custom-call(s32[1]{0:T(128)} %bitcast.1.core_ref, bf16[576,1536]{1,0:T(8,128)(2,1)S(1)} %copy-done, bf16[576,3072]{1,0:T(8,128)(2,1)S(1)} %activate.3.act_ref, bf16[192,4608]{1,0:T(8,128)(2,1)} %collective-permute-done.8.refs_0_, ...), custom_call_target="tpu_custom_call" | custom-call | flops 509607936 | bytes 884736 | tf_op jit(solution)/shard_map/project/pallas_call | solution.py:376
  148.3 3.9 %collective-permute-done.19.refs_5_ = bf16[288,768]{1,0:T(8,128)(2,1)S(1)} collective-permute-done((bf16[288,768]{1,0:T(8,128)(2,1)S(1)}, bf16[288,768]{1,0:T(8,128)(2,1)S(1)}, u32[]{:S(2)}, u32[]{:S(2)}) %collective-permute-start.19) | collective-permute-done | bytes 442400 | tf_op jit(solution)/shard_map/ppermute | solution.py:541
  152.2 0.7 collective-permute-done.12.refs_0_
  152.9 1.3 collective-permute-done.13.refs_2_
  154.2 0.5 collective-permute-start.21
  154.7 0.5 collective-permute-start.22
  155.2 1.4 collective-permute-done.20.refs_1_
  156.7 1.3 collective-permute-done.21.refs_3_
  157.9 4.4 %project.10 = (bf16[288,384]{1,0:T(8,128)(2,1)S(1)}, bf16[288,384]{1,0:T(8,128)(2,1)}) custom-call(s32[1]{0:T(128)} %bitcast.1.core_ref, bf16[576,1536]{1,0:T(8,128)(2,1)S(1)} %copy-done, bf16[576,3072]{1,0:T(8,128)(2,1)S(1)} %activate.3.act_ref, bf16[96,4608]{1,0:T(8,128)(2,1)S(1)} %collective-permute-done.12.refs_0_, ...), custom_call_target="tpu_custom_call" | custom-call | flops 254803968 | bytes 442368 | tf_op jit(solution)/shard_map/project/pallas_call | solution.py:376
  162.3 0.7 copy-done.17
  163.0 0.5 collective-permute-start.23
  163.5 0.7 copy.23.refs_16_
  164.9 0.0 copy-start.1
  164.9 1.5 copy-done.1
  166.4 0.0 copy-start.14
  166.4 0.0 copy-start.19
  166.4 0.0 copy-start.20
  166.4 0.0 copy-start.21
  166.4 0.0 copy-start.22
  166.5 0.0 copy-start.23
  166.5 0.0 copy-start.24
  166.5 0.0 copy-start.25
  166.5 3.7 %project.11.refs_0_ = bf16[288,384]{1,0:T(8,128)(2,1)S(1)} custom-call(s32[1]{0:T(128)} %bitcast.1.core_ref, bf16[576,1536]{1,0:T(8,128)(2,1)S(1)} %copy-done.1, bf16[576,3072]{1,0:T(8,128)(2,1)S(1)} %activate.3.act_ref, bf16[192,4608]{1,0:T(8,128)(2,1)} %pad_maximum_fusion.refs_0_, bf16[192,4608]{1,0:T(8,128)(2,1)} %collective-permute-done.3.refs_1_), custom_call_target="tpu_custom_call" | custom-call | flops 254803968 | bytes 442368 | tf_op jit(solution)/shard_map/project/pallas_call | solution.py:376
  170.2 1.6 collective-permute-done.23.refs_9_
  172.0 5.2 %finish.1 = (bf16[3,96,3072]{2,1,0:T(8,128)(2,1)}, f32[2,64,96]{2,1,0:T(8,128)}) custom-call(s32[1]{0:T(128)} %bitcast.tile_ref, s32[16]{0:T(128)S(1)} %copy-done.25, f32[1]{0:T(128)S(6)} %copy.27.step_ref, bf16[288,384]{1,0:T(8,128)(2,1)S(1)} %project.11.refs_0_, bf16[288,384]{1,0:T(8,128)(2,1)S(1)} %copy-done.16, bf16[288,768]{1,0:T(8,128)(2,1)S(1)} %copy-done.5, ...), custom_call_target="tpu_custom_call" | custom-call | flops 141557760 | bytes 8847360 | tf_op jit(solution)/shard_map/finish/pallas_call | solution.py:432
  (56 shorter events, 0.1 us)
Async XLA Ops:
  3.4 41.9 %collective-permute-start.1 = (bf16[192,4608]{1,0:T(8,128)(2,1)}, bf16[192,4608]{1,0:T(8,128)(2,1)}, u32[]{:S(2)}, u32[]{:S(2)}) collective-permute-start(bf16[192,4608]{1,0:T(8,128)(2,1)} %pad_maximum_fusion.refs_0_), channel_id=1, source_target_pairs={{0,4},{2,6},{4,12},{6,14},{12,20},{14,22},{20,28},{22,30},{28,24},... | collective-permute-start | bytes 5308424 | tf_op jit(solution)/shard_map/ppermute | solution.py:470
  6.4 40.4 %collective-permute-start.2 = (bf16[192,4608]{1,0:T(8,128)(2,1)}, bf16[192,4608]{1,0:T(8,128)(2,1)}, u32[]{:S(2)}, u32[]{:S(2)}) collective-permute-start(bf16[192,4608]{1,0:T(8,128)(2,1)} %pad_maximum_fusion.refs_0_), channel_id=1, source_target_pairs={{0,8},{2,10},{4,0},{6,2},{12,4},{14,6},{20,12},{22,14},{28,20},{30... | collective-permute-start | bytes 5308424 | tf_op jit(solution)/shard_map/ppermute | solution.py:470
  6.4 40.3 %collective-permute-start.3 = (bf16[192,4608]{1,0:T(8,128)(2,1)}, bf16[192,4608]{1,0:T(8,128)(2,1)}, u32[]{:S(2)}, u32[]{:S(2)}) collective-permute-start(bf16[192,4608]{1,0:T(8,128)(2,1)} %pad_maximum_fusion.refs_0_), channel_id=1, source_target_pairs={{0,2},{2,0},{4,6},{6,4},{8,10},{10,8},{12,14},{14,12},{16,18},{18,... | collective-permute-start | bytes 5308424 | tf_op jit(solution)/shard_map/ppermute | solution.py:474
  9.8 60.5 %collective-permute-start = (bf16[3,3,96,1536]{3,2,1,0:T(8,128)(2,1)}, bf16[3,3,96,1536]{3,2,1,0:T(8,128)(2,1)}, u32[]{:S(2)}, u32[]{:S(2)}) collective-permute-start(bf16[3,3,96,1536]{3,2,1,0:T(8,128)(2,1)} %dynamic-slice_bitcast_fusion), channel_id=1, source_target_pairs={{0,1},{1,0},{2,3},{3,2},{4,5},{5,4},{6,7},{7,6},{8,9},{9,8},{10,11... | collective-permute-start | bytes 7962632 | tf_op jit(solution)/shard_map/ppermute | solution.py:512
  15.8 2.0 %copy-start.2 = (bf16[1,3,96,6144]{3,2,1,0:T(8,128)(2,1)S(1)}, bf16[1,3,96,6144]{3,2,1,0:T(8,128)(2,1)}, u32[]{:S(2)}) copy-start(bf16[1,3,96,6144]{3,2,1,0:T(8,128)(2,1)} %param.20) | copy-start | bytes 10616836
  46.7 39.5 %collective-permute-start.4 = (bf16[192,4608]{1,0:T(8,128)(2,1)}, bf16[192,4608]{1,0:T(8,128)(2,1)}, u32[]{:S(2)}, u32[]{:S(2)}) collective-permute-start(bf16[192,4608]{1,0:T(8,128)(2,1)} %collective-permute-done.1.refs_0_), channel_id=1, source_target_pairs={{0,4},{2,6},{4,12},{6,14},{12,20},{14,22},{20,28},{22,30},{28,24},... | collective-permute-start | bytes 5308424 | tf_op jit(solution)/shard_map/ppermute | solution.py:470
  48.3 39.2 %collective-permute-start.5 = (bf16[192,4608]{1,0:T(8,128)(2,1)}, bf16[192,4608]{1,0:T(8,128)(2,1)}, u32[]{:S(2)}, u32[]{:S(2)}) collective-permute-start(bf16[192,4608]{1,0:T(8,128)(2,1)} %collective-permute-done.2.refs_2_), channel_id=1, source_target_pairs={{0,8},{2,10},{4,0},{6,2},{12,4},{14,6},{20,12},{22,14},{28,20},{30... | collective-permute-start | bytes 5308424 | tf_op jit(solution)/shard_map/ppermute | solution.py:470
  48.8 38.7 %collective-permute-start.6 = (bf16[192,4608]{1,0:T(8,128)(2,1)}, bf16[192,4608]{1,0:T(8,128)(2,1)}, u32[]{:S(2)}, u32[]{:S(2)}) collective-permute-start(bf16[192,4608]{1,0:T(8,128)(2,1)} %collective-permute-done.1.refs_0_), channel_id=1, source_target_pairs={{0,2},{2,0},{4,6},{6,4},{8,10},{10,8},{12,14},{14,12},{16,18},{18,... | collective-permute-start | bytes 5308424 | tf_op jit(solution)/shard_map/ppermute | solution.py:474
  48.8 38.7 %collective-permute-start.7 = (bf16[192,4608]{1,0:T(8,128)(2,1)}, bf16[192,4608]{1,0:T(8,128)(2,1)}, u32[]{:S(2)}, u32[]{:S(2)}) collective-permute-start(bf16[192,4608]{1,0:T(8,128)(2,1)} %collective-permute-done.2.refs_2_), channel_id=1, source_target_pairs={{0,2},{2,0},{4,6},{6,4},{8,10},{10,8},{12,14},{14,12},{16,18},{18,... | collective-permute-start | bytes 5308424 | tf_op jit(solution)/shard_map/ppermute | solution.py:474
  70.4 40.7 %collective-permute-start.10 = (bf16[3,96,3072]{2,1,0:T(8,128)(2,1)}, bf16[3,96,3072]{2,1,0:T(8,128)(2,1)}, u32[]{:S(2)}, u32[]{:S(2)}) collective-permute-start(bf16[3,96,3072]{2,1,0:T(8,128)(2,1)} %dynamic-slice_bitcast_fusion.1), channel_id=1, source_target_pairs={{0,1},{1,0},{2,3},{3,2},{4,5},{5,4},{6,7},{7,6},{8,9},{9,8},{10,11... | collective-permute-start | bytes 5308424 | tf_op jit(solution)/shard_map/ppermute | solution.py:526
  87.5 39.1 %collective-permute-start.8 = (bf16[192,4608]{1,0:T(8,128)(2,1)}, bf16[192,4608]{1,0:T(8,128)(2,1)}, u32[]{:S(2)}, u32[]{:S(2)}) collective-permute-start(bf16[192,4608]{1,0:T(8,128)(2,1)} %collective-permute-done.4.refs_0_), channel_id=1, source_target_pairs={{0,4},{2,6},{4,12},{6,14},{12,20},{14,22},{20,28},{22,30},{28,24},... | collective-permute-start | bytes 5308424 | tf_op jit(solution)/shard_map/ppermute | solution.py:470
  89.1 38.0 %collective-permute-start.9 = (bf16[192,4608]{1,0:T(8,128)(2,1)}, bf16[192,4608]{1,0:T(8,128)(2,1)}, u32[]{:S(2)}, u32[]{:S(2)}) collective-permute-start(bf16[192,4608]{1,0:T(8,128)(2,1)} %collective-permute-done.5.refs_2_), channel_id=1, source_target_pairs={{0,8},{2,10},{4,0},{6,2},{12,4},{14,6},{20,12},{22,14},{28,20},{30... | collective-permute-start | bytes 5308424 | tf_op jit(solution)/shard_map/ppermute | solution.py:470
  89.5 42.0 %collective-permute-start.14 = (bf16[192,4608]{1,0:T(8,128)(2,1)}, bf16[192,4608]{1,0:T(8,128)(2,1)}, u32[]{:S(2)}, u32[]{:S(2)}) collective-permute-start(bf16[192,4608]{1,0:T(8,128)(2,1)} %collective-permute-done.4.refs_0_), channel_id=1, source_target_pairs={{0,2},{2,0},{4,6},{6,4},{8,10},{10,8},{12,14},{14,12},{16,18},{18,... | collective-permute-start | bytes 5308424 | tf_op jit(solution)/shard_map/ppermute | solution.py:474
  89.5 43.7 %collective-permute-start.15 = (bf16[192,4608]{1,0:T(8,128)(2,1)}, bf16[192,4608]{1,0:T(8,128)(2,1)}, u32[]{:S(2)}, u32[]{:S(2)}) collective-permute-start(bf16[192,4608]{1,0:T(8,128)(2,1)} %collective-permute-done.5.refs_2_), channel_id=1, source_target_pairs={{0,2},{2,0},{4,6},{6,4},{8,10},{10,8},{12,14},{14,12},{16,18},{18,... | collective-permute-start | bytes 5308424 | tf_op jit(solution)/shard_map/ppermute | solution.py:474
  99.3 14.7 %copy-start = (bf16[576,1536]{1,0:T(8,128)(2,1)S(1)}, bf16[576,1536]{1,0:T(8,128)(2,1)}, u32[]{:S(2)}) copy-start(bf16[576,1536]{1,0:T(8,128)(2,1)} %attend.3.attn_ref) | copy-start | bytes 5308420
  117.6 8.2 %collective-permute-start.11 = (bf16[288,384]{1,0:T(8,128)(2,1)S(1)}, bf16[288,384]{1,0:T(8,128)(2,1)S(1)}, u32[]{:S(2)}, u32[]{:S(2)}) collective-permute-start(bf16[288,384]{1,0:T(8,128)(2,1)S(1)} %project.6), channel_id=1, source_target_pairs={{0,1},{1,0},{2,3},{3,2},{4,5},{5,4},{6,7},{7,6},{8,9},{9,8},{10,11... | collective-permute-start | bytes 663560 | tf_op jit(solution)/shard_map/ppermute | solution.py:545
  125.8 5.7 %copy-start.4 = (bf16[288,768]{1,0:T(8,128)(2,1)}, bf16[288,768]{1,0:T(8,128)(2,1)S(1)}, u32[]{:S(2)}) copy-start(bf16[288,768]{1,0:T(8,128)(2,1)S(1)} %get-tuple-element.100.refs_2_) | copy-start | bytes 1327108
  125.9 0.7 copy-start.15
  127.1 14.4 %collective-permute-start.17 = (bf16[192,4608]{1,0:T(8,128)(2,1)}, bf16[192,4608]{1,0:T(8,128)(2,1)S(1)}, u32[]{:S(2)}, u32[]{:S(2)}) collective-permute-start(bf16[192,4608]{1,0:T(8,128)(2,1)} %collective-permute-done.8.refs_0_), channel_id=1, source_target_pairs={{0,2},{2,0},{4,6},{6,4},{8,10},{10,8},{12,14},{14,12},{16,18},{18,... | collective-permute-start | bytes 5308424 | tf_op jit(solution)/shard_map/ppermute | solution.py:474
  127.1 14.4 %collective-permute-start.18 = (bf16[192,4608]{1,0:T(8,128)(2,1)}, bf16[192,4608]{1,0:T(8,128)(2,1)S(1)}, u32[]{:S(2)}, u32[]{:S(2)}) collective-permute-start(bf16[192,4608]{1,0:T(8,128)(2,1)} %collective-permute-done.9.refs_2_), channel_id=1, source_target_pairs={{0,2},{2,0},{4,6},{6,4},{8,10},{10,8},{12,14},{14,12},{16,18},{18,... | collective-permute-start | bytes 5308424 | tf_op jit(solution)/shard_map/ppermute | solution.py:474
  127.6 13.4 %collective-permute-start.16 = (bf16[288,768]{1,0:T(8,128)(2,1)S(1)}, bf16[288,768]{1,0:T(8,128)(2,1)S(1)}, u32[]{:S(2)}, u32[]{:S(2)}) collective-permute-start(bf16[288,768]{1,0:T(8,128)(2,1)S(1)} %get-tuple-element.85), channel_id=1, source_target_pairs={{0,1},{1,0},{2,3},{3,2},{4,5},{5,4},{6,7},{7,6},{8,9},{9,8},{10,11... | collective-permute-start | bytes 1327112 | tf_op jit(solution)/shard_map/ppermute | solution.py:541
  131.6 21.3 %collective-permute-start.12 = (bf16[96,4608]{1,0:T(8,128)(2,1)S(1)}, bf16[96,4608]{1,0:T(8,128)(2,1)S(1)}, u32[]{:S(2)}, u32[]{:S(2)}) collective-permute-start(bf16[96,4608]{1,0:T(8,128)(2,1)S(1)} %slice.6), channel_id=1, source_target_pairs={{0,4},{2,6},{4,12},{6,14},{12,20},{14,22},{20,28},{22,30},{28,24},... | collective-permute-start | bytes 2654216 | tf_op jit(solution)/shard_map/ppermute | solution.py:470
  133.2 21.0 %collective-permute-start.13 = (bf16[96,4608]{1,0:T(8,128)(2,1)S(1)}, bf16[96,4608]{1,0:T(8,128)(2,1)S(1)}, u32[]{:S(2)}, u32[]{:S(2)}) collective-permute-start(bf16[96,4608]{1,0:T(8,128)(2,1)S(1)} %slice.7), channel_id=1, source_target_pairs={{0,8},{2,10},{4,0},{6,2},{12,4},{14,6},{20,12},{22,14},{28,20},{30... | collective-permute-start | bytes 2654216 | tf_op jit(solution)/shard_map/ppermute | solution.py:470
  140.2 0.8 copy-start.8
  141.0 7.3 %copy-start.6 = (bf16[288,768]{1,0:T(8,128)(2,1)}, bf16[288,768]{1,0:T(8,128)(2,1)S(1)}, u32[]{:S(2)}) copy-start(bf16[288,768]{1,0:T(8,128)(2,1)S(1)} %collective-permute-done.16.refs_3_) | copy-start | bytes 1327108
  141.0 11.2 %collective-permute-start.19 = (bf16[288,768]{1,0:T(8,128)(2,1)S(1)}, bf16[288,768]{1,0:T(8,128)(2,1)S(1)}, u32[]{:S(2)}, u32[]{:S(2)}) collective-permute-start(bf16[288,768]{1,0:T(8,128)(2,1)S(1)} %get-tuple-element.89), channel_id=1, source_target_pairs={{0,1},{1,0},{2,3},{3,2},{4,5},{5,4},{6,7},{7,6},{8,9},{9,8},{10,11... | collective-permute-start | bytes 1327112 | tf_op jit(solution)/shard_map/ppermute | solution.py:541
  148.3 14.0 %copy-start.12 = (bf16[288,768]{1,0:T(8,128)(2,1)}, bf16[288,768]{1,0:T(8,128)(2,1)S(1)}, u32[]{:S(2)}) copy-start(bf16[288,768]{1,0:T(8,128)(2,1)S(1)} %get-tuple-element.104.refs_6_) | copy-start | bytes 1327108
  152.2 10.1 %copy-start.10 = (bf16[288,768]{1,0:T(8,128)(2,1)}, bf16[288,768]{1,0:T(8,128)(2,1)S(1)}, u32[]{:S(2)}) copy-start(bf16[288,768]{1,0:T(8,128)(2,1)S(1)} %collective-permute-done.19.refs_5_) | copy-start | bytes 1327108
  154.2 9.3 %copy-start.26 = (f32[64]{0:T(128)S(1)}, f32[64]{0:T(128)}, u32[]{:S(2)}) copy-start(f32[64]{0:T(128)} %param.32) | copy-start | bytes 772
  154.2 2.4 %collective-permute-start.20 = (bf16[96,4608]{1,0:T(8,128)(2,1)S(1)}, bf16[96,4608]{1,0:T(8,128)(2,1)S(1)}, u32[]{:S(2)}, u32[]{:S(2)}) collective-permute-start(bf16[96,4608]{1,0:T(8,128)(2,1)S(1)} %collective-permute-done.12.refs_0_), channel_id=1, source_target_pairs={{0,2},{2,0},{4,6},{6,4},{8,10},{10,8},{12,14},{14,12},{16,18},{18,... | collective-permute-start | bytes 2654216 | tf_op jit(solution)/shard_map/ppermute | solution.py:474
  154.2 3.7 %collective-permute-start.21 = (bf16[96,4608]{1,0:T(8,128)(2,1)S(1)}, bf16[96,4608]{1,0:T(8,128)(2,1)S(1)}, u32[]{:S(2)}, u32[]{:S(2)}) collective-permute-start(bf16[96,4608]{1,0:T(8,128)(2,1)S(1)} %collective-permute-done.13.refs_2_), channel_id=1, source_target_pairs={{0,2},{2,0},{4,6},{6,4},{8,10},{10,8},{12,14},{14,12},{16,18},{18,... | collective-permute-start | bytes 2654216 | tf_op jit(solution)/shard_map/ppermute | solution.py:474
  154.7 15.5 %collective-permute-start.22 = (bf16[288,768]{1,0:T(8,128)(2,1)}, bf16[288,768]{1,0:T(8,128)(2,1)}, u32[]{:S(2)}, u32[]{:S(2)}) collective-permute-start(bf16[288,768]{1,0:T(8,128)(2,1)} %get-tuple-element.92), channel_id=1, source_target_pairs={{0,1},{1,0},{2,3},{3,2},{4,5},{5,4},{6,7},{7,6},{8,9},{9,8},{10,11... | collective-permute-start | bytes 1327112 | tf_op jit(solution)/shard_map/ppermute | solution.py:541
  162.3 0.7 copy-start.17
  163.0 8.9 %collective-permute-start.23 = (bf16[288,384]{1,0:T(8,128)(2,1)}, bf16[288,384]{1,0:T(8,128)(2,1)}, u32[]{:S(2)}, u32[]{:S(2)}) collective-permute-start(bf16[288,384]{1,0:T(8,128)(2,1)} %get-tuple-element.97), channel_id=1, source_target_pairs={{0,1},{1,0},{2,3},{3,2},{4,5},{5,4},{6,7},{7,6},{8,9},{9,8},{10,11... | collective-permute-start | bytes 663560 | tf_op jit(solution)/shard_map/ppermute | solution.py:541
  164.9 1.5 copy-start.1
  166.3 5.5 %copy-start.3 = (bf16[1,3,96,3072]{3,2,1,0:T(8,128)(2,1)S(1)}, bf16[1,3,96,3072]{3,2,1,0:T(8,128)(2,1)}, u32[]{:S(2)}) copy-start(bf16[1,3,96,3072]{3,2,1,0:T(8,128)(2,1)} %param.21) | copy-start | bytes 5308420
  166.3 5.5 %copy-start.5 = (bf16[288,768]{1,0:T(8,128)(2,1)S(1)}, bf16[288,768]{1,0:T(8,128)(2,1)}, u32[]{:S(2)}) copy-start(bf16[288,768]{1,0:T(8,128)(2,1)} %copy-done.4) | copy-start | bytes 1327108
  166.3 5.5 %copy-start.7 = (bf16[288,768]{1,0:T(8,128)(2,1)S(1)}, bf16[288,768]{1,0:T(8,128)(2,1)}, u32[]{:S(2)}) copy-start(bf16[288,768]{1,0:T(8,128)(2,1)} %copy-done.6) | copy-start | bytes 1327108
  166.4 5.5 %copy-start.9 = (bf16[288,768]{1,0:T(8,128)(2,1)S(1)}, bf16[288,768]{1,0:T(8,128)(2,1)}, u32[]{:S(2)}) copy-start(bf16[288,768]{1,0:T(8,128)(2,1)} %copy-done.8) | copy-start | bytes 1327108
  166.4 5.5 %copy-start.11 = (bf16[288,768]{1,0:T(8,128)(2,1)S(1)}, bf16[288,768]{1,0:T(8,128)(2,1)}, u32[]{:S(2)}) copy-start(bf16[288,768]{1,0:T(8,128)(2,1)} %copy-done.10) | copy-start | bytes 1327108
  166.4 5.5 %copy-start.13 = (bf16[288,768]{1,0:T(8,128)(2,1)S(1)}, bf16[288,768]{1,0:T(8,128)(2,1)}, u32[]{:S(2)}) copy-start(bf16[288,768]{1,0:T(8,128)(2,1)} %copy-done.12) | copy-start | bytes 1327108
  166.4 5.5 %copy-start.14 = (bf16[3072,64]{0,1:T(8,128)(2,1)S(1)}, bf16[3072,64]{0,1:T(8,128)(2,1)}, u32[]{:S(2)}) copy-start(bf16[3072,64]{0,1:T(8,128)(2,1)} %param.31) | copy-start | bytes 1179652
  166.4 5.5 %copy-start.16 = (bf16[288,384]{1,0:T(8,128)(2,1)S(1)}, bf16[288,384]{1,0:T(8,128)(2,1)}, u32[]{:S(2)}) copy-start(bf16[288,384]{1,0:T(8,128)(2,1)} %copy-done.15) | copy-start | bytes 663556
  166.4 5.5 %copy-start.18 = (bf16[288,384]{1,0:T(8,128)(2,1)S(1)}, bf16[288,384]{1,0:T(8,128)(2,1)}, u32[]{:S(2)}) copy-start(bf16[288,384]{1,0:T(8,128)(2,1)} %copy-done.17) | copy-start | bytes 663556
  166.4 5.5 %copy-start.19 = (f32[64,1]{1,0:T(8,128)S(1)}, f32[64,1]{1,0:T(8,128)}, u32[]{:S(2)}) copy-start(f32[64,1]{1,0:T(8,128)} %copy.23.refs_16_) | copy-start | bytes 772
  166.4 5.5 %copy-start.20 = (f32[1,2,96,64]{2,3,1,0:T(8,128)S(1)}, f32[1,2,96,64]{2,3,1,0:T(8,128)}, u32[]{:S(2)}) copy-start(f32[1,2,96,64]{2,3,1,0:T(8,128)} %param.33) | copy-start | bytes 147460
  166.4 5.5 %copy-start.21 = (f32[3072]{0:T(1024)S(1)}, f32[3072]{0:T(1024)}, u32[]{:S(2)}) copy-start(f32[3072]{0:T(1024)} %param.27) | copy-start | bytes 36868
  166.4 5.5 %copy-start.22 = (f32[1,3072]{1,0:T(1,128)S(1)}, f32[1,3072]{1,0:T(1,128)}, u32[]{:S(2)}) copy-start(f32[1,3072]{1,0:T(1,128)} %refs_12_.1) | copy-start | bytes 36868
  166.5 5.5 %copy-start.23 = (f32[1,3072]{1,0:T(1,128)S(1)}, f32[1,3072]{1,0:T(1,128)}, u32[]{:S(2)}) copy-start(f32[1,3072]{1,0:T(1,128)} %refs_13_.1) | copy-start | bytes 36868
  166.5 5.5 %copy-start.24 = (f32[1,3072]{1,0:T(1,128)S(1)}, f32[1,3072]{1,0:T(1,128)}, u32[]{:S(2)}) copy-start(f32[1,3072]{1,0:T(1,128)} %refs_14_.1) | copy-start | bytes 36868
  166.5 5.5 %copy-start.25 = (s32[16]{0:T(128)S(1)}, s32[16]{0:T(128)}, u32[]{:S(2)}) copy-start(s32[16]{0:T(128)} %constant.41.clone.place_ref) | copy-start | bytes 196

commit v3 on v2

--- a/solution.py
+++ b/solution.py
@@ -396,27 +396,38 @@
     (
         stream_ref, bias_ref, gate_ref, scale_ref, shift_ref, w_ref, b_ref, latent_ref, hidden_ref, next_ref, proj_ref,
     ) = refs[2 * chunks :]
+    slots, width = proj_ref.shape
     places = len(PATH)
-    chip = proj_ref.shape[1] // places
+    chip = width // places
     mine = place_ref[places + tile_ref[0] // 2]
     behind = [0] + [distance for step in range(1, places // 2) for distance in (step, -step)] + [places // 2]
+    total = jnp.zeros((slots, chip), jnp.float32)
     for own_ref, far_ref in pairs:
         for first in range(0, own_ref.shape[1], chip):
             source = place_ref[(mine - behind.pop(0) + places) % places]
             target = pl.ds(pl.multiple_of(chip * source, 128), chip)
             part = slice(first, first + chip)
-            proj_ref[:, target] = own_ref[:, part].astype(jnp.float32) + far_ref[:, part].astype(jnp.float32)
-    updated = stream_ref[0].astype(jnp.float32) + gate_ref[...] * (proj_ref[...] + bias_ref[...])
-    hidden_ref[0] = updated.astype(jnp.bfloat16)
+            proj = own_ref[:, part].astype(jnp.float32) + far_ref[:, part].astype(jnp.float32)
+            updated = stream_ref[0, :, target].astype(jnp.float32) + gate_ref[:, target] * (proj + bias_ref[:, target])
+            hidden_ref[0, :, target] = updated.astype(jnp.bfloat16)
+            proj_ref[:, target] = updated
+            total += updated
 
     @pl.when(pl.program_id(0) > 0)
     def _():
-        center = updated - jnp.mean(updated, axis=-1, keepdims=True)
-        variance = jnp.mean(center * center, axis=-1, keepdims=True)
-        normed = center * lax.rsqrt(variance + EPS)
-        modulated = ((1.0 + scale_ref[...]) * normed + shift_ref[...]).astype(jnp.bfloat16)
-        velocity = lax.dot_general(w_ref[...], modulated, NT, preferred_element_type=jnp.float32)
-        next_ref[0] = latent_ref[0] + step_ref[0] * (velocity + b_ref[...])
+        parts = [slice(chip * index, chip * (index + 1)) for index in range(places)]
+        mean = jnp.sum(total, axis=-1, keepdims=True) / width
+        square = jnp.zeros((slots, chip), jnp.float32)
+        for part in parts:
+            center = proj_ref[:, part] - mean
+            square += center * center
+        inverse = lax.rsqrt(jnp.sum(square, axis=-1, keepdims=True) / width + EPS)
+        velocity = b_ref[...]
+        for part in parts:
+            normed = (proj_ref[:, part] - mean) * inverse
+            modulated = ((1.0 + scale_ref[:, part]) * normed + shift_ref[:, part]).astype(jnp.bfloat16)
+            velocity += lax.dot_general(w_ref[:, part], modulated, NT, preferred_element_type=jnp.float32)
+        next_ref[0] = latent_ref[0] + step_ref[0] * velocity
 
 
 def finish(tile, step, chunks, stream, bias, gate, scale, shift, w_final, b_final, latent):

time: 178 us -> 178 us (level)
  no operation moved by 1% of the time
where the time goes in v3:
time: 178 us; the launch traced here: 177 us
  waiting for transfers between devices  75.7 us (43%)
  Pallas kernels  62.9 us (35%)
  starting transfers between devices  19.6 us (11%)
  local copies, waits for them, and re-layouts  13.8 us (8%)
  other arithmetic  2.78 us (2%)
  between operations  2.35 us (1%)
    ppermute x8, waiting for transfers between devices, hop(): return lax.ppermute(array, 'tile', pairs)  34.7 us
    pallas_call x6, Pallas kernels, project(): pl.pallas_call(functools.partial(project_kernel, layout, sides), in_specs...  31.5 us
    ppermute x1, waiting for transfers between devices, paired(): far_attn = trade(sent_attn)  21.1 us
    pallas_call x2, Pallas kernels, attend(): pl.pallas_call(attend_kernel, grid_spec=pltpu.PrefetchScalarGridSpec(num_...  18.5 us
    ppermute x1, waiting for transfers between devices, paired(): far_units = trade(sent_units)  11.7 us
    ppermute x8, starting transfers between devices, hop(): return lax.ppermute(array, 'tile', pairs)  9.16 us
    unnamed x54, local copies, waits for them, and re-layouts  5.73 us
    ppermute x4, waiting for transfers between devices, send(): chunks.append((own, trade(sent)))  5.56 us
  transfers between devices with their start and end apart: 24, of which 13 were waited for; matrix products, arithmetic and copies ran while one was open for 5% of the time, Pallas kernels for 33%

profile of v3, /device:TPU:0, one launch (start us, length us, event | category | flops | bytes accessed | tf_op | source)
XLA Modules:
  0.0 177.2 jit_solution(859799655918705651)
XLA Ops:
  0.6 2.8 %pad_maximum_fusion.refs_0_ = bf16[192,4608]{1,0:T(8,128)(2,1)} fusion(bf16[192,3072]{1,0:T(8,128)(2,1)} %bitcast.35, bf16[192,1536]{1,0:T(8,128)(2,1)} %bitcast.36), kind=kLoop, calls=%fused_computation.1 | loop fusion | flops 3538944 | bytes 3538944 | tf_op jit(solution)/shard_map/concatenate | solution.py:520
  3.4 2.9 %collective-permute-start.1 = (bf16[192,4608]{1,0:T(8,128)(2,1)}, bf16[192,4608]{1,0:T(8,128)(2,1)}, u32[]{:S(2)}, u32[]{:S(2)}) collective-permute-start(bf16[192,4608]{1,0:T(8,128)(2,1)} %pad_maximum_fusion.refs_0_), channel_id=1, source_target_pairs={{0,4},{2,6},{4,12},{6,14},{12,20},{14,22},{20,28},{22,30},{28,24},... | collective-permute-start | bytes 5308424 | tf_op jit(solution)/shard_map/ppermute | solution.py:481
  6.4 0.1 collective-permute-start.2
  6.4 3.4 %dynamic-slice_bitcast_fusion = bf16[3,3,96,1536]{3,2,1,0:T(8,128)(2,1)} fusion(bf16[1,3,96,3,3072]{4,2,3,1,0:T(8,128)(2,1)} %param.19, s32[]{:T(128)S(6)} %select_n.14), kind=kLoop, calls=%fused_computation | loop fusion | bytes 5308420 | tf_op jit(solution)/shard_map/dynamic_slice | solution.py:519
  9.8 2.0 %collective-permute-start = (bf16[3,3,96,1536]{3,2,1,0:T(8,128)(2,1)}, bf16[3,3,96,1536]{3,2,1,0:T(8,128)(2,1)}, u32[]{:S(2)}, u32[]{:S(2)}) collective-permute-start(bf16[3,3,96,1536]{3,2,1,0:T(8,128)(2,1)} %dynamic-slice_bitcast_fusion), channel_id=1, source_target_pairs={{0,1},{1,0},{2,3},{3,2},{4,5},{5,4},{6,7},{7,6},{8,9},{9,8},{10,11... | collective-permute-start | bytes 7962632 | tf_op jit(solution)/shard_map/ppermute | solution.py:523
  12.5 3.3 %tables.1 = (f32[576,128]{1,0:T(8,128)}, f32[576,128]{1,0:T(8,128)}, f32[576,128]{1,0:T(8,128)}, f32[576,128]{1,0:T(8,128)}, f32[1,576]{1,0:T(1,128)}, /*index=5*/bf16[128,128]{1,0:T(8,128)(2,1)}) custom-call(s32[1]{0:T(128)} %bitcast.2.half_ref.part_ref, s32[1]{0:T(128)S(6)} %copy.26.len_ref, f32[1,128]{1,0:T(1,128)} %constant.39.clone.row_freq_ref, ...), custom_call_target="tpu_custom_call" | custom-call | flops 589824 | bytes 294912 | tf_op jit(solution)/shard_map/tables/pallas_call | solution.py:229
  15.8 2.0 %copy-done.2 = bf16[1,3,96,6144]{3,2,1,0:T(8,128)(2,1)S(1)} copy-done((bf16[1,3,96,6144]{3,2,1,0:T(8,128)(2,1)S(1)}, bf16[1,3,96,6144]{3,2,1,0:T(8,128)(2,1)}, u32[]{:S(2)}) %copy-start.2) | copy-done | bytes 3538968
  17.8 1.4 activate.2.refs_0_
  19.2 1.5 dynamic-slice_bitcast_fusion.1
  20.7 24.7 %collective-permute-done.1.refs_0_ = bf16[192,4608]{1,0:T(8,128)(2,1)} collective-permute-done((bf16[192,4608]{1,0:T(8,128)(2,1)}, bf16[192,4608]{1,0:T(8,128)(2,1)}, u32[]{:S(2)}, u32[]{:S(2)}) %collective-permute-start.1) | collective-permute-done | bytes 1769504 | tf_op jit(solution)/shard_map/ppermute | solution.py:481
  45.4 1.4 collective-permute-done.2.refs_2_
  46.7 1.6 collective-permute-start.4
  48.3 0.4 collective-permute-start.5
  48.8 0.5 collective-permute-start.7
  49.3 21.1 %collective-permute-done.far_ref = bf16[3,3,96,1536]{3,2,1,0:T(8,128)(2,1)} collective-permute-done((bf16[3,3,96,1536]{3,2,1,0:T(8,128)(2,1)}, bf16[3,3,96,1536]{3,2,1,0:T(8,128)(2,1)}, u32[]{:S(2)}, u32[]{:S(2)}) %collective-permute-start) | collective-permute-done | bytes 2654240 | tf_op jit(solution)/shard_map/ppermute | solution.py:523
  70.4 1.7 collective-permute-start.10
  72.1 9.3 %attend.2.refs_0_ = bf16[576,1536]{1,0:T(8,128)(2,1)} custom-call(s32[1]{0:T(128)} %bitcast.2.half_ref.part_ref, bf16[3,3,96,3072]{3,2,1,0:T(8,128)(2,1)} %bitcast.33, bf16[3,3,96,1536]{3,2,1,0:T(8,128)(2,1)} %collective-permute-done.far_ref, f32[576,128]{1,0:T(8,128)} %get-tuple-element.63.cq_ref, f32[576,128]{1,0:T(8,128)} %get-tuple-element.64.sq_ref, ...), custom_call_target="tpu_custom_call" | custom-call | flops 1019215872 | bytes 7077888 | tf_op jit(solution)/shard_map/attend/pallas_call | solution.py:286
  81.4 4.8 %collective-permute-done.4.refs_0_ = bf16[192,4608]{1,0:T(8,128)(2,1)} collective-permute-done((bf16[192,4608]{1,0:T(8,128)(2,1)}, bf16[192,4608]{1,0:T(8,128)(2,1)}, u32[]{:S(2)}, u32[]{:S(2)}) %collective-permute-start.4) | collective-permute-done | bytes 1769504 | tf_op jit(solution)/shard_map/ppermute | solution.py:481
  86.2 1.3 collective-permute-done.5.refs_2_
  87.5 1.6 collective-permute-start.8
  89.1 0.4 collective-permute-start.9
  89.5 0.5 collective-permute-start.15
  90.1 9.3 %attend.3.attn_ref = bf16[576,1536]{1,0:T(8,128)(2,1)} custom-call(s32[1]{0:T(128)} %bitcast.2.half_ref.part_ref, bf16[3,3,96,3072]{3,2,1,0:T(8,128)(2,1)} %bitcast.34, bf16[3,3,96,1536]{3,2,1,0:T(8,128)(2,1)} %collective-permute-done.far_ref, f32[576,128]{1,0:T(8,128)} %get-tuple-element.63.cq_ref, ...), custom_call_target="tpu_custom_call", output_to_operand_aliasing={{}: (9, {})} | custom-call | flops 1019215872 | bytes 7077888 | tf_op jit(solution)/shard_map/attend/pallas_call | solution.py:286
  99.3 11.7 %collective-permute-done.10.units_ref = bf16[3,96,3072]{2,1,0:T(8,128)(2,1)} collective-permute-done((bf16[3,96,3072]{2,1,0:T(8,128)(2,1)}, bf16[3,96,3072]{2,1,0:T(8,128)(2,1)}, u32[]{:S(2)}, u32[]{:S(2)}) %collective-permute-start.10) | collective-permute-done | bytes 1769504 | tf_op jit(solution)/shard_map/ppermute | solution.py:537
  111.1 3.0 %activate.3.act_ref = bf16[576,3072]{1,0:T(8,128)(2,1)S(1)} custom-call(s32[1]{0:T(128)} %constant.38.clone.1.part_ref, bf16[3,96,3072]{2,1,0:T(8,128)(2,1)} %collective-permute-done.10.units_ref, bf16[576,3072]{1,0:T(8,128)(2,1)S(1)} %activate.2.refs_0_), custom_call_target="tpu_custom_call", output_to_operand_aliasing={{}: (2, {})} | custom-call | flops 3538944 | bytes 884736 | tf_op jit(solution)/shard_map/activate/pallas_call | solution.py:323
  114.0 3.6 %project.6 = bf16[288,384]{1,0:T(8,128)(2,1)S(1)} custom-call(s32[1]{0:T(128)} %bitcast.1.core_ref, bf16[576,1536]{1,0:T(8,128)(2,1)S(1)} %copy-done, bf16[576,3072]{1,0:T(8,128)(2,1)S(1)} %activate.3.act_ref, bf16[192,4608]{1,0:T(8,128)(2,1)} %pad_maximum_fusion.refs_0_, bf16[192,4608]{1,0:T(8,128)(2,1)} %collective-permute-done.3.refs_1_), custom_call_target="tpu_custom_call" | custom-call | flops 254803968 | bytes 442368 | tf_op jit(solution)/shard_map/project/pallas_call | solution.py:376
  117.6 1.7 collective-permute-start.11
  119.3 6.5 %project.7 = (bf16[288,768]{1,0:T(8,128)(2,1)S(1)}, bf16[288,768]{1,0:T(8,128)(2,1)S(1)}) custom-call(s32[1]{0:T(128)} %bitcast.1.core_ref, bf16[576,1536]{1,0:T(8,128)(2,1)S(1)} %copy-done, bf16[576,3072]{1,0:T(8,128)(2,1)S(1)} %activate.3.act_ref, bf16[192,4608]{1,0:T(8,128)(2,1)} %collective-permute-done.1.refs_0_, ...), custom_call_target="tpu_custom_call" | custom-call | flops 509607936 | bytes 884736 | tf_op jit(solution)/shard_map/project/pallas_call | solution.py:376
  125.9 0.7 copy-done.15
  126.6 0.5 collective-permute-done.9.refs_2_
  127.1 0.5 collective-permute-start.18
  127.6 1.5 collective-permute-start.16
  129.1 1.2 slice.6
  130.3 1.2 slice.7
  131.6 1.6 collective-permute-start.12
  133.2 0.5 collective-permute-start.13
  133.7 6.5 %project.8 = (bf16[288,768]{1,0:T(8,128)(2,1)S(1)}, bf16[288,768]{1,0:T(8,128)(2,1)S(1)}) custom-call(s32[1]{0:T(128)} %bitcast.1.core_ref, bf16[576,1536]{1,0:T(8,128)(2,1)S(1)} %copy-done, bf16[576,3072]{1,0:T(8,128)(2,1)S(1)} %activate.3.act_ref, bf16[192,4608]{1,0:T(8,128)(2,1)} %collective-permute-done.4.refs_0_, ...), custom_call_target="tpu_custom_call" | custom-call | flops 509607936 | bytes 884736 | tf_op jit(solution)/shard_map/project/pallas_call | solution.py:376
  140.2 0.7 copy-done.8
  141.0 0.5 collective-permute-start.19
  141.5 6.8 %project.9 = (bf16[288,768]{1,0:T(8,128)(2,1)S(1)}, bf16[288,768]{1,0:T(8,128)(2,1)}) custom-call(s32[1]{0:T(128)} %bitcast.1.core_ref, bf16[576,1536]{1,0:T(8,128)(2,1)S(1)} %copy-done, bf16[576,3072]{1,0:T(8,128)(2,1)S(1)} %activate.3.act_ref, bf16[192,4608]{1,0:T(8,128)(2,1)} %collective-permute-done.8.refs_0_, ...), custom_call_target="tpu_custom_call" | custom-call | flops 509607936 | bytes 884736 | tf_op jit(solution)/shard_map/project/pallas_call | solution.py:376
  148.3 3.9 %collective-permute-done.19.refs_5_ = bf16[288,768]{1,0:T(8,128)(2,1)S(1)} collective-permute-done((bf16[288,768]{1,0:T(8,128)(2,1)S(1)}, bf16[288,768]{1,0:T(8,128)(2,1)S(1)}, u32[]{:S(2)}, u32[]{:S(2)}) %collective-permute-start.19) | collective-permute-done | bytes 442400 | tf_op jit(solution)/shard_map/ppermute | solution.py:552
  152.2 0.7 collective-permute-done.12.refs_0_
  152.9 1.3 collective-permute-done.13.refs_2_
  154.2 0.5 collective-permute-start.21
  154.7 0.5 collective-permute-start.22
  155.2 1.4 collective-permute-done.20.refs_1_
  156.7 1.3 collective-permute-done.21.refs_3_
  157.9 4.4 %project.10 = (bf16[288,384]{1,0:T(8,128)(2,1)S(1)}, bf16[288,384]{1,0:T(8,128)(2,1)}) custom-call(s32[1]{0:T(128)} %bitcast.1.core_ref, bf16[576,1536]{1,0:T(8,128)(2,1)S(1)} %copy-done, bf16[576,3072]{1,0:T(8,128)(2,1)S(1)} %activate.3.act_ref, bf16[96,4608]{1,0:T(8,128)(2,1)S(1)} %collective-permute-done.12.refs_0_, ...), custom_call_target="tpu_custom_call" | custom-call | flops 254803968 | bytes 442368 | tf_op jit(solution)/shard_map/project/pallas_call | solution.py:376
  162.3 0.7 copy-done.17
  163.0 0.5 collective-permute-start.23
  163.5 0.7 copy.23.refs_16_
  164.9 0.0 copy-start.1
  164.9 1.5 copy-done.1
  166.4 0.0 copy-start.14
  166.4 0.0 copy-start.19
  166.4 0.0 copy-start.20
  166.4 0.0 copy-start.21
  166.4 0.0 copy-start.22
  166.5 0.0 copy-start.23
  166.5 0.0 copy-start.24
  166.5 0.0 copy-start.25
  166.5 3.7 %project.11.refs_0_ = bf16[288,384]{1,0:T(8,128)(2,1)S(1)} custom-call(s32[1]{0:T(128)} %bitcast.1.core_ref, bf16[576,1536]{1,0:T(8,128)(2,1)S(1)} %copy-done.1, bf16[576,3072]{1,0:T(8,128)(2,1)S(1)} %activate.3.act_ref, bf16[192,4608]{1,0:T(8,128)(2,1)} %pad_maximum_fusion.refs_0_, bf16[192,4608]{1,0:T(8,128)(2,1)} %collective-permute-done.3.refs_1_), custom_call_target="tpu_custom_call" | custom-call | flops 254803968 | bytes 442368 | tf_op jit(solution)/shard_map/project/pallas_call | solution.py:376
  170.2 1.6 collective-permute-done.23.refs_9_
  172.0 5.2 %finish.1 = (bf16[3,96,3072]{2,1,0:T(8,128)(2,1)}, f32[2,64,96]{2,1,0:T(8,128)}) custom-call(s32[1]{0:T(128)} %bitcast.tile_ref, s32[16]{0:T(128)S(1)} %copy-done.25, f32[1]{0:T(128)S(6)} %copy.27.step_ref, bf16[288,384]{1,0:T(8,128)(2,1)S(1)} %project.11.refs_0_, bf16[288,384]{1,0:T(8,128)(2,1)S(1)} %copy-done.16, bf16[288,768]{1,0:T(8,128)(2,1)S(1)} %copy-done.5, ...), custom_call_target="tpu_custom_call" | custom-call | flops 141557760 | bytes 8847360 | tf_op jit(solution)/shard_map/finish/pallas_call | solution.py:443
  (56 shorter events, 0.1 us)
Async XLA Ops:
  3.4 41.9 %collective-permute-start.1 = (bf16[192,4608]{1,0:T(8,128)(2,1)}, bf16[192,4608]{1,0:T(8,128)(2,1)}, u32[]{:S(2)}, u32[]{:S(2)}) collective-permute-start(bf16[192,4608]{1,0:T(8,128)(2,1)} %pad_maximum_fusion.refs_0_), channel_id=1, source_target_pairs={{0,4},{2,6},{4,12},{6,14},{12,20},{14,22},{20,28},{22,30},{28,24},... | collective-permute-start | bytes 5308424 | tf_op jit(solution)/shard_map/ppermute | solution.py:481
  6.4 40.4 %collective-permute-start.2 = (bf16[192,4608]{1,0:T(8,128)(2,1)}, bf16[192,4608]{1,0:T(8,128)(2,1)}, u32[]{:S(2)}, u32[]{:S(2)}) collective-permute-start(bf16[192,4608]{1,0:T(8,128)(2,1)} %pad_maximum_fusion.refs_0_), channel_id=1, source_target_pairs={{0,8},{2,10},{4,0},{6,2},{12,4},{14,6},{20,12},{22,14},{28,20},{30... | collective-permute-start | bytes 5308424 | tf_op jit(solution)/shard_map/ppermute | solution.py:481
  6.4 40.3 %collective-permute-start.3 = (bf16[192,4608]{1,0:T(8,128)(2,1)}, bf16[192,4608]{1,0:T(8,128)(2,1)}, u32[]{:S(2)}, u32[]{:S(2)}) collective-permute-start(bf16[192,4608]{1,0:T(8,128)(2,1)} %pad_maximum_fusion.refs_0_), channel_id=1, source_target_pairs={{0,2},{2,0},{4,6},{6,4},{8,10},{10,8},{12,14},{14,12},{16,18},{18,... | collective-permute-start | bytes 5308424 | tf_op jit(solution)/shard_map/ppermute | solution.py:485
  9.8 60.5 %collective-permute-start = (bf16[3,3,96,1536]{3,2,1,0:T(8,128)(2,1)}, bf16[3,3,96,1536]{3,2,1,0:T(8,128)(2,1)}, u32[]{:S(2)}, u32[]{:S(2)}) collective-permute-start(bf16[3,3,96,1536]{3,2,1,0:T(8,128)(2,1)} %dynamic-slice_bitcast_fusion), channel_id=1, source_target_pairs={{0,1},{1,0},{2,3},{3,2},{4,5},{5,4},{6,7},{7,6},{8,9},{9,8},{10,11... | collective-permute-start | bytes 7962632 | tf_op jit(solution)/shard_map/ppermute | solution.py:523
  15.8 2.0 %copy-start.2 = (bf16[1,3,96,6144]{3,2,1,0:T(8,128)(2,1)S(1)}, bf16[1,3,96,6144]{3,2,1,0:T(8,128)(2,1)}, u32[]{:S(2)}) copy-start(bf16[1,3,96,6144]{3,2,1,0:T(8,128)(2,1)} %param.20) | copy-start | bytes 10616836
  46.7 39.5 %collective-permute-start.4 = (bf16[192,4608]{1,0:T(8,128)(2,1)}, bf16[192,4608]{1,0:T(8,128)(2,1)}, u32[]{:S(2)}, u32[]{:S(2)}) collective-permute-start(bf16[192,4608]{1,0:T(8,128)(2,1)} %collective-permute-done.1.refs_0_), channel_id=1, source_target_pairs={{0,4},{2,6},{4,12},{6,14},{12,20},{14,22},{20,28},{22,30},{28,24},... | collective-permute-start | bytes 5308424 | tf_op jit(solution)/shard_map/ppermute | solution.py:481
  48.3 39.2 %collective-permute-start.5 = (bf16[192,4608]{1,0:T(8,128)(2,1)}, bf16[192,4608]{1,0:T(8,128)(2,1)}, u32[]{:S(2)}, u32[]{:S(2)}) collective-permute-start(bf16[192,4608]{1,0:T(8,128)(2,1)} %collective-permute-done.2.refs_2_), channel_id=1, source_target_pairs={{0,8},{2,10},{4,0},{6,2},{12,4},{14,6},{20,12},{22,14},{28,20},{30... | collective-permute-start | bytes 5308424 | tf_op jit(solution)/shard_map/ppermute | solution.py:481
  48.8 38.7 %collective-permute-start.6 = (bf16[192,4608]{1,0:T(8,128)(2,1)}, bf16[192,4608]{1,0:T(8,128)(2,1)}, u32[]{:S(2)}, u32[]{:S(2)}) collective-permute-start(bf16[192,4608]{1,0:T(8,128)(2,1)} %collective-permute-done.1.refs_0_), channel_id=1, source_target_pairs={{0,2},{2,0},{4,6},{6,4},{8,10},{10,8},{12,14},{14,12},{16,18},{18,... | collective-permute-start | bytes 5308424 | tf_op jit(solution)/shard_map/ppermute | solution.py:485
  48.8 38.7 %collective-permute-start.7 = (bf16[192,4608]{1,0:T(8,128)(2,1)}, bf16[192,4608]{1,0:T(8,128)(2,1)}, u32[]{:S(2)}, u32[]{:S(2)}) collective-permute-start(bf16[192,4608]{1,0:T(8,128)(2,1)} %collective-permute-done.2.refs_2_), channel_id=1, source_target_pairs={{0,2},{2,0},{4,6},{6,4},{8,10},{10,8},{12,14},{14,12},{16,18},{18,... | collective-permute-start | bytes 5308424 | tf_op jit(solution)/shard_map/ppermute | solution.py:485
  70.4 40.7 %collective-permute-start.10 = (bf16[3,96,3072]{2,1,0:T(8,128)(2,1)}, bf16[3,96,3072]{2,1,0:T(8,128)(2,1)}, u32[]{:S(2)}, u32[]{:S(2)}) collective-permute-start(bf16[3,96,3072]{2,1,0:T(8,128)(2,1)} %dynamic-slice_bitcast_fusion.1), channel_id=1, source_target_pairs={{0,1},{1,0},{2,3},{3,2},{4,5},{5,4},{6,7},{7,6},{8,9},{9,8},{10,11... | collective-permute-start | bytes 5308424 | tf_op jit(solution)/shard_map/ppermute | solution.py:537
  87.5 39.1 %collective-permute-start.8 = (bf16[192,4608]{1,0:T(8,128)(2,1)}, bf16[192,4608]{1,0:T(8,128)(2,1)}, u32[]{:S(2)}, u32[]{:S(2)}) collective-permute-start(bf16[192,4608]{1,0:T(8,128)(2,1)} %collective-permute-done.4.refs_0_), channel_id=1, source_target_pairs={{0,4},{2,6},{4,12},{6,14},{12,20},{14,22},{20,28},{22,30},{28,24},... | collective-permute-start | bytes 5308424 | tf_op jit(solution)/shard_map/ppermute | solution.py:481
  89.1 38.0 %collective-permute-start.9 = (bf16[192,4608]{1,0:T(8,128)(2,1)}, bf16[192,4608]{1,0:T(8,128)(2,1)}, u32[]{:S(2)}, u32[]{:S(2)}) collective-permute-start(bf16[192,4608]{1,0:T(8,128)(2,1)} %collective-permute-done.5.refs_2_), channel_id=1, source_target_pairs={{0,8},{2,10},{4,0},{6,2},{12,4},{14,6},{20,12},{22,14},{28,20},{30... | collective-permute-start | bytes 5308424 | tf_op jit(solution)/shard_map/ppermute | solution.py:481
  89.5 42.0 %collective-permute-start.14 = (bf16[192,4608]{1,0:T(8,128)(2,1)}, bf16[192,4608]{1,0:T(8,128)(2,1)}, u32[]{:S(2)}, u32[]{:S(2)}) collective-permute-start(bf16[192,4608]{1,0:T(8,128)(2,1)} %collective-permute-done.4.refs_0_), channel_id=1, source_target_pairs={{0,2},{2,0},{4,6},{6,4},{8,10},{10,8},{12,14},{14,12},{16,18},{18,... | collective-permute-start | bytes 5308424 | tf_op jit(solution)/shard_map/ppermute | solution.py:485
  89.5 43.7 %collective-permute-start.15 = (bf16[192,4608]{1,0:T(8,128)(2,1)}, bf16[192,4608]{1,0:T(8,128)(2,1)}, u32[]{:S(2)}, u32[]{:S(2)}) collective-permute-start(bf16[192,4608]{1,0:T(8,128)(2,1)} %collective-permute-done.5.refs_2_), channel_id=1, source_target_pairs={{0,2},{2,0},{4,6},{6,4},{8,10},{10,8},{12,14},{14,12},{16,18},{18,... | collective-permute-start | bytes 5308424 | tf_op jit(solution)/shard_map/ppermute | solution.py:485
  99.3 14.7 %copy-start = (bf16[576,1536]{1,0:T(8,128)(2,1)S(1)}, bf16[576,1536]{1,0:T(8,128)(2,1)}, u32[]{:S(2)}) copy-start(bf16[576,1536]{1,0:T(8,128)(2,1)} %attend.3.attn_ref) | copy-start | bytes 5308420
  117.6 8.2 %collective-permute-start.11 = (bf16[288,384]{1,0:T(8,128)(2,1)S(1)}, bf16[288,384]{1,0:T(8,128)(2,1)S(1)}, u32[]{:S(2)}, u32[]{:S(2)}) collective-permute-start(bf16[288,384]{1,0:T(8,128)(2,1)S(1)} %project.6), channel_id=1, source_target_pairs={{0,1},{1,0},{2,3},{3,2},{4,5},{5,4},{6,7},{7,6},{8,9},{9,8},{10,11... | collective-permute-start | bytes 663560 | tf_op jit(solution)/shard_map/ppermute | solution.py:556
  125.8 5.7 %copy-start.4 = (bf16[288,768]{1,0:T(8,128)(2,1)}, bf16[288,768]{1,0:T(8,128)(2,1)S(1)}, u32[]{:S(2)}) copy-start(bf16[288,768]{1,0:T(8,128)(2,1)S(1)} %get-tuple-element.100.refs_2_) | copy-start | bytes 1327108
  125.9 0.7 copy-start.15
  127.1 14.4 %collective-permute-start.17 = (bf16[192,4608]{1,0:T(8,128)(2,1)}, bf16[192,4608]{1,0:T(8,128)(2,1)S(1)}, u32[]{:S(2)}, u32[]{:S(2)}) collective-permute-start(bf16[192,4608]{1,0:T(8,128)(2,1)} %collective-permute-done.8.refs_0_), channel_id=1, source_target_pairs={{0,2},{2,0},{4,6},{6,4},{8,10},{10,8},{12,14},{14,12},{16,18},{18,... | collective-permute-start | bytes 5308424 | tf_op jit(solution)/shard_map/ppermute | solution.py:485
  127.1 14.4 %collective-permute-start.18 = (bf16[192,4608]{1,0:T(8,128)(2,1)}, bf16[192,4608]{1,0:T(8,128)(2,1)S(1)}, u32[]{:S(2)}, u32[]{:S(2)}) collective-permute-start(bf16[192,4608]{1,0:T(8,128)(2,1)} %collective-permute-done.9.refs_2_), channel_id=1, source_target_pairs={{0,2},{2,0},{4,6},{6,4},{8,10},{10,8},{12,14},{14,12},{16,18},{18,... | collective-permute-start | bytes 5308424 | tf_op jit(solution)/shard_map/ppermute | solution.py:485
  127.6 13.4 %collective-permute-start.16 = (bf16[288,768]{1,0:T(8,128)(2,1)S(1)}, bf16[288,768]{1,0:T(8,128)(2,1)S(1)}, u32[]{:S(2)}, u32[]{:S(2)}) collective-permute-start(bf16[288,768]{1,0:T(8,128)(2,1)S(1)} %get-tuple-element.85), channel_id=1, source_target_pairs={{0,1},{1,0},{2,3},{3,2},{4,5},{5,4},{6,7},{7,6},{8,9},{9,8},{10,11... | collective-permute-start | bytes 1327112 | tf_op jit(solution)/shard_map/ppermute | solution.py:552
  131.6 21.3 %collective-permute-start.12 = (bf16[96,4608]{1,0:T(8,128)(2,1)S(1)}, bf16[96,4608]{1,0:T(8,128)(2,1)S(1)}, u32[]{:S(2)}, u32[]{:S(2)}) collective-permute-start(bf16[96,4608]{1,0:T(8,128)(2,1)S(1)} %slice.6), channel_id=1, source_target_pairs={{0,4},{2,6},{4,12},{6,14},{12,20},{14,22},{20,28},{22,30},{28,24},... | collective-permute-start | bytes 2654216 | tf_op jit(solution)/shard_map/ppermute | solution.py:481
  133.2 21.0 %collective-permute-start.13 = (bf16[96,4608]{1,0:T(8,128)(2,1)S(1)}, bf16[96,4608]{1,0:T(8,128)(2,1)S(1)}, u32[]{:S(2)}, u32[]{:S(2)}) collective-permute-start(bf16[96,4608]{1,0:T(8,128)(2,1)S(1)} %slice.7), channel_id=1, source_target_pairs={{0,8},{2,10},{4,0},{6,2},{12,4},{14,6},{20,12},{22,14},{28,20},{30... | collective-permute-start | bytes 2654216 | tf_op jit(solution)/shard_map/ppermute | solution.py:481
  140.2 0.8 copy-start.8
  141.0 7.3 %copy-start.6 = (bf16[288,768]{1,0:T(8,128)(2,1)}, bf16[288,768]{1,0:T(8,128)(2,1)S(1)}, u32[]{:S(2)}) copy-start(bf16[288,768]{1,0:T(8,128)(2,1)S(1)} %collective-permute-done.16.refs_3_) | copy-start | bytes 1327108
  141.0 11.2 %collective-permute-start.19 = (bf16[288,768]{1,0:T(8,128)(2,1)S(1)}, bf16[288,768]{1,0:T(8,128)(2,1)S(1)}, u32[]{:S(2)}, u32[]{:S(2)}) collective-permute-start(bf16[288,768]{1,0:T(8,128)(2,1)S(1)} %get-tuple-element.89), channel_id=1, source_target_pairs={{0,1},{1,0},{2,3},{3,2},{4,5},{5,4},{6,7},{7,6},{8,9},{9,8},{10,11... | collective-permute-start | bytes 1327112 | tf_op jit(solution)/shard_map/ppermute | solution.py:552
  148.3 14.0 %copy-start.12 = (bf16[288,768]{1,0:T(8,128)(2,1)}, bf16[288,768]{1,0:T(8,128)(2,1)S(1)}, u32[]{:S(2)}) copy-start(bf16[288,768]{1,0:T(8,128)(2,1)S(1)} %get-tuple-element.104.refs_6_) | copy-start | bytes 1327108
  152.2 10.1 %copy-start.10 = (bf16[288,768]{1,0:T(8,128)(2,1)}, bf16[288,768]{1,0:T(8,128)(2,1)S(1)}, u32[]{:S(2)}) copy-start(bf16[288,768]{1,0:T(8,128)(2,1)S(1)} %collective-permute-done.19.refs_5_) | copy-start | bytes 1327108
  154.2 9.3 %copy-start.26 = (f32[64]{0:T(128)S(1)}, f32[64]{0:T(128)}, u32[]{:S(2)}) copy-start(f32[64]{0:T(128)} %param.32) | copy-start | bytes 772
  154.2 2.4 %collective-permute-start.20 = (bf16[96,4608]{1,0:T(8,128)(2,1)S(1)}, bf16[96,4608]{1,0:T(8,128)(2,1)S(1)}, u32[]{:S(2)}, u32[]{:S(2)}) collective-permute-start(bf16[96,4608]{1,0:T(8,128)(2,1)S(1)} %collective-permute-done.12.refs_0_), channel_id=1, source_target_pairs={{0,2},{2,0},{4,6},{6,4},{8,10},{10,8},{12,14},{14,12},{16,18},{18,... | collective-permute-start | bytes 2654216 | tf_op jit(solution)/shard_map/ppermute | solution.py:485
  154.2 3.7 %collective-permute-start.21 = (bf16[96,4608]{1,0:T(8,128)(2,1)S(1)}, bf16[96,4608]{1,0:T(8,128)(2,1)S(1)}, u32[]{:S(2)}, u32[]{:S(2)}) collective-permute-start(bf16[96,4608]{1,0:T(8,128)(2,1)S(1)} %collective-permute-done.13.refs_2_), channel_id=1, source_target_pairs={{0,2},{2,0},{4,6},{6,4},{8,10},{10,8},{12,14},{14,12},{16,18},{18,... | collective-permute-start | bytes 2654216 | tf_op jit(solution)/shard_map/ppermute | solution.py:485
  154.7 15.5 %collective-permute-start.22 = (bf16[288,768]{1,0:T(8,128)(2,1)}, bf16[288,768]{1,0:T(8,128)(2,1)}, u32[]{:S(2)}, u32[]{:S(2)}) collective-permute-start(bf16[288,768]{1,0:T(8,128)(2,1)} %get-tuple-element.92), channel_id=1, source_target_pairs={{0,1},{1,0},{2,3},{3,2},{4,5},{5,4},{6,7},{7,6},{8,9},{9,8},{10,11... | collective-permute-start | bytes 1327112 | tf_op jit(solution)/shard_map/ppermute | solution.py:552
  162.3 0.7 copy-start.17
  163.0 8.9 %collective-permute-start.23 = (bf16[288,384]{1,0:T(8,128)(2,1)}, bf16[288,384]{1,0:T(8,128)(2,1)}, u32[]{:S(2)}, u32[]{:S(2)}) collective-permute-start(bf16[288,384]{1,0:T(8,128)(2,1)} %get-tuple-element.97), channel_id=1, source_target_pairs={{0,1},{1,0},{2,3},{3,2},{4,5},{5,4},{6,7},{7,6},{8,9},{9,8},{10,11... | collective-permute-start | bytes 663560 | tf_op jit(solution)/shard_map/ppermute | solution.py:552
  164.9 1.5 copy-start.1
  166.3 5.5 %copy-start.3 = (bf16[1,3,96,3072]{3,2,1,0:T(8,128)(2,1)S(1)}, bf16[1,3,96,3072]{3,2,1,0:T(8,128)(2,1)}, u32[]{:S(2)}) copy-start(bf16[1,3,96,3072]{3,2,1,0:T(8,128)(2,1)} %param.21) | copy-start | bytes 5308420
  166.3 5.5 %copy-start.5 = (bf16[288,768]{1,0:T(8,128)(2,1)S(1)}, bf16[288,768]{1,0:T(8,128)(2,1)}, u32[]{:S(2)}) copy-start(bf16[288,768]{1,0:T(8,128)(2,1)} %copy-done.4) | copy-start | bytes 1327108
  166.3 5.5 %copy-start.7 = (bf16[288,768]{1,0:T(8,128)(2,1)S(1)}, bf16[288,768]{1,0:T(8,128)(2,1)}, u32[]{:S(2)}) copy-start(bf16[288,768]{1,0:T(8,128)(2,1)} %copy-done.6) | copy-start | bytes 1327108
  166.4 5.5 %copy-start.9 = (bf16[288,768]{1,0:T(8,128)(2,1)S(1)}, bf16[288,768]{1,0:T(8,128)(2,1)}, u32[]{:S(2)}) copy-start(bf16[288,768]{1,0:T(8,128)(2,1)} %copy-done.8) | copy-start | bytes 1327108
  166.4 5.5 %copy-start.11 = (bf16[288,768]{1,0:T(8,128)(2,1)S(1)}, bf16[288,768]{1,0:T(8,128)(2,1)}, u32[]{:S(2)}) copy-start(bf16[288,768]{1,0:T(8,128)(2,1)} %copy-done.10) | copy-start | bytes 1327108
  166.4 5.5 %copy-start.13 = (bf16[288,768]{1,0:T(8,128)(2,1)S(1)}, bf16[288,768]{1,0:T(8,128)(2,1)}, u32[]{:S(2)}) copy-start(bf16[288,768]{1,0:T(8,128)(2,1)} %copy-done.12) | copy-start | bytes 1327108
  166.4 5.5 %copy-start.14 = (bf16[3072,64]{0,1:T(8,128)(2,1)S(1)}, bf16[3072,64]{0,1:T(8,128)(2,1)}, u32[]{:S(2)}) copy-start(bf16[3072,64]{0,1:T(8,128)(2,1)} %param.31) | copy-start | bytes 1179652
  166.4 5.5 %copy-start.16 = (bf16[288,384]{1,0:T(8,128)(2,1)S(1)}, bf16[288,384]{1,0:T(8,128)(2,1)}, u32[]{:S(2)}) copy-start(bf16[288,384]{1,0:T(8,128)(2,1)} %copy-done.15) | copy-start | bytes 663556
  166.4 5.5 %copy-start.18 = (bf16[288,384]{1,0:T(8,128)(2,1)S(1)}, bf16[288,384]{1,0:T(8,128)(2,1)}, u32[]{:S(2)}) copy-start(bf16[288,384]{1,0:T(8,128)(2,1)} %copy-done.17) | copy-start | bytes 663556
  166.4 5.5 %copy-start.19 = (f32[64,1]{1,0:T(8,128)S(1)}, f32[64,1]{1,0:T(8,128)}, u32[]{:S(2)}) copy-start(f32[64,1]{1,0:T(8,128)} %copy.23.refs_16_) | copy-start | bytes 772
  166.4 5.5 %copy-start.20 = (f32[1,2,96,64]{2,3,1,0:T(8,128)S(1)}, f32[1,2,96,64]{2,3,1,0:T(8,128)}, u32[]{:S(2)}) copy-start(f32[1,2,96,64]{2,3,1,0:T(8,128)} %param.33) | copy-start | bytes 147460
  166.4 5.5 %copy-start.21 = (f32[3072]{0:T(1024)S(1)}, f32[3072]{0:T(1024)}, u32[]{:S(2)}) copy-start(f32[3072]{0:T(1024)} %param.27) | copy-start | bytes 36868
  166.4 5.5 %copy-start.22 = (f32[1,3072]{1,0:T(1,128)S(1)}, f32[1,3072]{1,0:T(1,128)}, u32[]{:S(2)}) copy-start(f32[1,3072]{1,0:T(1,128)} %refs_12_.1) | copy-start | bytes 36868
  166.5 5.5 %copy-start.23 = (f32[1,3072]{1,0:T(1,128)S(1)}, f32[1,3072]{1,0:T(1,128)}, u32[]{:S(2)}) copy-start(f32[1,3072]{1,0:T(1,128)} %refs_13_.1) | copy-start | bytes 36868
  166.5 5.5 %copy-start.24 = (f32[1,3072]{1,0:T(1,128)S(1)}, f32[1,3072]{1,0:T(1,128)}, u32[]{:S(2)}) copy-start(f32[1,3072]{1,0:T(1,128)} %refs_14_.1) | copy-start | bytes 36868
  166.5 5.5 %copy-start.25 = (s32[16]{0:T(128)S(1)}, s32[16]{0:T(128)}, u32[]{:S(2)}) copy-start(s32[16]{0:T(128)} %constant.41.clone.place_ref) | copy-start | bytes 196

commit v4 on v3

--- a/solution.py
+++ b/solution.py
@@ -397,6 +397,7 @@
         stream_ref, bias_ref, gate_ref, scale_ref, shift_ref, w_ref, b_ref, latent_ref, hidden_ref, next_ref, proj_ref,
     ) = refs[2 * chunks :]
     slots, width = proj_ref.shape
+    rows = pl.ds(pl.multiple_of(pl.program_id(0) * slots, slots), slots)
     places = len(PATH)
     chip = width // places
     mine = place_ref[places + tile_ref[0] // 2]
@@ -407,8 +408,8 @@
             source = place_ref[(mine - behind.pop(0) + places) % places]
             target = pl.ds(pl.multiple_of(chip * source, 128), chip)
             part = slice(first, first + chip)
-            proj = own_ref[:, part].astype(jnp.float32) + far_ref[:, part].astype(jnp.float32)
-            updated = stream_ref[0, :, target].astype(jnp.float32) + gate_ref[:, target] * (proj + bias_ref[:, target])
+            proj = own_ref[rows, part].astype(jnp.float32) + far_ref[rows, part].astype(jnp.float32)
+            updated = stream_ref[rows, target].astype(jnp.float32) + gate_ref[:, target] * (proj + bias_ref[:, target])
             hidden_ref[0, :, target] = updated.astype(jnp.bfloat16)
             proj_ref[:, target] = updated
             total += updated
@@ -445,9 +446,8 @@
         grid_spec=pltpu.PrefetchScalarGridSpec(
             num_scalar_prefetch=3,
             grid=(blocks,),
-            in_specs=[pl.BlockSpec((slots, array.shape[1]), lambda b, *_: (b, 0)) for array in flat]
+            in_specs=[pl.BlockSpec(memory_space=pltpu.VMEM)] * (len(flat) + 1)
             + [
-                tokens,
                 whole(bias),
                 whole(gate),
                 whole(scale),
@@ -468,7 +468,7 @@
             flops=blocks * slots * width * 160, bytes_accessed=blocks * slots * width * 10, transcendentals=0
         ),
         name="finish",
-    )(tile, np.array(PATH + PLACE, np.int32), step, *flat, stream, bias, gate, scale, shift, w_final, b_final, latent)
+    )(tile, np.array(PATH + PLACE, np.int32), step, *flat, stream.reshape(blocks * slots, width), bias, gate, scale, shift, w_final, b_final, latent)
 
 
 PATH = (0, 1, 3, 5, 7, 6, 4, 2)

time: 178 us -> 178 us (level)
  no operation moved by 1% of the time
where the time goes in v4:
time: 178 us; the launch traced here: 177 us
  waiting for transfers between devices  75.7 us (43%)
  Pallas kernels  63.1 us (35%)
  starting transfers between devices  19.6 us (11%)
  local copies, waits for them, and re-layouts  13.8 us (8%)
  other arithmetic  2.78 us (2%)
  between operations  2.35 us (1%)
    ppermute x8, waiting for transfers between devices, hop(): return lax.ppermute(array, 'tile', pairs)  34.7 us
    pallas_call x6, Pallas kernels, project(): pl.pallas_call(functools.partial(project_kernel, layout, sides), in_specs...  31.5 us
    ppermute x1, waiting for transfers between devices, paired(): far_attn = trade(sent_attn)  21.1 us
    pallas_call x2, Pallas kernels, attend(): pl.pallas_call(attend_kernel, grid_spec=pltpu.PrefetchScalarGridSpec(num_...  18.5 us
    ppermute x1, waiting for transfers between devices, paired(): far_units = trade(sent_units)  11.7 us
    ppermute x8, starting transfers between devices, hop(): return lax.ppermute(array, 'tile', pairs)  9.16 us
    unnamed x54, local copies, waits for them, and re-layouts  5.73 us
    ppermute x4, waiting for transfers between devices, send(): chunks.append((own, trade(sent)))  5.56 us
  transfers between devices with their start and end apart: 24, of which 13 were waited for; matrix products, arithmetic and copies ran while one was open for 5% of the time, Pallas kernels for 33%

profile of v4, /device:TPU:0, one launch (start us, length us, event | category | flops | bytes accessed | tf_op | source)
XLA Modules:
  0.0 177.4 jit_solution(12066577153318189527)
XLA Ops:
  0.6 2.8 %pad_maximum_fusion.refs_0_ = bf16[192,4608]{1,0:T(8,128)(2,1)} fusion(bf16[192,3072]{1,0:T(8,128)(2,1)} %bitcast.35, bf16[192,1536]{1,0:T(8,128)(2,1)} %bitcast.36), kind=kLoop, calls=%fused_computation.1 | loop fusion | flops 3538944 | bytes 3538944 | tf_op jit(solution)/shard_map/concatenate | solution.py:520
  3.4 2.9 %collective-permute-start.1 = (bf16[192,4608]{1,0:T(8,128)(2,1)}, bf16[192,4608]{1,0:T(8,128)(2,1)}, u32[]{:S(2)}, u32[]{:S(2)}) collective-permute-start(bf16[192,4608]{1,0:T(8,128)(2,1)} %pad_maximum_fusion.refs_0_), channel_id=1, source_target_pairs={{0,4},{2,6},{4,12},{6,14},{12,20},{14,22},{20,28},{22,30},{28,24},... | collective-permute-start | bytes 5308424 | tf_op jit(solution)/shard_map/ppermute | solution.py:481
  6.4 0.1 collective-permute-start.2
  6.4 3.4 %dynamic-slice_bitcast_fusion = bf16[3,3,96,1536]{3,2,1,0:T(8,128)(2,1)} fusion(bf16[1,3,96,3,3072]{4,2,3,1,0:T(8,128)(2,1)} %param.19, s32[]{:T(128)S(6)} %select_n.14), kind=kLoop, calls=%fused_computation | loop fusion | bytes 5308420 | tf_op jit(solution)/shard_map/dynamic_slice | solution.py:519
  9.8 2.0 %collective-permute-start = (bf16[3,3,96,1536]{3,2,1,0:T(8,128)(2,1)}, bf16[3,3,96,1536]{3,2,1,0:T(8,128)(2,1)}, u32[]{:S(2)}, u32[]{:S(2)}) collective-permute-start(bf16[3,3,96,1536]{3,2,1,0:T(8,128)(2,1)} %dynamic-slice_bitcast_fusion), channel_id=1, source_target_pairs={{0,1},{1,0},{2,3},{3,2},{4,5},{5,4},{6,7},{7,6},{8,9},{9,8},{10,11... | collective-permute-start | bytes 7962632 | tf_op jit(solution)/shard_map/ppermute | solution.py:523
  12.5 3.3 %tables.1 = (f32[576,128]{1,0:T(8,128)}, f32[576,128]{1,0:T(8,128)}, f32[576,128]{1,0:T(8,128)}, f32[576,128]{1,0:T(8,128)}, f32[1,576]{1,0:T(1,128)}, /*index=5*/bf16[128,128]{1,0:T(8,128)(2,1)}) custom-call(s32[1]{0:T(128)} %bitcast.2.half_ref.part_ref, s32[1]{0:T(128)S(6)} %copy.26.len_ref, f32[1,128]{1,0:T(1,128)} %constant.39.clone.row_freq_ref, ...), custom_call_target="tpu_custom_call" | custom-call | flops 589824 | bytes 294912 | tf_op jit(solution)/shard_map/tables/pallas_call | solution.py:229
  15.8 2.0 %copy-done.2 = bf16[1,3,96,6144]{3,2,1,0:T(8,128)(2,1)S(1)} copy-done((bf16[1,3,96,6144]{3,2,1,0:T(8,128)(2,1)S(1)}, bf16[1,3,96,6144]{3,2,1,0:T(8,128)(2,1)}, u32[]{:S(2)}) %copy-start.2) | copy-done | bytes 3538968
  17.8 1.4 activate.2.refs_0_
  19.2 1.5 dynamic-slice_bitcast_fusion.1
  20.7 24.7 %collective-permute-done.1.refs_0_ = bf16[192,4608]{1,0:T(8,128)(2,1)} collective-permute-done((bf16[192,4608]{1,0:T(8,128)(2,1)}, bf16[192,4608]{1,0:T(8,128)(2,1)}, u32[]{:S(2)}, u32[]{:S(2)}) %collective-permute-start.1) | collective-permute-done | bytes 1769504 | tf_op jit(solution)/shard_map/ppermute | solution.py:481
  45.4 1.4 collective-permute-done.2.refs_2_
  46.7 1.6 collective-permute-start.4
  48.3 0.4 collective-permute-start.5
  48.8 0.5 collective-permute-start.7
  49.3 21.1 %collective-permute-done.far_ref = bf16[3,3,96,1536]{3,2,1,0:T(8,128)(2,1)} collective-permute-done((bf16[3,3,96,1536]{3,2,1,0:T(8,128)(2,1)}, bf16[3,3,96,1536]{3,2,1,0:T(8,128)(2,1)}, u32[]{:S(2)}, u32[]{:S(2)}) %collective-permute-start) | collective-permute-done | bytes 2654240 | tf_op jit(solution)/shard_map/ppermute | solution.py:523
  70.4 1.7 collective-permute-start.10
  72.1 9.3 %attend.2.refs_0_ = bf16[576,1536]{1,0:T(8,128)(2,1)} custom-call(s32[1]{0:T(128)} %bitcast.2.half_ref.part_ref, bf16[3,3,96,3072]{3,2,1,0:T(8,128)(2,1)} %bitcast.33, bf16[3,3,96,1536]{3,2,1,0:T(8,128)(2,1)} %collective-permute-done.far_ref, f32[576,128]{1,0:T(8,128)} %get-tuple-element.63.cq_ref, f32[576,128]{1,0:T(8,128)} %get-tuple-element.64.sq_ref, ...), custom_call_target="tpu_custom_call" | custom-call | flops 1019215872 | bytes 7077888 | tf_op jit(solution)/shard_map/attend/pallas_call | solution.py:286
  81.4 4.8 %collective-permute-done.4.refs_0_ = bf16[192,4608]{1,0:T(8,128)(2,1)} collective-permute-done((bf16[192,4608]{1,0:T(8,128)(2,1)}, bf16[192,4608]{1,0:T(8,128)(2,1)}, u32[]{:S(2)}, u32[]{:S(2)}) %collective-permute-start.4) | collective-permute-done | bytes 1769504 | tf_op jit(solution)/shard_map/ppermute | solution.py:481
  86.2 1.3 collective-permute-done.5.refs_2_
  87.5 1.6 collective-permute-start.8
  89.1 0.4 collective-permute-start.9
  89.5 0.5 collective-permute-start.15
  90.1 9.3 %attend.3.attn_ref = bf16[576,1536]{1,0:T(8,128)(2,1)} custom-call(s32[1]{0:T(128)} %bitcast.2.half_ref.part_ref, bf16[3,3,96,3072]{3,2,1,0:T(8,128)(2,1)} %bitcast.34, bf16[3,3,96,1536]{3,2,1,0:T(8,128)(2,1)} %collective-permute-done.far_ref, f32[576,128]{1,0:T(8,128)} %get-tuple-element.63.cq_ref, ...), custom_call_target="tpu_custom_call", output_to_operand_aliasing={{}: (9, {})} | custom-call | flops 1019215872 | bytes 7077888 | tf_op jit(solution)/shard_map/attend/pallas_call | solution.py:286
  99.3 11.7 %collective-permute-done.10.units_ref = bf16[3,96,3072]{2,1,0:T(8,128)(2,1)} collective-permute-done((bf16[3,96,3072]{2,1,0:T(8,128)(2,1)}, bf16[3,96,3072]{2,1,0:T(8,128)(2,1)}, u32[]{:S(2)}, u32[]{:S(2)}) %collective-permute-start.10) | collective-permute-done | bytes 1769504 | tf_op jit(solution)/shard_map/ppermute | solution.py:537
  111.1 3.0 %activate.3.act_ref = bf16[576,3072]{1,0:T(8,128)(2,1)S(1)} custom-call(s32[1]{0:T(128)} %constant.38.clone.1.part_ref, bf16[3,96,3072]{2,1,0:T(8,128)(2,1)} %collective-permute-done.10.units_ref, bf16[576,3072]{1,0:T(8,128)(2,1)S(1)} %activate.2.refs_0_), custom_call_target="tpu_custom_call", output_to_operand_aliasing={{}: (2, {})} | custom-call | flops 3538944 | bytes 884736 | tf_op jit(solution)/shard_map/activate/pallas_call | solution.py:323
  114.0 3.6 %project.6 = bf16[288,384]{1,0:T(8,128)(2,1)S(1)} custom-call(s32[1]{0:T(128)} %bitcast.1.core_ref, bf16[576,1536]{1,0:T(8,128)(2,1)S(1)} %copy-done, bf16[576,3072]{1,0:T(8,128)(2,1)S(1)} %activate.3.act_ref, bf16[192,4608]{1,0:T(8,128)(2,1)} %pad_maximum_fusion.refs_0_, bf16[192,4608]{1,0:T(8,128)(2,1)} %collective-permute-done.3.refs_1_), custom_call_target="tpu_custom_call" | custom-call | flops 254803968 | bytes 442368 | tf_op jit(solution)/shard_map/project/pallas_call | solution.py:376
  117.6 1.7 collective-permute-start.11
  119.3 6.5 %project.7 = (bf16[288,768]{1,0:T(8,128)(2,1)S(1)}, bf16[288,768]{1,0:T(8,128)(2,1)S(1)}) custom-call(s32[1]{0:T(128)} %bitcast.1.core_ref, bf16[576,1536]{1,0:T(8,128)(2,1)S(1)} %copy-done, bf16[576,3072]{1,0:T(8,128)(2,1)S(1)} %activate.3.act_ref, bf16[192,4608]{1,0:T(8,128)(2,1)} %collective-permute-done.1.refs_0_, ...), custom_call_target="tpu_custom_call" | custom-call | flops 509607936 | bytes 884736 | tf_op jit(solution)/shard_map/project/pallas_call | solution.py:376
  125.9 0.7 copy-done.15
  126.6 0.5 collective-permute-done.9.refs_2_
  127.1 0.5 collective-permute-start.18
  127.6 1.5 collective-permute-start.16
  129.1 1.2 slice.6
  130.3 1.2 slice.7
  131.6 1.6 collective-permute-start.12
  133.2 0.5 collective-permute-start.13
  133.7 6.5 %project.8 = (bf16[288,768]{1,0:T(8,128)(2,1)S(1)}, bf16[288,768]{1,0:T(8,128)(2,1)S(1)}) custom-call(s32[1]{0:T(128)} %bitcast.1.core_ref, bf16[576,1536]{1,0:T(8,128)(2,1)S(1)} %copy-done, bf16[576,3072]{1,0:T(8,128)(2,1)S(1)} %activate.3.act_ref, bf16[192,4608]{1,0:T(8,128)(2,1)} %collective-permute-done.4.refs_0_, ...), custom_call_target="tpu_custom_call" | custom-call | flops 509607936 | bytes 884736 | tf_op jit(solution)/shard_map/project/pallas_call | solution.py:376
  140.2 0.7 copy-done.8
  141.0 0.5 collective-permute-start.19
  141.5 6.8 %project.9 = (bf16[288,768]{1,0:T(8,128)(2,1)S(1)}, bf16[288,768]{1,0:T(8,128)(2,1)}) custom-call(s32[1]{0:T(128)} %bitcast.1.core_ref, bf16[576,1536]{1,0:T(8,128)(2,1)S(1)} %copy-done, bf16[576,3072]{1,0:T(8,128)(2,1)S(1)} %activate.3.act_ref, bf16[192,4608]{1,0:T(8,128)(2,1)} %collective-permute-done.8.refs_0_, ...), custom_call_target="tpu_custom_call" | custom-call | flops 509607936 | bytes 884736 | tf_op jit(solution)/shard_map/project/pallas_call | solution.py:376
  148.3 3.9 %collective-permute-done.19.refs_5_ = bf16[288,768]{1,0:T(8,128)(2,1)S(1)} collective-permute-done((bf16[288,768]{1,0:T(8,128)(2,1)S(1)}, bf16[288,768]{1,0:T(8,128)(2,1)S(1)}, u32[]{:S(2)}, u32[]{:S(2)}) %collective-permute-start.19) | collective-permute-done | bytes 442400 | tf_op jit(solution)/shard_map/ppermute | solution.py:552
  152.2 0.7 collective-permute-done.12.refs_0_
  152.9 1.3 collective-permute-done.13.refs_2_
  154.2 0.5 collective-permute-start.21
  154.7 0.5 collective-permute-start.22
  155.2 1.4 collective-permute-done.20.refs_1_
  156.7 1.3 collective-permute-done.21.refs_3_
  157.9 4.4 %project.10 = (bf16[288,384]{1,0:T(8,128)(2,1)S(1)}, bf16[288,384]{1,0:T(8,128)(2,1)}) custom-call(s32[1]{0:T(128)} %bitcast.1.core_ref, bf16[576,1536]{1,0:T(8,128)(2,1)S(1)} %copy-done, bf16[576,3072]{1,0:T(8,128)(2,1)S(1)} %activate.3.act_ref, bf16[96,4608]{1,0:T(8,128)(2,1)S(1)} %collective-permute-done.12.refs_0_, ...), custom_call_target="tpu_custom_call" | custom-call | flops 254803968 | bytes 442368 | tf_op jit(solution)/shard_map/project/pallas_call | solution.py:376
  162.3 0.7 copy-done.17
  163.0 0.5 collective-permute-start.23
  163.5 0.7 copy.23.refs_16_
  164.9 0.0 copy-start.1
  164.9 1.5 copy-done.1
  166.4 0.0 copy-start.14
  166.4 0.0 copy-start.19
  166.4 0.0 copy-start.20
  166.4 0.0 copy-start.21
  166.4 0.0 copy-start.22
  166.5 0.0 copy-start.23
  166.5 0.0 copy-start.24
  166.5 0.0 copy-start.25
  166.5 3.7 %project.11.refs_0_ = bf16[288,384]{1,0:T(8,128)(2,1)S(1)} custom-call(s32[1]{0:T(128)} %bitcast.1.core_ref, bf16[576,1536]{1,0:T(8,128)(2,1)S(1)} %copy-done.1, bf16[576,3072]{1,0:T(8,128)(2,1)S(1)} %activate.3.act_ref, bf16[192,4608]{1,0:T(8,128)(2,1)} %pad_maximum_fusion.refs_0_, bf16[192,4608]{1,0:T(8,128)(2,1)} %collective-permute-done.3.refs_1_), custom_call_target="tpu_custom_call" | custom-call | flops 254803968 | bytes 442368 | tf_op jit(solution)/shard_map/project/pallas_call | solution.py:376
  170.2 1.6 collective-permute-done.23.refs_9_
  172.0 5.3 %finish.1 = (bf16[3,96,3072]{2,1,0:T(8,128)(2,1)}, f32[2,64,96]{2,1,0:T(8,128)}) custom-call(s32[1]{0:T(128)} %bitcast.tile_ref, s32[16]{0:T(128)S(1)} %copy-done.25, f32[1]{0:T(128)S(6)} %copy.27.step_ref, bf16[288,384]{1,0:T(8,128)(2,1)S(1)} %project.11.refs_0_, bf16[288,384]{1,0:T(8,128)(2,1)S(1)} %copy-done.16, bf16[288,768]{1,0:T(8,128)(2,1)S(1)} %copy-done.5, ...), custom_call_target="tpu_custom_call" | custom-call | flops 141557760 | bytes 8847360 | tf_op jit(solution)/shard_map/finish/pallas_call | solution.py:444
  (56 shorter events, 0.1 us)
Async XLA Ops:
  3.4 41.9 %collective-permute-start.1 = (bf16[192,4608]{1,0:T(8,128)(2,1)}, bf16[192,4608]{1,0:T(8,128)(2,1)}, u32[]{:S(2)}, u32[]{:S(2)}) collective-permute-start(bf16[192,4608]{1,0:T(8,128)(2,1)} %pad_maximum_fusion.refs_0_), channel_id=1, source_target_pairs={{0,4},{2,6},{4,12},{6,14},{12,20},{14,22},{20,28},{22,30},{28,24},... | collective-permute-start | bytes 5308424 | tf_op jit(solution)/shard_map/ppermute | solution.py:481
  6.4 40.4 %collective-permute-start.2 = (bf16[192,4608]{1,0:T(8,128)(2,1)}, bf16[192,4608]{1,0:T(8,128)(2,1)}, u32[]{:S(2)}, u32[]{:S(2)}) collective-permute-start(bf16[192,4608]{1,0:T(8,128)(2,1)} %pad_maximum_fusion.refs_0_), channel_id=1, source_target_pairs={{0,8},{2,10},{4,0},{6,2},{12,4},{14,6},{20,12},{22,14},{28,20},{30... | collective-permute-start | bytes 5308424 | tf_op jit(solution)/shard_map/ppermute | solution.py:481
  6.4 40.3 %collective-permute-start.3 = (bf16[192,4608]{1,0:T(8,128)(2,1)}, bf16[192,4608]{1,0:T(8,128)(2,1)}, u32[]{:S(2)}, u32[]{:S(2)}) collective-permute-start(bf16[192,4608]{1,0:T(8,128)(2,1)} %pad_maximum_fusion.refs_0_), channel_id=1, source_target_pairs={{0,2},{2,0},{4,6},{6,4},{8,10},{10,8},{12,14},{14,12},{16,18},{18,... | collective-permute-start | bytes 5308424 | tf_op jit(solution)/shard_map/ppermute | solution.py:485
  9.8 60.5 %collective-permute-start = (bf16[3,3,96,1536]{3,2,1,0:T(8,128)(2,1)}, bf16[3,3,96,1536]{3,2,1,0:T(8,128)(2,1)}, u32[]{:S(2)}, u32[]{:S(2)}) collective-permute-start(bf16[3,3,96,1536]{3,2,1,0:T(8,128)(2,1)} %dynamic-slice_bitcast_fusion), channel_id=1, source_target_pairs={{0,1},{1,0},{2,3},{3,2},{4,5},{5,4},{6,7},{7,6},{8,9},{9,8},{10,11... | collective-permute-start | bytes 7962632 | tf_op jit(solution)/shard_map/ppermute | solution.py:523
  15.8 2.0 %copy-start.2 = (bf16[1,3,96,6144]{3,2,1,0:T(8,128)(2,1)S(1)}, bf16[1,3,96,6144]{3,2,1,0:T(8,128)(2,1)}, u32[]{:S(2)}) copy-start(bf16[1,3,96,6144]{3,2,1,0:T(8,128)(2,1)} %param.20) | copy-start | bytes 10616836
  46.7 39.5 %collective-permute-start.4 = (bf16[192,4608]{1,0:T(8,128)(2,1)}, bf16[192,4608]{1,0:T(8,128)(2,1)}, u32[]{:S(2)}, u32[]{:S(2)}) collective-permute-start(bf16[192,4608]{1,0:T(8,128)(2,1)} %collective-permute-done.1.refs_0_), channel_id=1, source_target_pairs={{0,4},{2,6},{4,12},{6,14},{12,20},{14,22},{20,28},{22,30},{28,24},... | collective-permute-start | bytes 5308424 | tf_op jit(solution)/shard_map/ppermute | solution.py:481
  48.3 39.2 %collective-permute-start.5 = (bf16[192,4608]{1,0:T(8,128)(2,1)}, bf16[192,4608]{1,0:T(8,128)(2,1)}, u32[]{:S(2)}, u32[]{:S(2)}) collective-permute-start(bf16[192,4608]{1,0:T(8,128)(2,1)} %collective-permute-done.2.refs_2_), channel_id=1, source_target_pairs={{0,8},{2,10},{4,0},{6,2},{12,4},{14,6},{20,12},{22,14},{28,20},{30... | collective-permute-start | bytes 5308424 | tf_op jit(solution)/shard_map/ppermute | solution.py:481
  48.8 38.7 %collective-permute-start.6 = (bf16[192,4608]{1,0:T(8,128)(2,1)}, bf16[192,4608]{1,0:T(8,128)(2,1)}, u32[]{:S(2)}, u32[]{:S(2)}) collective-permute-start(bf16[192,4608]{1,0:T(8,128)(2,1)} %collective-permute-done.1.refs_0_), channel_id=1, source_target_pairs={{0,2},{2,0},{4,6},{6,4},{8,10},{10,8},{12,14},{14,12},{16,18},{18,... | collective-permute-start | bytes 5308424 | tf_op jit(solution)/shard_map/ppermute | solution.py:485
  48.8 38.7 %collective-permute-start.7 = (bf16[192,4608]{1,0:T(8,128)(2,1)}, bf16[192,4608]{1,0:T(8,128)(2,1)}, u32[]{:S(2)}, u32[]{:S(2)}) collective-permute-start(bf16[192,4608]{1,0:T(8,128)(2,1)} %collective-permute-done.2.refs_2_), channel_id=1, source_target_pairs={{0,2},{2,0},{4,6},{6,4},{8,10},{10,8},{12,14},{14,12},{16,18},{18,... | collective-permute-start | bytes 5308424 | tf_op jit(solution)/shard_map/ppermute | solution.py:485
  70.4 40.7 %collective-permute-start.10 = (bf16[3,96,3072]{2,1,0:T(8,128)(2,1)}, bf16[3,96,3072]{2,1,0:T(8,128)(2,1)}, u32[]{:S(2)}, u32[]{:S(2)}) collective-permute-start(bf16[3,96,3072]{2,1,0:T(8,128)(2,1)} %dynamic-slice_bitcast_fusion.1), channel_id=1, source_target_pairs={{0,1},{1,0},{2,3},{3,2},{4,5},{5,4},{6,7},{7,6},{8,9},{9,8},{10,11... | collective-permute-start | bytes 5308424 | tf_op jit(solution)/shard_map/ppermute | solution.py:537
  87.5 39.1 %collective-permute-start.8 = (bf16[192,4608]{1,0:T(8,128)(2,1)}, bf16[192,4608]{1,0:T(8,128)(2,1)}, u32[]{:S(2)}, u32[]{:S(2)}) collective-permute-start(bf16[192,4608]{1,0:T(8,128)(2,1)} %collective-permute-done.4.refs_0_), channel_id=1, source_target_pairs={{0,4},{2,6},{4,12},{6,14},{12,20},{14,22},{20,28},{22,30},{28,24},... | collective-permute-start | bytes 5308424 | tf_op jit(solution)/shard_map/ppermute | solution.py:481
  89.1 38.0 %collective-permute-start.9 = (bf16[192,4608]{1,0:T(8,128)(2,1)}, bf16[192,4608]{1,0:T(8,128)(2,1)}, u32[]{:S(2)}, u32[]{:S(2)}) collective-permute-start(bf16[192,4608]{1,0:T(8,128)(2,1)} %collective-permute-done.5.refs_2_), channel_id=1, source_target_pairs={{0,8},{2,10},{4,0},{6,2},{12,4},{14,6},{20,12},{22,14},{28,20},{30... | collective-permute-start | bytes 5308424 | tf_op jit(solution)/shard_map/ppermute | solution.py:481
  89.5 42.0 %collective-permute-start.14 = (bf16[192,4608]{1,0:T(8,128)(2,1)}, bf16[192,4608]{1,0:T(8,128)(2,1)}, u32[]{:S(2)}, u32[]{:S(2)}) collective-permute-start(bf16[192,4608]{1,0:T(8,128)(2,1)} %collective-permute-done.4.refs_0_), channel_id=1, source_target_pairs={{0,2},{2,0},{4,6},{6,4},{8,10},{10,8},{12,14},{14,12},{16,18},{18,... | collective-permute-start | bytes 5308424 | tf_op jit(solution)/shard_map/ppermute | solution.py:485
  89.5 43.7 %collective-permute-start.15 = (bf16[192,4608]{1,0:T(8,128)(2,1)}, bf16[192,4608]{1,0:T(8,128)(2,1)}, u32[]{:S(2)}, u32[]{:S(2)}) collective-permute-start(bf16[192,4608]{1,0:T(8,128)(2,1)} %collective-permute-done.5.refs_2_), channel_id=1, source_target_pairs={{0,2},{2,0},{4,6},{6,4},{8,10},{10,8},{12,14},{14,12},{16,18},{18,... | collective-permute-start | bytes 5308424 | tf_op jit(solution)/shard_map/ppermute | solution.py:485
  99.3 14.7 %copy-start = (bf16[576,1536]{1,0:T(8,128)(2,1)S(1)}, bf16[576,1536]{1,0:T(8,128)(2,1)}, u32[]{:S(2)}) copy-start(bf16[576,1536]{1,0:T(8,128)(2,1)} %attend.3.attn_ref) | copy-start | bytes 5308420
  117.6 8.2 %collective-permute-start.11 = (bf16[288,384]{1,0:T(8,128)(2,1)S(1)}, bf16[288,384]{1,0:T(8,128)(2,1)S(1)}, u32[]{:S(2)}, u32[]{:S(2)}) collective-permute-start(bf16[288,384]{1,0:T(8,128)(2,1)S(1)} %project.6), channel_id=1, source_target_pairs={{0,1},{1,0},{2,3},{3,2},{4,5},{5,4},{6,7},{7,6},{8,9},{9,8},{10,11... | collective-permute-start | bytes 663560 | tf_op jit(solution)/shard_map/ppermute | solution.py:556
  125.8 5.7 %copy-start.4 = (bf16[288,768]{1,0:T(8,128)(2,1)}, bf16[288,768]{1,0:T(8,128)(2,1)S(1)}, u32[]{:S(2)}) copy-start(bf16[288,768]{1,0:T(8,128)(2,1)S(1)} %get-tuple-element.100.refs_2_) | copy-start | bytes 1327108
  125.9 0.7 copy-start.15
  127.1 14.4 %collective-permute-start.17 = (bf16[192,4608]{1,0:T(8,128)(2,1)}, bf16[192,4608]{1,0:T(8,128)(2,1)S(1)}, u32[]{:S(2)}, u32[]{:S(2)}) collective-permute-start(bf16[192,4608]{1,0:T(8,128)(2,1)} %collective-permute-done.8.refs_0_), channel_id=1, source_target_pairs={{0,2},{2,0},{4,6},{6,4},{8,10},{10,8},{12,14},{14,12},{16,18},{18,... | collective-permute-start | bytes 5308424 | tf_op jit(solution)/shard_map/ppermute | solution.py:485
  127.1 14.4 %collective-permute-start.18 = (bf16[192,4608]{1,0:T(8,128)(2,1)}, bf16[192,4608]{1,0:T(8,128)(2,1)S(1)}, u32[]{:S(2)}, u32[]{:S(2)}) collective-permute-start(bf16[192,4608]{1,0:T(8,128)(2,1)} %collective-permute-done.9.refs_2_), channel_id=1, source_target_pairs={{0,2},{2,0},{4,6},{6,4},{8,10},{10,8},{12,14},{14,12},{16,18},{18,... | collective-permute-start | bytes 5308424 | tf_op jit(solution)/shard_map/ppermute | solution.py:485
  127.6 13.4 %collective-permute-start.16 = (bf16[288,768]{1,0:T(8,128)(2,1)S(1)}, bf16[288,768]{1,0:T(8,128)(2,1)S(1)}, u32[]{:S(2)}, u32[]{:S(2)}) collective-permute-start(bf16[288,768]{1,0:T(8,128)(2,1)S(1)} %get-tuple-element.85), channel_id=1, source_target_pairs={{0,1},{1,0},{2,3},{3,2},{4,5},{5,4},{6,7},{7,6},{8,9},{9,8},{10,11... | collective-permute-start | bytes 1327112 | tf_op jit(solution)/shard_map/ppermute | solution.py:552
  131.6 21.3 %collective-permute-start.12 = (bf16[96,4608]{1,0:T(8,128)(2,1)S(1)}, bf16[96,4608]{1,0:T(8,128)(2,1)S(1)}, u32[]{:S(2)}, u32[]{:S(2)}) collective-permute-start(bf16[96,4608]{1,0:T(8,128)(2,1)S(1)} %slice.6), channel_id=1, source_target_pairs={{0,4},{2,6},{4,12},{6,14},{12,20},{14,22},{20,28},{22,30},{28,24},... | collective-permute-start | bytes 2654216 | tf_op jit(solution)/shard_map/ppermute | solution.py:481
  133.2 21.0 %collective-permute-start.13 = (bf16[96,4608]{1,0:T(8,128)(2,1)S(1)}, bf16[96,4608]{1,0:T(8,128)(2,1)S(1)}, u32[]{:S(2)}, u32[]{:S(2)}) collective-permute-start(bf16[96,4608]{1,0:T(8,128)(2,1)S(1)} %slice.7), channel_id=1, source_target_pairs={{0,8},{2,10},{4,0},{6,2},{12,4},{14,6},{20,12},{22,14},{28,20},{30... | collective-permute-start | bytes 2654216 | tf_op jit(solution)/shard_map/ppermute | solution.py:481
  140.2 0.8 copy-start.8
  141.0 7.3 %copy-start.6 = (bf16[288,768]{1,0:T(8,128)(2,1)}, bf16[288,768]{1,0:T(8,128)(2,1)S(1)}, u32[]{:S(2)}) copy-start(bf16[288,768]{1,0:T(8,128)(2,1)S(1)} %collective-permute-done.16.refs_3_) | copy-start | bytes 1327108
  141.0 11.2 %collective-permute-start.19 = (bf16[288,768]{1,0:T(8,128)(2,1)S(1)}, bf16[288,768]{1,0:T(8,128)(2,1)S(1)}, u32[]{:S(2)}, u32[]{:S(2)}) collective-permute-start(bf16[288,768]{1,0:T(8,128)(2,1)S(1)} %get-tuple-element.89), channel_id=1, source_target_pairs={{0,1},{1,0},{2,3},{3,2},{4,5},{5,4},{6,7},{7,6},{8,9},{9,8},{10,11... | collective-permute-start | bytes 1327112 | tf_op jit(solution)/shard_map/ppermute | solution.py:552
  148.3 14.0 %copy-start.12 = (bf16[288,768]{1,0:T(8,128)(2,1)}, bf16[288,768]{1,0:T(8,128)(2,1)S(1)}, u32[]{:S(2)}) copy-start(bf16[288,768]{1,0:T(8,128)(2,1)S(1)} %get-tuple-element.104.refs_6_) | copy-start | bytes 1327108
  152.2 10.1 %copy-start.10 = (bf16[288,768]{1,0:T(8,128)(2,1)}, bf16[288,768]{1,0:T(8,128)(2,1)S(1)}, u32[]{:S(2)}) copy-start(bf16[288,768]{1,0:T(8,128)(2,1)S(1)} %collective-permute-done.19.refs_5_) | copy-start | bytes 1327108
  154.2 9.3 %copy-start.26 = (f32[64]{0:T(128)S(1)}, f32[64]{0:T(128)}, u32[]{:S(2)}) copy-start(f32[64]{0:T(128)} %param.32) | copy-start | bytes 772
  154.2 2.4 %collective-permute-start.20 = (bf16[96,4608]{1,0:T(8,128)(2,1)S(1)}, bf16[96,4608]{1,0:T(8,128)(2,1)S(1)}, u32[]{:S(2)}, u32[]{:S(2)}) collective-permute-start(bf16[96,4608]{1,0:T(8,128)(2,1)S(1)} %collective-permute-done.12.refs_0_), channel_id=1, source_target_pairs={{0,2},{2,0},{4,6},{6,4},{8,10},{10,8},{12,14},{14,12},{16,18},{18,... | collective-permute-start | bytes 2654216 | tf_op jit(solution)/shard_map/ppermute | solution.py:485
  154.2 3.7 %collective-permute-start.21 = (bf16[96,4608]{1,0:T(8,128)(2,1)S(1)}, bf16[96,4608]{1,0:T(8,128)(2,1)S(1)}, u32[]{:S(2)}, u32[]{:S(2)}) collective-permute-start(bf16[96,4608]{1,0:T(8,128)(2,1)S(1)} %collective-permute-done.13.refs_2_), channel_id=1, source_target_pairs={{0,2},{2,0},{4,6},{6,4},{8,10},{10,8},{12,14},{14,12},{16,18},{18,... | collective-permute-start | bytes 2654216 | tf_op jit(solution)/shard_map/ppermute | solution.py:485
  154.7 15.5 %collective-permute-start.22 = (bf16[288,768]{1,0:T(8,128)(2,1)}, bf16[288,768]{1,0:T(8,128)(2,1)}, u32[]{:S(2)}, u32[]{:S(2)}) collective-permute-start(bf16[288,768]{1,0:T(8,128)(2,1)} %get-tuple-element.92), channel_id=1, source_target_pairs={{0,1},{1,0},{2,3},{3,2},{4,5},{5,4},{6,7},{7,6},{8,9},{9,8},{10,11... | collective-permute-start | bytes 1327112 | tf_op jit(solution)/shard_map/ppermute | solution.py:552
  162.3 0.7 copy-start.17
  163.0 8.9 %collective-permute-start.23 = (bf16[288,384]{1,0:T(8,128)(2,1)}, bf16[288,384]{1,0:T(8,128)(2,1)}, u32[]{:S(2)}, u32[]{:S(2)}) collective-permute-start(bf16[288,384]{1,0:T(8,128)(2,1)} %get-tuple-element.97), channel_id=1, source_target_pairs={{0,1},{1,0},{2,3},{3,2},{4,5},{5,4},{6,7},{7,6},{8,9},{9,8},{10,11... | collective-permute-start | bytes 663560 | tf_op jit(solution)/shard_map/ppermute | solution.py:552
  164.9 1.5 copy-start.1
  166.3 5.5 %copy-start.3 = (bf16[1,3,96,3072]{3,2,1,0:T(8,128)(2,1)S(1)}, bf16[1,3,96,3072]{3,2,1,0:T(8,128)(2,1)}, u32[]{:S(2)}) copy-start(bf16[1,3,96,3072]{3,2,1,0:T(8,128)(2,1)} %param.21) | copy-start | bytes 5308420
  166.3 5.5 %copy-start.5 = (bf16[288,768]{1,0:T(8,128)(2,1)S(1)}, bf16[288,768]{1,0:T(8,128)(2,1)}, u32[]{:S(2)}) copy-start(bf16[288,768]{1,0:T(8,128)(2,1)} %copy-done.4) | copy-start | bytes 1327108
  166.3 5.5 %copy-start.7 = (bf16[288,768]{1,0:T(8,128)(2,1)S(1)}, bf16[288,768]{1,0:T(8,128)(2,1)}, u32[]{:S(2)}) copy-start(bf16[288,768]{1,0:T(8,128)(2,1)} %copy-done.6) | copy-start | bytes 1327108
  166.4 5.5 %copy-start.9 = (bf16[288,768]{1,0:T(8,128)(2,1)S(1)}, bf16[288,768]{1,0:T(8,128)(2,1)}, u32[]{:S(2)}) copy-start(bf16[288,768]{1,0:T(8,128)(2,1)} %copy-done.8) | copy-start | bytes 1327108
  166.4 5.5 %copy-start.11 = (bf16[288,768]{1,0:T(8,128)(2,1)S(1)}, bf16[288,768]{1,0:T(8,128)(2,1)}, u32[]{:S(2)}) copy-start(bf16[288,768]{1,0:T(8,128)(2,1)} %copy-done.10) | copy-start | bytes 1327108
  166.4 5.5 %copy-start.13 = (bf16[288,768]{1,0:T(8,128)(2,1)S(1)}, bf16[288,768]{1,0:T(8,128)(2,1)}, u32[]{:S(2)}) copy-start(bf16[288,768]{1,0:T(8,128)(2,1)} %copy-done.12) | copy-start | bytes 1327108
  166.4 5.5 %copy-start.14 = (bf16[3072,64]{0,1:T(8,128)(2,1)S(1)}, bf16[3072,64]{0,1:T(8,128)(2,1)}, u32[]{:S(2)}) copy-start(bf16[3072,64]{0,1:T(8,128)(2,1)} %param.31) | copy-start | bytes 1179652
  166.4 5.5 %copy-start.16 = (bf16[288,384]{1,0:T(8,128)(2,1)S(1)}, bf16[288,384]{1,0:T(8,128)(2,1)}, u32[]{:S(2)}) copy-start(bf16[288,384]{1,0:T(8,128)(2,1)} %copy-done.15) | copy-start | bytes 663556
  166.4 5.5 %copy-start.18 = (bf16[288,384]{1,0:T(8,128)(2,1)S(1)}, bf16[288,384]{1,0:T(8,128)(2,1)}, u32[]{:S(2)}) copy-start(bf16[288,384]{1,0:T(8,128)(2,1)} %copy-done.17) | copy-start | bytes 663556
  166.4 5.5 %copy-start.19 = (f32[64,1]{1,0:T(8,128)S(1)}, f32[64,1]{1,0:T(8,128)}, u32[]{:S(2)}) copy-start(f32[64,1]{1,0:T(8,128)} %copy.23.refs_16_) | copy-start | bytes 772
  166.4 5.5 %copy-start.20 = (f32[1,2,96,64]{2,3,1,0:T(8,128)S(1)}, f32[1,2,96,64]{2,3,1,0:T(8,128)}, u32[]{:S(2)}) copy-start(f32[1,2,96,64]{2,3,1,0:T(8,128)} %param.33) | copy-start | bytes 147460
  166.4 5.5 %copy-start.21 = (f32[3072]{0:T(1024)S(1)}, f32[3072]{0:T(1024)}, u32[]{:S(2)}) copy-start(f32[3072]{0:T(1024)} %param.27) | copy-start | bytes 36868
  166.4 5.5 %copy-start.22 = (f32[1,3072]{1,0:T(1,128)S(1)}, f32[1,3072]{1,0:T(1,128)}, u32[]{:S(2)}) copy-start(f32[1,3072]{1,0:T(1,128)} %refs_12_.1) | copy-start | bytes 36868
  166.5 5.5 %copy-start.23 = (f32[1,3072]{1,0:T(1,128)S(1)}, f32[1,3072]{1,0:T(1,128)}, u32[]{:S(2)}) copy-start(f32[1,3072]{1,0:T(1,128)} %refs_13_.1) | copy-start | bytes 36868
  166.5 5.5 %copy-start.24 = (f32[1,3072]{1,0:T(1,128)S(1)}, f32[1,3072]{1,0:T(1,128)}, u32[]{:S(2)}) copy-start(f32[1,3072]{1,0:T(1,128)} %refs_14_.1) | copy-start | bytes 36868
  166.5 5.5 %copy-start.25 = (s32[16]{0:T(128)S(1)}, s32[16]{0:T(128)}, u32[]{:S(2)}) copy-start(s32[16]{0:T(128)} %constant.41.clone.place_ref) | copy-start | bytes 196

commit v5 on v4

--- a/solution.py
+++ b/solution.py
@@ -250,14 +250,13 @@
     )
 
 
-def attend_kernel(half_ref, own_ref, far_ref, cq_ref, sq_ref, ck_ref, sk_ref, mask_ref, swap_ref, *refs):
+def attend_kernel(half_ref, own_ref, far_q_ref, far_kv_ref, cq_ref, sq_ref, ck_ref, sk_ref, mask_ref, swap_ref, *refs):
     out_ref = refs[-1]
     rows = own_ref.shape[0] * own_ref.shape[2]
 
     def load(part):
-        return jnp.concatenate(
-            [own_ref[:, part].reshape(rows, HEAD_DIM), far_ref[:, part].reshape(rows, HEAD_DIM)], axis=0
-        )
+        far = far_q_ref[...] if part == 0 else far_kv_ref[:, part - 1]
+        return jnp.concatenate([own_ref[:, part].reshape(rows, HEAD_DIM), far.reshape(rows, HEAD_DIM)], axis=0)
 
     def turn(raw, straight, crossed):
         wide = raw.astype(jnp.float32)
@@ -276,12 +275,12 @@
 
 
 def attend(half, own, far, tables, part, parts, into=None):
-    blocks, kinds, slots, width = far.shape
+    far_q, far_kv = far
+    blocks, slots, width = far_q.shape
     heads = width // HEAD_DIM
     count = heads // parts
     first = part * count
     rows = 2 * blocks * slots
-    shape = (blocks, kinds, slots, HEAD_DIM)
     whole = pl.BlockSpec((rows, HEAD_DIM), lambda g, half: (0, 0))
     return pl.pallas_call(
         attend_kernel,
@@ -289,8 +288,9 @@
             num_scalar_prefetch=1,
             grid=(count,),
             in_specs=[
-                pl.BlockSpec(shape, lambda g, half: (0, 0, 0, half[0] * heads + first + g)),
-                pl.BlockSpec(shape, lambda g, half: (0, 0, 0, first + g)),
+                pl.BlockSpec((blocks, 3, slots, HEAD_DIM), lambda g, half: (0, 0, 0, half[0] * heads + first + g)),
+                pl.BlockSpec((blocks, slots, HEAD_DIM), lambda g, half: (0, 0, first + g)),
+                pl.BlockSpec((blocks, 2, slots, HEAD_DIM), lambda g, half: (0, 0, 0, first + g)),
                 whole,
                 whole,
                 whole,
@@ -302,7 +302,7 @@
             out_specs=pl.BlockSpec((rows, HEAD_DIM), lambda g, half: (0, first + g)),
         ),
         out_shape=jax.ShapeDtypeStruct((rows, width), jnp.bfloat16),
-        input_output_aliases={} if into is None else {9: 0},
+        input_output_aliases={} if into is None else {10: 0},
         compiler_params=pltpu.CompilerParams(vmem_limit_bytes=VMEM),
         cost_estimate=pl.CostEstimate(
             flops=count * rows * rows * HEAD_DIM * 4,
@@ -310,7 +310,7 @@
             transcendentals=0,
         ),
         name="attend",
-    )(half, own, far, *tables, *([] if into is None else [into]))
+    )(half, own, far_q, far_kv, *tables, *([] if into is None else [into]))
 
 
 def gelu_kernel(part_ref, units_ref, *refs):
@@ -516,11 +516,16 @@
     slots = own_attn.shape[2]
     units = own_units.shape[2] // partners
     width = own_attn.shape[3] // partners
-    sent_attn = lax.dynamic_slice_in_dim(own_attn, (1 - me) * width, width, axis=3)
+    blocks, kinds, slots, _ = own_attn.shape
+    sent_attn = [
+        lax.dynamic_slice(own_attn, (0, first, 0, (1 - me) * width), (blocks, count, slots, width))
+        for first, count in ((0, 1), (1, kinds - 1))
+    ]
     block = jnp.concatenate([w_out_attn.T, w_out_mlp.T], axis=1)
 
     onward, back = hop(block, 1), hop(block, -1)
-    far_attn = trade(sent_attn)
+    far_attn = [trade(part) for part in sent_attn]
+    far_attn[0] = far_attn[0][:, 0]
     chips = [both_cores(block)]
 
     tables = make_tables(half, text_len, q_gain, k_gain, 6 * slots)

time: 178 us -> 181 us (1.017)
    ppermute x8, waiting for transfers between devices: 34.7 us -> 40.7 us  [hop(): return lax.ppermute(array, 'tile', pairs)]
    ppermute x1, waiting for transfers between devices: 11.7 us -> 8.36 us  [paired(): far_units = trade(sent_units)]
    dynamic_slice x1 -> x2, local copies, waits for them, and re-layouts: 3.4 us -> 5.11 us  [paired(): lax.dynamic_slice(own_attn, (0, first, 0, (1 - me) * width), (blocks, cou...]
    ppermute x1 -> x2, waiting for transfers between devices: 21.1 us -> 20.2 us  [paired(): far_attn = [trade(part) for part in sent_attn]]
  transfers between devices with their start and end apart: 24 -> 25, of which waited for: 13 -> 14; matrix products, arithmetic and copies ran while one was open for 5% -> 5% of each run, Pallas kernels for 33% -> 32%
where the time goes in v5:
time: 181 us
  waiting for transfers between devices  77.5 us (43%)
  Pallas kernels  63.2 us (35%)
  starting transfers between devices  19.4 us (11%)
  local copies, waits for them, and re-layouts  15.4 us (9%)
  other arithmetic  2.79 us (2%)
  between operations  2.35 us (1%)
    ppermute x8, waiting for transfers between devices, hop(): return lax.ppermute(array, 'tile', pairs)  40.7 us
    pallas_call x6, Pallas kernels, project(): pl.pallas_call(functools.partial(project_kernel, layout, sides), in_specs...  31.6 us
    ppermute x2, waiting for transfers between devices, paired(): far_attn = [trade(part) for part in sent_attn]  20.2 us
    pallas_call x2, Pallas kernels, attend(): pl.pallas_call(attend_kernel, grid_spec=pltpu.PrefetchScalarGridSpec(num_...  18.7 us
    ppermute x8, starting transfers between devices, hop(): return lax.ppermute(array, 'tile', pairs)  9.16 us
    ppermute x1, waiting for transfers between devices, paired(): far_units = trade(sent_units)  8.36 us
    unnamed x54, local copies, waits for them, and re-layouts  5.74 us
    ppermute x4, waiting for transfers between devices, send(): chunks.append((own, trade(sent)))  5.55 us
  transfers between devices with their start and end apart: 25, of which 14 were waited for; matrix products, arithmetic and copies ran while one was open for 5% of the time, Pallas kernels for 32%

profile of v5, /device:TPU:0, one launch (start us, length us, event | category | flops | bytes accessed | tf_op | source)
XLA Modules:
  0.0 180.7 jit_solution(1222134220879688665)
XLA Ops:
  0.6 2.8 %pad_maximum_fusion.refs_0_ = bf16[192,4608]{1,0:T(8,128)(2,1)} fusion(bf16[192,3072]{1,0:T(8,128)(2,1)} %bitcast.38, bf16[192,1536]{1,0:T(8,128)(2,1)} %bitcast.39), kind=kLoop, calls=%fused_computation | loop fusion | flops 3538944 | bytes 3538944 | tf_op jit(solution)/shard_map/concatenate | solution.py:524
  3.4 2.9 %collective-permute-start.2 = (bf16[192,4608]{1,0:T(8,128)(2,1)}, bf16[192,4608]{1,0:T(8,128)(2,1)}, u32[]{:S(2)}, u32[]{:S(2)}) collective-permute-start(bf16[192,4608]{1,0:T(8,128)(2,1)} %pad_maximum_fusion.refs_0_), channel_id=1, source_target_pairs={{0,4},{2,6},{4,12},{6,14},{12,20},{14,22},{20,28},{22,30},{28,24},... | collective-permute-start | bytes 5308424 | tf_op jit(solution)/shard_map/ppermute | solution.py:481
  6.4 0.1 collective-permute-start.3
  6.5 2.2 %dynamic-slice_bitcast_fusion.2 = bf16[3,1,96,1536]{3,2,0,1:T(8,128)(2,1)} fusion(bf16[1,3,96,3,3072]{4,2,3,1,0:T(8,128)(2,1)} %param.19, s32[]{:T(128)S(6)} %select_n.15), kind=kLoop, calls=%fused_computation.3 | loop fusion | bytes 1769476 | tf_op jit(solution)/shard_map/dynamic_slice | solution.py:521
  8.7 2.0 %collective-permute-start = (bf16[3,1,96,1536]{3,2,0,1:T(8,128)(2,1)}, bf16[3,1,96,1536]{3,2,0,1:T(8,128)(2,1)}, u32[]{:S(2)}, u32[]{:S(2)}) collective-permute-start(bf16[3,1,96,1536]{3,2,0,1:T(8,128)(2,1)} %dynamic-slice_bitcast_fusion.2), channel_id=1, source_target_pairs={{0,1},{1,0},{2,3},{3,2},{4,5},{5,4},{6,7},{7,6},{8,9},{9,8},{10,11... | collective-permute-start | bytes 2654216 | tf_op jit(solution)/shard_map/ppermute | solution.py:527
  10.7 2.9 %dynamic-slice_bitcast_fusion.1 = bf16[3,2,96,1536]{3,2,1,0:T(8,128)(2,1)} fusion(bf16[1,3,96,3,3072]{4,2,3,1,0:T(8,128)(2,1)} %param.19, s32[]{:T(128)S(6)} %select_n.15), kind=kLoop, calls=%fused_computation.2 | loop fusion | bytes 3538948 | tf_op jit(solution)/shard_map/dynamic_slice | solution.py:521
  13.5 0.1 collective-permute-start.1
  14.2 3.3 %tables.1 = (f32[576,128]{1,0:T(8,128)}, f32[576,128]{1,0:T(8,128)}, f32[576,128]{1,0:T(8,128)}, f32[576,128]{1,0:T(8,128)}, f32[1,576]{1,0:T(1,128)}, /*index=5*/bf16[128,128]{1,0:T(8,128)(2,1)}) custom-call(s32[1]{0:T(128)} %bitcast.2.half_ref.part_ref, s32[1]{0:T(128)S(6)} %copy.26.len_ref, f32[1,128]{1,0:T(1,128)} %constant.40.clone.row_freq_ref, ...), custom_call_target="tpu_custom_call" | custom-call | flops 589824 | bytes 294912 | tf_op jit(solution)/shard_map/tables/pallas_call | solution.py:229
  17.5 2.0 %copy-done.2 = bf16[1,3,96,6144]{3,2,1,0:T(8,128)(2,1)S(1)} copy-done((bf16[1,3,96,6144]{3,2,1,0:T(8,128)(2,1)S(1)}, bf16[1,3,96,6144]{3,2,1,0:T(8,128)(2,1)}, u32[]{:S(2)}) %copy-start.2) | copy-done | bytes 3538968
  19.5 1.4 activate.2.refs_0_
  20.9 1.4 dynamic-slice_bitcast_fusion
  22.3 23.0 %collective-permute-done.2.refs_0_ = bf16[192,4608]{1,0:T(8,128)(2,1)} collective-permute-done((bf16[192,4608]{1,0:T(8,128)(2,1)}, bf16[192,4608]{1,0:T(8,128)(2,1)}, u32[]{:S(2)}, u32[]{:S(2)}) %collective-permute-start.2) | collective-permute-done | bytes 1769504 | tf_op jit(solution)/shard_map/ppermute | solution.py:481
  45.4 1.4 collective-permute-done.3.refs_2_
  46.7 1.6 collective-permute-start.5
  48.3 0.4 collective-permute-start.6
  48.8 0.2 collective-permute-start.8
  49.0 20.2 %collective-permute-done.1.far_kv_ref = bf16[3,2,96,1536]{3,2,1,0:T(8,128)(2,1)} collective-permute-done((bf16[3,2,96,1536]{3,2,1,0:T(8,128)(2,1)}, bf16[3,2,96,1536]{3,2,1,0:T(8,128)(2,1)}, u32[]{:S(2)}, u32[]{:S(2)}) %collective-permute-start.1) | collective-permute-done | bytes 1769504 | tf_op jit(solution)/shard_map/ppermute | solution.py:527
  69.2 1.7 collective-permute-start.11
  71.0 9.4 %attend.2.refs_0_ = bf16[576,1536]{1,0:T(8,128)(2,1)} custom-call(s32[1]{0:T(128)} %bitcast.2.half_ref.part_ref, bf16[3,3,96,3072]{3,2,1,0:T(8,128)(2,1)} %bitcast.36, bf16[3,96,1536]{2,1,0:T(8,128)(2,1)} %bitcast.6.far_q_ref, bf16[3,2,96,1536]{3,2,1,0:T(8,128)(2,1)} %collective-permute-done.1.far_kv_ref, f32[576,128]{1,0:T(8,128)} %get-tuple-element.65.cq_ref, ...), custom_call_target="tpu_custom_call" | custom-call | flops 1019215872 | bytes 7077888 | tf_op jit(solution)/shard_map/attend/pallas_call | solution.py:285
  80.3 5.9 %collective-permute-done.5.refs_0_ = bf16[192,4608]{1,0:T(8,128)(2,1)} collective-permute-done((bf16[192,4608]{1,0:T(8,128)(2,1)}, bf16[192,4608]{1,0:T(8,128)(2,1)}, u32[]{:S(2)}, u32[]{:S(2)}) %collective-permute-start.5) | collective-permute-done | bytes 1769504 | tf_op jit(solution)/shard_map/ppermute | solution.py:481
  86.2 3.4 %collective-permute-done.6.refs_2_ = bf16[192,4608]{1,0:T(8,128)(2,1)} collective-permute-done((bf16[192,4608]{1,0:T(8,128)(2,1)}, bf16[192,4608]{1,0:T(8,128)(2,1)}, u32[]{:S(2)}, u32[]{:S(2)}) %collective-permute-start.6) | collective-permute-done | bytes 1769504 | tf_op jit(solution)/shard_map/ppermute | solution.py:481
  89.7 0.5 collective-permute-start.10
  90.1 1.6 collective-permute-start.9
  91.7 0.5 collective-permute-start.16
  92.2 9.3 %attend.3.attn_ref = bf16[576,1536]{1,0:T(8,128)(2,1)} custom-call(s32[1]{0:T(128)} %bitcast.2.half_ref.part_ref, bf16[3,3,96,3072]{3,2,1,0:T(8,128)(2,1)} %bitcast.37, bf16[3,96,1536]{2,1,0:T(8,128)(2,1)} %bitcast.6.far_q_ref, bf16[3,2,96,1536]{3,2,1,0:T(8,128)(2,1)} %collective-permute-done.1.far_kv_ref, ...), custom_call_target="tpu_custom_call", output_to_operand_aliasing={{}: (10, {})} | custom-call | flops 1019215872 | bytes 7077888 | tf_op jit(solution)/shard_map/attend/pallas_call | solution.py:285
  101.6 8.4 %collective-permute-done.11.units_ref = bf16[3,96,3072]{2,1,0:T(8,128)(2,1)} collective-permute-done((bf16[3,96,3072]{2,1,0:T(8,128)(2,1)}, bf16[3,96,3072]{2,1,0:T(8,128)(2,1)}, u32[]{:S(2)}, u32[]{:S(2)}) %collective-permute-start.11) | collective-permute-done | bytes 1769504 | tf_op jit(solution)/shard_map/ppermute | solution.py:542
  109.9 3.0 %activate.3.act_ref = bf16[576,3072]{1,0:T(8,128)(2,1)S(1)} custom-call(s32[1]{0:T(128)} %constant.39.clone.1.part_ref, bf16[3,96,3072]{2,1,0:T(8,128)(2,1)} %collective-permute-done.11.units_ref, bf16[576,3072]{1,0:T(8,128)(2,1)S(1)} %activate.2.refs_0_), custom_call_target="tpu_custom_call", output_to_operand_aliasing={{}: (2, {})} | custom-call | flops 3538944 | bytes 884736 | tf_op jit(solution)/shard_map/activate/pallas_call | solution.py:323
  112.9 3.6 %project.6 = bf16[288,384]{1,0:T(8,128)(2,1)S(1)} custom-call(s32[1]{0:T(128)} %bitcast.1.core_ref, bf16[576,1536]{1,0:T(8,128)(2,1)S(1)} %copy-done, bf16[576,3072]{1,0:T(8,128)(2,1)S(1)} %activate.3.act_ref, bf16[192,4608]{1,0:T(8,128)(2,1)} %pad_maximum_fusion.refs_0_, bf16[192,4608]{1,0:T(8,128)(2,1)} %collective-permute-done.4.refs_1_), custom_call_target="tpu_custom_call" | custom-call | flops 254803968 | bytes 442368 | tf_op jit(solution)/shard_map/project/pallas_call | solution.py:376
  116.5 1.7 collective-permute-start.12
  118.2 6.5 %project.7 = (bf16[288,768]{1,0:T(8,128)(2,1)S(1)}, bf16[288,768]{1,0:T(8,128)(2,1)S(1)}) custom-call(s32[1]{0:T(128)} %bitcast.1.core_ref, bf16[576,1536]{1,0:T(8,128)(2,1)S(1)} %copy-done, bf16[576,3072]{1,0:T(8,128)(2,1)S(1)} %activate.3.act_ref, bf16[192,4608]{1,0:T(8,128)(2,1)} %collective-permute-done.2.refs_0_, ...), custom_call_target="tpu_custom_call" | custom-call | flops 509607936 | bytes 884736 | tf_op jit(solution)/shard_map/project/pallas_call | solution.py:376
  124.7 0.7 copy-done.15
  125.5 4.8 %collective-permute-done.10.refs_2_ = bf16[192,4608]{1,0:T(8,128)(2,1)} collective-permute-done((bf16[192,4608]{1,0:T(8,128)(2,1)}, bf16[192,4608]{1,0:T(8,128)(2,1)}, u32[]{:S(2)}, u32[]{:S(2)}) %collective-permute-start.10) | collective-permute-done | bytes 1769504 | tf_op jit(solution)/shard_map/ppermute | solution.py:481
  130.2 0.2 collective-permute-done.9.refs_0_
  130.4 0.5 collective-permute-start.19
  130.9 1.5 collective-permute-start.17
  132.4 1.2 slice.6
  133.7 1.2 slice.7
  134.9 1.6 collective-permute-start.13
  136.5 0.5 collective-permute-start.14
  137.0 6.5 %project.8 = (bf16[288,768]{1,0:T(8,128)(2,1)S(1)}, bf16[288,768]{1,0:T(8,128)(2,1)S(1)}) custom-call(s32[1]{0:T(128)} %bitcast.1.core_ref, bf16[576,1536]{1,0:T(8,128)(2,1)S(1)} %copy-done, bf16[576,3072]{1,0:T(8,128)(2,1)S(1)} %activate.3.act_ref, bf16[192,4608]{1,0:T(8,128)(2,1)} %collective-permute-done.5.refs_0_, ...), custom_call_target="tpu_custom_call" | custom-call | flops 509607936 | bytes 884736 | tf_op jit(solution)/shard_map/project/pallas_call | solution.py:376
  143.6 0.8 copy-done.8
  144.3 0.5 collective-permute-start.20
  144.8 6.8 %project.9 = (bf16[288,768]{1,0:T(8,128)(2,1)S(1)}, bf16[288,768]{1,0:T(8,128)(2,1)}) custom-call(s32[1]{0:T(128)} %bitcast.1.core_ref, bf16[576,1536]{1,0:T(8,128)(2,1)S(1)} %copy-done, bf16[576,3072]{1,0:T(8,128)(2,1)S(1)} %activate.3.act_ref, bf16[192,4608]{1,0:T(8,128)(2,1)} %collective-permute-done.9.refs_0_, ...), custom_call_target="tpu_custom_call" | custom-call | flops 509607936 | bytes 884736 | tf_op jit(solution)/shard_map/project/pallas_call | solution.py:376
  151.6 3.9 %collective-permute-done.20.refs_5_ = bf16[288,768]{1,0:T(8,128)(2,1)S(1)} collective-permute-done((bf16[288,768]{1,0:T(8,128)(2,1)S(1)}, bf16[288,768]{1,0:T(8,128)(2,1)S(1)}, u32[]{:S(2)}, u32[]{:S(2)}) %collective-permute-start.20) | collective-permute-done | bytes 442400 | tf_op jit(solution)/shard_map/ppermute | solution.py:557
  155.6 0.7 collective-permute-done.13.refs_0_
  156.2 1.3 collective-permute-done.14.refs_2_
  157.5 0.5 collective-permute-start.22
  158.0 0.5 collective-permute-start.23
  158.6 1.4 collective-permute-done.21.refs_1_
  160.0 1.3 collective-permute-done.22.refs_3_
  161.2 4.4 %project.10 = (bf16[288,384]{1,0:T(8,128)(2,1)S(1)}, bf16[288,384]{1,0:T(8,128)(2,1)}) custom-call(s32[1]{0:T(128)} %bitcast.1.core_ref, bf16[576,1536]{1,0:T(8,128)(2,1)S(1)} %copy-done, bf16[576,3072]{1,0:T(8,128)(2,1)S(1)} %activate.3.act_ref, bf16[96,4608]{1,0:T(8,128)(2,1)S(1)} %collective-permute-done.13.refs_0_, ...), custom_call_target="tpu_custom_call" | custom-call | flops 254803968 | bytes 442368 | tf_op jit(solution)/shard_map/project/pallas_call | solution.py:376
  165.6 0.7 copy-done.17
  166.3 0.5 collective-permute-start.24
  166.8 0.7 copy.23.refs_16_
  168.2 0.0 copy-start.1
  168.2 1.5 copy-done.1
  169.7 0.0 copy-start.14
  169.7 0.0 copy-start.19
  169.7 0.0 copy-start.21
  169.8 0.0 copy-start.22
  169.8 0.0 copy-start.25
  169.8 3.7 %project.11.refs_0_ = bf16[288,384]{1,0:T(8,128)(2,1)S(1)} custom-call(s32[1]{0:T(128)} %bitcast.1.core_ref, bf16[576,1536]{1,0:T(8,128)(2,1)S(1)} %copy-done.1, bf16[576,3072]{1,0:T(8,128)(2,1)S(1)} %activate.3.act_ref, bf16[192,4608]{1,0:T(8,128)(2,1)} %pad_maximum_fusion.refs_0_, bf16[192,4608]{1,0:T(8,128)(2,1)} %collective-permute-done.4.refs_1_), custom_call_target="tpu_custom_call" | custom-call | flops 254803968 | bytes 442368 | tf_op jit(solution)/shard_map/project/pallas_call | solution.py:376
  173.6 1.6 collective-permute-done.24.refs_9_
  175.3 5.3 %finish.1 = (bf16[3,96,3072]{2,1,0:T(8,128)(2,1)}, f32[2,64,96]{2,1,0:T(8,128)}) custom-call(s32[1]{0:T(128)} %bitcast.tile_ref, s32[16]{0:T(128)S(1)} %copy-done.25, f32[1]{0:T(128)S(6)} %copy.27.step_ref, bf16[288,384]{1,0:T(8,128)(2,1)S(1)} %project.11.refs_0_, bf16[288,384]{1,0:T(8,128)(2,1)S(1)} %copy-done.16, bf16[288,768]{1,0:T(8,128)(2,1)S(1)} %copy-done.5, ...), custom_call_target="tpu_custom_call" | custom-call | flops 141557760 | bytes 8847360 | tf_op jit(solution)/shard_map/finish/pallas_call | solution.py:444
  (59 shorter events, 0.1 us)
Async XLA Ops:
  3.4 41.9 %collective-permute-start.2 = (bf16[192,4608]{1,0:T(8,128)(2,1)}, bf16[192,4608]{1,0:T(8,128)(2,1)}, u32[]{:S(2)}, u32[]{:S(2)}) collective-permute-start(bf16[192,4608]{1,0:T(8,128)(2,1)} %pad_maximum_fusion.refs_0_), channel_id=1, source_target_pairs={{0,4},{2,6},{4,12},{6,14},{12,20},{14,22},{20,28},{22,30},{28,24},... | collective-permute-start | bytes 5308424 | tf_op jit(solution)/shard_map/ppermute | solution.py:481
  6.4 40.4 %collective-permute-start.3 = (bf16[192,4608]{1,0:T(8,128)(2,1)}, bf16[192,4608]{1,0:T(8,128)(2,1)}, u32[]{:S(2)}, u32[]{:S(2)}) collective-permute-start(bf16[192,4608]{1,0:T(8,128)(2,1)} %pad_maximum_fusion.refs_0_), channel_id=1, source_target_pairs={{0,8},{2,10},{4,0},{6,2},{12,4},{14,6},{20,12},{22,14},{28,20},{30... | collective-permute-start | bytes 5308424 | tf_op jit(solution)/shard_map/ppermute | solution.py:481
  6.4 40.3 %collective-permute-start.4 = (bf16[192,4608]{1,0:T(8,128)(2,1)}, bf16[192,4608]{1,0:T(8,128)(2,1)}, u32[]{:S(2)}, u32[]{:S(2)}) collective-permute-start(bf16[192,4608]{1,0:T(8,128)(2,1)} %pad_maximum_fusion.refs_0_), channel_id=1, source_target_pairs={{0,2},{2,0},{4,6},{6,4},{8,10},{10,8},{12,14},{14,12},{16,18},{18,... | collective-permute-start | bytes 5308424 | tf_op jit(solution)/shard_map/ppermute | solution.py:485
  8.7 40.1 %collective-permute-start = (bf16[3,1,96,1536]{3,2,0,1:T(8,128)(2,1)}, bf16[3,1,96,1536]{3,2,0,1:T(8,128)(2,1)}, u32[]{:S(2)}, u32[]{:S(2)}) collective-permute-start(bf16[3,1,96,1536]{3,2,0,1:T(8,128)(2,1)} %dynamic-slice_bitcast_fusion.2), channel_id=1, source_target_pairs={{0,1},{1,0},{2,3},{3,2},{4,5},{5,4},{6,7},{7,6},{8,9},{9,8},{10,11... | collective-permute-start | bytes 2654216 | tf_op jit(solution)/shard_map/ppermute | solution.py:527
  13.5 55.7 %collective-permute-start.1 = (bf16[3,2,96,1536]{3,2,1,0:T(8,128)(2,1)}, bf16[3,2,96,1536]{3,2,1,0:T(8,128)(2,1)}, u32[]{:S(2)}, u32[]{:S(2)}) collective-permute-start(bf16[3,2,96,1536]{3,2,1,0:T(8,128)(2,1)} %dynamic-slice_bitcast_fusion.1), channel_id=1, source_target_pairs={{0,1},{1,0},{2,3},{3,2},{4,5},{5,4},{6,7},{7,6},{8,9},{9,8},{10,11... | collective-permute-start | bytes 5308424 | tf_op jit(solution)/shard_map/ppermute | solution.py:527
  17.5 2.0 %copy-start.2 = (bf16[1,3,96,6144]{3,2,1,0:T(8,128)(2,1)S(1)}, bf16[1,3,96,6144]{3,2,1,0:T(8,128)(2,1)}, u32[]{:S(2)}) copy-start(bf16[1,3,96,6144]{3,2,1,0:T(8,128)(2,1)} %param.20) | copy-start | bytes 10616836
  46.7 39.5 %collective-permute-start.5 = (bf16[192,4608]{1,0:T(8,128)(2,1)}, bf16[192,4608]{1,0:T(8,128)(2,1)}, u32[]{:S(2)}, u32[]{:S(2)}) collective-permute-start(bf16[192,4608]{1,0:T(8,128)(2,1)} %collective-permute-done.2.refs_0_), channel_id=1, source_target_pairs={{0,4},{2,6},{4,12},{6,14},{12,20},{14,22},{20,28},{22,30},{28,24},... | collective-permute-start | bytes 5308424 | tf_op jit(solution)/shard_map/ppermute | solution.py:481
  48.3 41.3 %collective-permute-start.7 = (bf16[192,4608]{1,0:T(8,128)(2,1)}, bf16[192,4608]{1,0:T(8,128)(2,1)}, u32[]{:S(2)}, u32[]{:S(2)}) collective-permute-start(bf16[192,4608]{1,0:T(8,128)(2,1)} %collective-permute-done.2.refs_0_), channel_id=1, source_target_pairs={{0,2},{2,0},{4,6},{6,4},{8,10},{10,8},{12,14},{14,12},{16,18},{18,... | collective-permute-start | bytes 5308424 | tf_op jit(solution)/shard_map/ppermute | solution.py:485
  48.3 41.3 %collective-permute-start.6 = (bf16[192,4608]{1,0:T(8,128)(2,1)}, bf16[192,4608]{1,0:T(8,128)(2,1)}, u32[]{:S(2)}, u32[]{:S(2)}) collective-permute-start(bf16[192,4608]{1,0:T(8,128)(2,1)} %collective-permute-done.3.refs_2_), channel_id=1, source_target_pairs={{0,8},{2,10},{4,0},{6,2},{12,4},{14,6},{20,12},{22,14},{28,20},{30... | collective-permute-start | bytes 5308424 | tf_op jit(solution)/shard_map/ppermute | solution.py:481
  48.8 40.9 %collective-permute-start.8 = (bf16[192,4608]{1,0:T(8,128)(2,1)}, bf16[192,4608]{1,0:T(8,128)(2,1)}, u32[]{:S(2)}, u32[]{:S(2)}) collective-permute-start(bf16[192,4608]{1,0:T(8,128)(2,1)} %collective-permute-done.3.refs_2_), channel_id=1, source_target_pairs={{0,2},{2,0},{4,6},{6,4},{8,10},{10,8},{12,14},{14,12},{16,18},{18,... | collective-permute-start | bytes 5308424 | tf_op jit(solution)/shard_map/ppermute | solution.py:485
  69.2 40.7 %collective-permute-start.11 = (bf16[3,96,3072]{2,1,0:T(8,128)(2,1)}, bf16[3,96,3072]{2,1,0:T(8,128)(2,1)}, u32[]{:S(2)}, u32[]{:S(2)}) collective-permute-start(bf16[3,96,3072]{2,1,0:T(8,128)(2,1)} %dynamic-slice_bitcast_fusion), channel_id=1, source_target_pairs={{0,1},{1,0},{2,3},{3,2},{4,5},{5,4},{6,7},{7,6},{8,9},{9,8},{10,11... | collective-permute-start | bytes 5308424 | tf_op jit(solution)/shard_map/ppermute | solution.py:542
  89.7 40.6 %collective-permute-start.10 = (bf16[192,4608]{1,0:T(8,128)(2,1)}, bf16[192,4608]{1,0:T(8,128)(2,1)}, u32[]{:S(2)}, u32[]{:S(2)}) collective-permute-start(bf16[192,4608]{1,0:T(8,128)(2,1)} %collective-permute-done.6.refs_2_), channel_id=1, source_target_pairs={{0,8},{2,10},{4,0},{6,2},{12,4},{14,6},{20,12},{22,14},{28,20},{30... | collective-permute-start | bytes 5308424 | tf_op jit(solution)/shard_map/ppermute | solution.py:481
  90.1 40.3 %collective-permute-start.9 = (bf16[192,4608]{1,0:T(8,128)(2,1)}, bf16[192,4608]{1,0:T(8,128)(2,1)}, u32[]{:S(2)}, u32[]{:S(2)}) collective-permute-start(bf16[192,4608]{1,0:T(8,128)(2,1)} %collective-permute-done.5.refs_0_), channel_id=1, source_target_pairs={{0,4},{2,6},{4,12},{6,14},{12,20},{14,22},{20,28},{22,30},{28,24},... | collective-permute-start | bytes 5308424 | tf_op jit(solution)/shard_map/ppermute | solution.py:481
  91.7 43.2 %collective-permute-start.15 = (bf16[192,4608]{1,0:T(8,128)(2,1)}, bf16[192,4608]{1,0:T(8,128)(2,1)}, u32[]{:S(2)}, u32[]{:S(2)}) collective-permute-start(bf16[192,4608]{1,0:T(8,128)(2,1)} %collective-permute-done.5.refs_0_), channel_id=1, source_target_pairs={{0,2},{2,0},{4,6},{6,4},{8,10},{10,8},{12,14},{14,12},{16,18},{18,... | collective-permute-start | bytes 5308424 | tf_op jit(solution)/shard_map/ppermute | solution.py:485
  91.7 44.8 %collective-permute-start.16 = (bf16[192,4608]{1,0:T(8,128)(2,1)}, bf16[192,4608]{1,0:T(8,128)(2,1)}, u32[]{:S(2)}, u32[]{:S(2)}) collective-permute-start(bf16[192,4608]{1,0:T(8,128)(2,1)} %collective-permute-done.6.refs_2_), channel_id=1, source_target_pairs={{0,2},{2,0},{4,6},{6,4},{8,10},{10,8},{12,14},{14,12},{16,18},{18,... | collective-permute-start | bytes 5308424 | tf_op jit(solution)/shard_map/ppermute | solution.py:485
  101.6 11.3 %copy-start = (bf16[576,1536]{1,0:T(8,128)(2,1)S(1)}, bf16[576,1536]{1,0:T(8,128)(2,1)}, u32[]{:S(2)}) copy-start(bf16[576,1536]{1,0:T(8,128)(2,1)} %attend.3.attn_ref) | copy-start | bytes 5308420
  116.5 8.2 %collective-permute-start.12 = (bf16[288,384]{1,0:T(8,128)(2,1)S(1)}, bf16[288,384]{1,0:T(8,128)(2,1)S(1)}, u32[]{:S(2)}, u32[]{:S(2)}) collective-permute-start(bf16[288,384]{1,0:T(8,128)(2,1)S(1)} %project.6), channel_id=1, source_target_pairs={{0,1},{1,0},{2,3},{3,2},{4,5},{5,4},{6,7},{7,6},{8,9},{9,8},{10,11... | collective-permute-start | bytes 663560 | tf_op jit(solution)/shard_map/ppermute | solution.py:561
  124.7 10.2 %copy-start.4 = (bf16[288,768]{1,0:T(8,128)(2,1)}, bf16[288,768]{1,0:T(8,128)(2,1)S(1)}, u32[]{:S(2)}) copy-start(bf16[288,768]{1,0:T(8,128)(2,1)S(1)} %get-tuple-element.102.refs_2_) | copy-start | bytes 1327108
  124.7 0.7 copy-start.15
  130.4 14.4 %collective-permute-start.18 = (bf16[192,4608]{1,0:T(8,128)(2,1)}, bf16[192,4608]{1,0:T(8,128)(2,1)S(1)}, u32[]{:S(2)}, u32[]{:S(2)}) collective-permute-start(bf16[192,4608]{1,0:T(8,128)(2,1)} %collective-permute-done.9.refs_0_), channel_id=1, source_target_pairs={{0,2},{2,0},{4,6},{6,4},{8,10},{10,8},{12,14},{14,12},{16,18},{18,... | collective-permute-start | bytes 5308424 | tf_op jit(solution)/shard_map/ppermute | solution.py:485
  130.4 14.4 %collective-permute-start.19 = (bf16[192,4608]{1,0:T(8,128)(2,1)}, bf16[192,4608]{1,0:T(8,128)(2,1)S(1)}, u32[]{:S(2)}, u32[]{:S(2)}) collective-permute-start(bf16[192,4608]{1,0:T(8,128)(2,1)} %collective-permute-done.10.refs_2_), channel_id=1, source_target_pairs={{0,2},{2,0},{4,6},{6,4},{8,10},{10,8},{12,14},{14,12},{16,18},{18,... | collective-permute-start | bytes 5308424 | tf_op jit(solution)/shard_map/ppermute | solution.py:485
  130.9 13.4 %collective-permute-start.17 = (bf16[288,768]{1,0:T(8,128)(2,1)S(1)}, bf16[288,768]{1,0:T(8,128)(2,1)S(1)}, u32[]{:S(2)}, u32[]{:S(2)}) collective-permute-start(bf16[288,768]{1,0:T(8,128)(2,1)S(1)} %get-tuple-element.87), channel_id=1, source_target_pairs={{0,1},{1,0},{2,3},{3,2},{4,5},{5,4},{6,7},{7,6},{8,9},{9,8},{10,11... | collective-permute-start | bytes 1327112 | tf_op jit(solution)/shard_map/ppermute | solution.py:557
  134.9 21.3 %collective-permute-start.13 = (bf16[96,4608]{1,0:T(8,128)(2,1)S(1)}, bf16[96,4608]{1,0:T(8,128)(2,1)S(1)}, u32[]{:S(2)}, u32[]{:S(2)}) collective-permute-start(bf16[96,4608]{1,0:T(8,128)(2,1)S(1)} %slice.6), channel_id=1, source_target_pairs={{0,4},{2,6},{4,12},{6,14},{12,20},{14,22},{20,28},{22,30},{28,24},... | collective-permute-start | bytes 2654216 | tf_op jit(solution)/shard_map/ppermute | solution.py:481
  136.5 21.0 %collective-permute-start.14 = (bf16[96,4608]{1,0:T(8,128)(2,1)S(1)}, bf16[96,4608]{1,0:T(8,128)(2,1)S(1)}, u32[]{:S(2)}, u32[]{:S(2)}) collective-permute-start(bf16[96,4608]{1,0:T(8,128)(2,1)S(1)} %slice.7), channel_id=1, source_target_pairs={{0,8},{2,10},{4,0},{6,2},{12,4},{14,6},{20,12},{22,14},{28,20},{30... | collective-permute-start | bytes 2654216 | tf_op jit(solution)/shard_map/ppermute | solution.py:481
  143.5 0.8 copy-start.8
  144.3 7.3 %copy-start.6 = (bf16[288,768]{1,0:T(8,128)(2,1)}, bf16[288,768]{1,0:T(8,128)(2,1)S(1)}, u32[]{:S(2)}) copy-start(bf16[288,768]{1,0:T(8,128)(2,1)S(1)} %collective-permute-done.17.refs_3_) | copy-start | bytes 1327108
  144.3 11.2 %collective-permute-start.20 = (bf16[288,768]{1,0:T(8,128)(2,1)S(1)}, bf16[288,768]{1,0:T(8,128)(2,1)S(1)}, u32[]{:S(2)}, u32[]{:S(2)}) collective-permute-start(bf16[288,768]{1,0:T(8,128)(2,1)S(1)} %get-tuple-element.91), channel_id=1, source_target_pairs={{0,1},{1,0},{2,3},{3,2},{4,5},{5,4},{6,7},{7,6},{8,9},{9,8},{10,11... | collective-permute-start | bytes 1327112 | tf_op jit(solution)/shard_map/ppermute | solution.py:557
  151.6 14.0 %copy-start.12 = (bf16[288,768]{1,0:T(8,128)(2,1)}, bf16[288,768]{1,0:T(8,128)(2,1)S(1)}, u32[]{:S(2)}) copy-start(bf16[288,768]{1,0:T(8,128)(2,1)S(1)} %get-tuple-element.106.refs_6_) | copy-start | bytes 1327108
  155.5 10.1 %copy-start.10 = (bf16[288,768]{1,0:T(8,128)(2,1)}, bf16[288,768]{1,0:T(8,128)(2,1)S(1)}, u32[]{:S(2)}) copy-start(bf16[288,768]{1,0:T(8,128)(2,1)S(1)} %collective-permute-done.20.refs_5_) | copy-start | bytes 1327108
  157.5 9.3 %copy-start.26 = (f32[64]{0:T(128)S(1)}, f32[64]{0:T(128)}, u32[]{:S(2)}) copy-start(f32[64]{0:T(128)} %param.32) | copy-start | bytes 772
  157.5 2.4 %collective-permute-start.21 = (bf16[96,4608]{1,0:T(8,128)(2,1)S(1)}, bf16[96,4608]{1,0:T(8,128)(2,1)S(1)}, u32[]{:S(2)}, u32[]{:S(2)}) collective-permute-start(bf16[96,4608]{1,0:T(8,128)(2,1)S(1)} %collective-permute-done.13.refs_0_), channel_id=1, source_target_pairs={{0,2},{2,0},{4,6},{6,4},{8,10},{10,8},{12,14},{14,12},{16,18},{18,... | collective-permute-start | bytes 2654216 | tf_op jit(solution)/shard_map/ppermute | solution.py:485
  157.5 3.7 %collective-permute-start.22 = (bf16[96,4608]{1,0:T(8,128)(2,1)S(1)}, bf16[96,4608]{1,0:T(8,128)(2,1)S(1)}, u32[]{:S(2)}, u32[]{:S(2)}) collective-permute-start(bf16[96,4608]{1,0:T(8,128)(2,1)S(1)} %collective-permute-done.14.refs_2_), channel_id=1, source_target_pairs={{0,2},{2,0},{4,6},{6,4},{8,10},{10,8},{12,14},{14,12},{16,18},{18,... | collective-permute-start | bytes 2654216 | tf_op jit(solution)/shard_map/ppermute | solution.py:485
  158.0 15.5 %collective-permute-start.23 = (bf16[288,768]{1,0:T(8,128)(2,1)}, bf16[288,768]{1,0:T(8,128)(2,1)}, u32[]{:S(2)}, u32[]{:S(2)}) collective-permute-start(bf16[288,768]{1,0:T(8,128)(2,1)} %get-tuple-element.94), channel_id=1, source_target_pairs={{0,1},{1,0},{2,3},{3,2},{4,5},{5,4},{6,7},{7,6},{8,9},{9,8},{10,11... | collective-permute-start | bytes 1327112 | tf_op jit(solution)/shard_map/ppermute | solution.py:557
  165.6 0.7 copy-start.17
  166.3 8.9 %collective-permute-start.24 = (bf16[288,384]{1,0:T(8,128)(2,1)}, bf16[288,384]{1,0:T(8,128)(2,1)}, u32[]{:S(2)}, u32[]{:S(2)}) collective-permute-start(bf16[288,384]{1,0:T(8,128)(2,1)} %get-tuple-element.99), channel_id=1, source_target_pairs={{0,1},{1,0},{2,3},{3,2},{4,5},{5,4},{6,7},{7,6},{8,9},{9,8},{10,11... | collective-permute-start | bytes 663560 | tf_op jit(solution)/shard_map/ppermute | solution.py:557
  168.2 1.5 copy-start.1
  169.7 5.5 %copy-start.3 = (bf16[1,3,96,3072]{3,2,1,0:T(8,128)(2,1)S(1)}, bf16[1,3,96,3072]{3,2,1,0:T(8,128)(2,1)}, u32[]{:S(2)}) copy-start(bf16[1,3,96,3072]{3,2,1,0:T(8,128)(2,1)} %param.21) | copy-start | bytes 5308420
  169.7 5.5 %copy-start.5 = (bf16[288,768]{1,0:T(8,128)(2,1)S(1)}, bf16[288,768]{1,0:T(8,128)(2,1)}, u32[]{:S(2)}) copy-start(bf16[288,768]{1,0:T(8,128)(2,1)} %copy-done.4) | copy-start | bytes 1327108
  169.7 5.5 %copy-start.7 = (bf16[288,768]{1,0:T(8,128)(2,1)S(1)}, bf16[288,768]{1,0:T(8,128)(2,1)}, u32[]{:S(2)}) copy-start(bf16[288,768]{1,0:T(8,128)(2,1)} %copy-done.6) | copy-start | bytes 1327108
  169.7 5.5 %copy-start.9 = (bf16[288,768]{1,0:T(8,128)(2,1)S(1)}, bf16[288,768]{1,0:T(8,128)(2,1)}, u32[]{:S(2)}) copy-start(bf16[288,768]{1,0:T(8,128)(2,1)} %copy-done.8) | copy-start | bytes 1327108
  169.7 5.5 %copy-start.11 = (bf16[288,768]{1,0:T(8,128)(2,1)S(1)}, bf16[288,768]{1,0:T(8,128)(2,1)}, u32[]{:S(2)}) copy-start(bf16[288,768]{1,0:T(8,128)(2,1)} %copy-done.10) | copy-start | bytes 1327108
  169.7 5.5 %copy-start.13 = (bf16[288,768]{1,0:T(8,128)(2,1)S(1)}, bf16[288,768]{1,0:T(8,128)(2,1)}, u32[]{:S(2)}) copy-start(bf16[288,768]{1,0:T(8,128)(2,1)} %copy-done.12) | copy-start | bytes 1327108
  169.7 5.5 %copy-start.14 = (bf16[3072,64]{0,1:T(8,128)(2,1)S(1)}, bf16[3072,64]{0,1:T(8,128)(2,1)}, u32[]{:S(2)}) copy-start(bf16[3072,64]{0,1:T(8,128)(2,1)} %param.31) | copy-start | bytes 1179652
  169.7 5.5 %copy-start.16 = (bf16[288,384]{1,0:T(8,128)(2,1)S(1)}, bf16[288,384]{1,0:T(8,128)(2,1)}, u32[]{:S(2)}) copy-start(bf16[288,384]{1,0:T(8,128)(2,1)} %copy-done.15) | copy-start | bytes 663556
  169.7 5.5 %copy-start.18 = (bf16[288,384]{1,0:T(8,128)(2,1)S(1)}, bf16[288,384]{1,0:T(8,128)(2,1)}, u32[]{:S(2)}) copy-start(bf16[288,384]{1,0:T(8,128)(2,1)} %copy-done.17) | copy-start | bytes 663556
  169.7 5.5 %copy-start.19 = (f32[64,1]{1,0:T(8,128)S(1)}, f32[64,1]{1,0:T(8,128)}, u32[]{:S(2)}) copy-start(f32[64,1]{1,0:T(8,128)} %copy.23.refs_16_) | copy-start | bytes 772
  169.7 5.5 %copy-start.20 = (f32[1,2,96,64]{2,3,1,0:T(8,128)S(1)}, f32[1,2,96,64]{2,3,1,0:T(8,128)}, u32[]{:S(2)}) copy-start(f32[1,2,96,64]{2,3,1,0:T(8,128)} %param.33) | copy-start | bytes 147460
  169.7 5.5 %copy-start.21 = (f32[3072]{0:T(1024)S(1)}, f32[3072]{0:T(1024)}, u32[]{:S(2)}) copy-start(f32[3072]{0:T(1024)} %param.27) | copy-start | bytes 36868
  169.8 5.5 %copy-start.22 = (f32[1,3072]{1,0:T(1,128)S(1)}, f32[1,3072]{1,0:T(1,128)}, u32[]{:S(2)}) copy-start(f32[1,3072]{1,0:T(1,128)} %refs_12_.1) | copy-start | bytes 36868
  169.8 5.5 %copy-start.23 = (f32[1,3072]{1,0:T(1,128)S(1)}, f32[1,3072]{1,0:T(1,128)}, u32[]{:S(2)}) copy-start(f32[1,3072]{1,0:T(1,128)} %refs_13_.1) | copy-start | bytes 36868
  169.8 5.5 %copy-start.24 = (f32[1,3072]{1,0:T(1,128)S(1)}, f32[1,3072]{1,0:T(1,128)}, u32[]{:S(2)}) copy-start(f32[1,3072]{1,0:T(1,128)} %refs_14_.1) | copy-start | bytes 36868
  169.8 5.5 %copy-start.25 = (s32[16]{0:T(128)S(1)}, s32[16]{0:T(128)}, u32[]{:S(2)}) copy-start(s32[16]{0:T(128)} %constant.42.clone.place_ref) | copy-start | bytes 196

commit v6 on v4

--- a/solution.py
+++ b/solution.py
@@ -563,11 +563,15 @@
     sent = send(chips[3:5])
     attn, sent, chunks[1] = lax.optimization_barrier((attn, sent, chunks[1]))
     sent = send(chips[5:7])
+    attn, sent = lax.optimization_barrier((attn, sent))
+    (chunks[0][0],) = project(core, attn, act, chips[0:1], (0,))
+    attn, chunks[0] = lax.optimization_barrier((attn, chunks[0]))
     onward, back, attn, sent, chunks[2] = lax.optimization_barrier((*last, attn, sent, chunks[2]))
     chips.append(both_cores(onward) + both_cores(back, middle))
-    sent = send(chips[7:8])
+    (sent,) = project(core, attn, act, chips[7:8], (1,))
+    far = trade(sent)
     attn, sent = lax.optimization_barrier((attn, sent))
-    (chunks[0][0],) = project(core, attn, act, chips[0:1], (0,))
+    chunks.append([project(core, attn, act, chips[7:8], (0,))[0], far])
 
     hidden, following = finish(
         tile[None],

time: 178 us -> 178 us (level)
  waiting for transfers between devices: 75.7 us -> 69.5 us
  local copies, waits for them, and re-layouts: 13.8 us -> 18.6 us
    ppermute x4 -> x3, waiting for transfers between devices: 5.56 us -> 0.01 us  [send(): chunks.append((own, trade(sent)))]
    unnamed x54 -> x70, local copies, waits for them, and re-layouts: 5.73 us -> 10.5 us
    pallas_call x6 -> x7, Pallas kernels: 31.5 us -> 32.3 us  [project(): pl.pallas_call(functools.partial(project_kernel, layout, sides), in_specs...]
  transfers between devices with their start and end apart: 24 -> 24, of which waited for: 13 -> 11; matrix products, arithmetic and copies ran while one was open for 5% -> 5% of each run, Pallas kernels for 33% -> 33%
where the time goes in v6:
time: 178 us; the launch traced here: 177 us
  waiting for transfers between devices  69.5 us (39%)
  Pallas kernels  63.9 us (36%)
  starting transfers between devices  20.2 us (11%)
  local copies, waits for them, and re-layouts  18.6 us (10%)
  other arithmetic  2.79 us (2%)
  between operations  2.42 us (1%)
    ppermute x8, waiting for transfers between devices, hop(): return lax.ppermute(array, 'tile', pairs)  34 us
    pallas_call x7, Pallas kernels, project(): pl.pallas_call(functools.partial(project_kernel, layout, sides), in_specs...  32.3 us
    ppermute x1, waiting for transfers between devices, paired(): far_attn = trade(sent_attn)  21.2 us
    pallas_call x2, Pallas kernels, attend(): pl.pallas_call(attend_kernel, grid_spec=pltpu.PrefetchScalarGridSpec(num_...  18.5 us
    ppermute x1, waiting for transfers between devices, paired(): far_units = trade(sent_units)  11.8 us
    unnamed x70, local copies, waits for them, and re-layouts  10.5 us
    ppermute x8, starting transfers between devices, hop(): return lax.ppermute(array, 'tile', pairs)  9.16 us
    pallas_call x1, Pallas kernels, finish(): pl.pallas_call(functools.partial(finish_kernel, len(chunks)), grid_spec=p...  5.34 us
  transfers between devices with their start and end apart: 24, of which 11 were waited for; matrix products, arithmetic and copies ran while one was open for 5% of the time, Pallas kernels for 33%

profile of v6, /device:TPU:0, one launch (start us, length us, event | category | flops | bytes accessed | tf_op | source)
XLA Modules:
  0.0 177.4 jit_solution(15701612613150159975)
XLA Ops:
  0.6 2.8 %pad_maximum_fusion.refs_0_ = bf16[192,4608]{1,0:T(8,128)(2,1)} fusion(bf16[192,3072]{1,0:T(8,128)(2,1)} %bitcast.35, bf16[192,1536]{1,0:T(8,128)(2,1)} %bitcast.36), kind=kLoop, calls=%fused_computation.1 | loop fusion | flops 3538944 | bytes 3538944 | tf_op jit(solution)/shard_map/concatenate | solution.py:520
  3.4 2.9 %collective-permute-start.1 = (bf16[192,4608]{1,0:T(8,128)(2,1)}, bf16[192,4608]{1,0:T(8,128)(2,1)}, u32[]{:S(2)}, u32[]{:S(2)}) collective-permute-start(bf16[192,4608]{1,0:T(8,128)(2,1)} %pad_maximum_fusion.refs_0_), channel_id=1, source_target_pairs={{0,4},{2,6},{4,12},{6,14},{12,20},{14,22},{20,28},{22,30},{28,24},... | collective-permute-start | bytes 5308424 | tf_op jit(solution)/shard_map/ppermute | solution.py:481
  6.4 0.1 collective-permute-start.2
  6.4 3.5 %dynamic-slice_bitcast_fusion = bf16[3,3,96,1536]{3,2,1,0:T(8,128)(2,1)} fusion(bf16[1,3,96,3,3072]{4,2,3,1,0:T(8,128)(2,1)} %param.19, s32[]{:T(128)S(6)} %select_n.13), kind=kLoop, calls=%fused_computation | loop fusion | bytes 5308420 | tf_op jit(solution)/shard_map/dynamic_slice | solution.py:519
  10.0 2.0 %collective-permute-start = (bf16[3,3,96,1536]{3,2,1,0:T(8,128)(2,1)}, bf16[3,3,96,1536]{3,2,1,0:T(8,128)(2,1)}, u32[]{:S(2)}, u32[]{:S(2)}) collective-permute-start(bf16[3,3,96,1536]{3,2,1,0:T(8,128)(2,1)} %dynamic-slice_bitcast_fusion), channel_id=1, source_target_pairs={{0,1},{1,0},{2,3},{3,2},{4,5},{5,4},{6,7},{7,6},{8,9},{9,8},{10,11... | collective-permute-start | bytes 7962632 | tf_op jit(solution)/shard_map/ppermute | solution.py:523
  12.6 3.3 %tables.1 = (f32[576,128]{1,0:T(8,128)}, f32[576,128]{1,0:T(8,128)}, f32[576,128]{1,0:T(8,128)}, f32[576,128]{1,0:T(8,128)}, f32[1,576]{1,0:T(1,128)}, /*index=5*/bf16[128,128]{1,0:T(8,128)(2,1)}) custom-call(s32[1]{0:T(128)} %bitcast.1.half_ref.part_ref, s32[1]{0:T(128)S(6)} %copy.26.len_ref, f32[1,128]{1,0:T(1,128)} %constant.39.clone.row_freq_ref, ...), custom_call_target="tpu_custom_call" | custom-call | flops 589824 | bytes 294912 | tf_op jit(solution)/shard_map/tables/pallas_call | solution.py:229
  15.9 2.0 %copy-done.2 = bf16[1,3,96,6144]{3,2,1,0:T(8,128)(2,1)S(1)} copy-done((bf16[1,3,96,6144]{3,2,1,0:T(8,128)(2,1)S(1)}, bf16[1,3,96,6144]{3,2,1,0:T(8,128)(2,1)}, u32[]{:S(2)}) %copy-start.2) | copy-done | bytes 3538968
  17.9 1.4 activate.2.refs_0_
  19.3 1.5 dynamic-slice_bitcast_fusion.1
  20.7 24.6 %collective-permute-done.1.refs_0_ = bf16[192,4608]{1,0:T(8,128)(2,1)} collective-permute-done((bf16[192,4608]{1,0:T(8,128)(2,1)}, bf16[192,4608]{1,0:T(8,128)(2,1)}, u32[]{:S(2)}, u32[]{:S(2)}) %collective-permute-start.1) | collective-permute-done | bytes 1769504 | tf_op jit(solution)/shard_map/ppermute | solution.py:481
  45.4 1.4 collective-permute-done.2.refs_2_
  46.7 1.6 collective-permute-start.4
  48.3 0.4 collective-permute-start.5
  48.8 0.5 collective-permute-start.7
  49.3 21.2 %collective-permute-done.far_ref = bf16[3,3,96,1536]{3,2,1,0:T(8,128)(2,1)} collective-permute-done((bf16[3,3,96,1536]{3,2,1,0:T(8,128)(2,1)}, bf16[3,3,96,1536]{3,2,1,0:T(8,128)(2,1)}, u32[]{:S(2)}, u32[]{:S(2)}) %collective-permute-start) | collective-permute-done | bytes 2654240 | tf_op jit(solution)/shard_map/ppermute | solution.py:523
  70.5 1.7 collective-permute-start.10
  72.2 9.3 %attend.2.refs_0_ = bf16[576,1536]{1,0:T(8,128)(2,1)} custom-call(s32[1]{0:T(128)} %bitcast.1.half_ref.part_ref, bf16[3,3,96,3072]{3,2,1,0:T(8,128)(2,1)} %bitcast.33, bf16[3,3,96,1536]{3,2,1,0:T(8,128)(2,1)} %collective-permute-done.far_ref, f32[576,128]{1,0:T(8,128)} %get-tuple-element.65.cq_ref, f32[576,128]{1,0:T(8,128)} %get-tuple-element.66.sq_ref, ...), custom_call_target="tpu_custom_call" | custom-call | flops 1019215872 | bytes 7077888 | tf_op jit(solution)/shard_map/attend/pallas_call | solution.py:286
  81.5 4.7 %collective-permute-done.4.refs_0_ = bf16[192,4608]{1,0:T(8,128)(2,1)} collective-permute-done((bf16[192,4608]{1,0:T(8,128)(2,1)}, bf16[192,4608]{1,0:T(8,128)(2,1)}, u32[]{:S(2)}, u32[]{:S(2)}) %collective-permute-start.4) | collective-permute-done | bytes 1769504 | tf_op jit(solution)/shard_map/ppermute | solution.py:481
  86.2 1.3 collective-permute-done.5.refs_2_
  87.5 1.6 collective-permute-start.8
  89.1 0.4 collective-permute-start.9
  89.6 0.5 collective-permute-start.13
  90.1 9.3 %attend.3.attn_ref = bf16[576,1536]{1,0:T(8,128)(2,1)} custom-call(s32[1]{0:T(128)} %bitcast.1.half_ref.part_ref, bf16[3,3,96,3072]{3,2,1,0:T(8,128)(2,1)} %bitcast.34, bf16[3,3,96,1536]{3,2,1,0:T(8,128)(2,1)} %collective-permute-done.far_ref, f32[576,128]{1,0:T(8,128)} %get-tuple-element.65.cq_ref, ...), custom_call_target="tpu_custom_call", output_to_operand_aliasing={{}: (9, {})} | custom-call | flops 1019215872 | bytes 7077888 | tf_op jit(solution)/shard_map/attend/pallas_call | solution.py:286
  99.3 11.8 %collective-permute-done.10.units_ref = bf16[3,96,3072]{2,1,0:T(8,128)(2,1)} collective-permute-done((bf16[3,96,3072]{2,1,0:T(8,128)(2,1)}, bf16[3,96,3072]{2,1,0:T(8,128)(2,1)}, u32[]{:S(2)}, u32[]{:S(2)}) %collective-permute-start.10) | collective-permute-done | bytes 1769504 | tf_op jit(solution)/shard_map/ppermute | solution.py:537
  111.2 3.0 %activate.3.act_ref = bf16[576,3072]{1,0:T(8,128)(2,1)S(1)} custom-call(s32[1]{0:T(128)} %constant.38.clone.1.part_ref, bf16[3,96,3072]{2,1,0:T(8,128)(2,1)} %collective-permute-done.10.units_ref, bf16[576,3072]{1,0:T(8,128)(2,1)S(1)} %activate.2.refs_0_), custom_call_target="tpu_custom_call", output_to_operand_aliasing={{}: (2, {})} | custom-call | flops 3538944 | bytes 884736 | tf_op jit(solution)/shard_map/activate/pallas_call | solution.py:323
  114.2 3.6 %project.7 = bf16[288,384]{1,0:T(8,128)(2,1)S(1)} custom-call(s32[1]{0:T(128)} %bitcast.13.core_ref, bf16[576,1536]{1,0:T(8,128)(2,1)S(1)} %copy-done, bf16[576,3072]{1,0:T(8,128)(2,1)S(1)} %activate.3.act_ref, bf16[192,4608]{1,0:T(8,128)(2,1)} %pad_maximum_fusion.refs_0_, bf16[192,4608]{1,0:T(8,128)(2,1)} %collective-permute-done.3.refs_1_), custom_call_target="tpu_custom_call" | custom-call | flops 254803968 | bytes 442368 | tf_op jit(solution)/shard_map/project/pallas_call | solution.py:376
  117.8 1.7 collective-permute-start.11
  119.4 6.5 %project.8 = (bf16[288,768]{1,0:T(8,128)(2,1)S(1)}, bf16[288,768]{1,0:T(8,128)(2,1)S(1)}) custom-call(s32[1]{0:T(128)} %bitcast.13.core_ref, bf16[576,1536]{1,0:T(8,128)(2,1)S(1)} %copy-done, bf16[576,3072]{1,0:T(8,128)(2,1)S(1)} %activate.3.act_ref, bf16[192,4608]{1,0:T(8,128)(2,1)} %collective-permute-done.1.refs_0_, ...), custom_call_target="tpu_custom_call" | custom-call | flops 509607936 | bytes 884736 | tf_op jit(solution)/shard_map/project/pallas_call | solution.py:376
  126.0 1.1 collective-permute-done.9.refs_2_
  127.1 0.5 collective-permute-start.16
  127.6 1.5 collective-permute-start.14
  129.1 1.2 slice.6
  130.4 1.2 slice.7
  131.6 1.6 collective-permute-start.17
  133.2 0.5 collective-permute-start.18
  133.7 6.5 %project.9 = (bf16[288,768]{1,0:T(8,128)(2,1)S(1)}, bf16[288,768]{1,0:T(8,128)(2,1)S(1)}) custom-call(s32[1]{0:T(128)} %bitcast.13.core_ref, bf16[576,1536]{1,0:T(8,128)(2,1)S(1)} %copy-done, bf16[576,3072]{1,0:T(8,128)(2,1)S(1)} %activate.3.act_ref, bf16[192,4608]{1,0:T(8,128)(2,1)} %collective-permute-done.4.refs_0_, ...), custom_call_target="tpu_custom_call" | custom-call | flops 509607936 | bytes 884736 | tf_op jit(solution)/shard_map/project/pallas_call | solution.py:376
  140.3 0.8 copy-done.18
  141.0 0.5 collective-permute-start.19
  141.5 6.8 %project.10 = (bf16[288,768]{1,0:T(8,128)(2,1)S(1)}, bf16[288,768]{1,0:T(8,128)(2,1)}) custom-call(s32[1]{0:T(128)} %bitcast.13.core_ref, bf16[576,1536]{1,0:T(8,128)(2,1)S(1)} %copy-done, bf16[576,3072]{1,0:T(8,128)(2,1)S(1)} %activate.3.act_ref, bf16[192,4608]{1,0:T(8,128)(2,1)} %collective-permute-done.8.refs_0_, ...), custom_call_target="tpu_custom_call" | custom-call | flops 509607936 | bytes 884736 | tf_op jit(solution)/shard_map/project/pallas_call | solution.py:376
  148.3 0.8 copy-done.22
  149.1 3.6 %project.11.refs_0_ = bf16[288,384]{1,0:T(8,128)(2,1)S(1)} custom-call(s32[1]{0:T(128)} %bitcast.13.core_ref, bf16[576,1536]{1,0:T(8,128)(2,1)S(1)} %copy-done, bf16[576,3072]{1,0:T(8,128)(2,1)S(1)} %activate.3.act_ref, bf16[192,4608]{1,0:T(8,128)(2,1)} %pad_maximum_fusion.refs_0_, bf16[192,4608]{1,0:T(8,128)(2,1)} %collective-permute-done.3.refs_1_), custom_call_target="tpu_custom_call" | custom-call | flops 254803968 | bytes 442368 | tf_op jit(solution)/shard_map/project/pallas_call | solution.py:376
  152.7 0.7 copy-done.12
  153.4 0.8 collective-permute-done.18.refs_2_
  154.2 0.5 collective-permute-start.22
  154.8 0.8 collective-permute-start.20
  155.5 1.1 collective-permute-done.21.refs_1_
  156.7 1.3 collective-permute-done.22.refs_3_
  157.9 3.0 %project.12 = bf16[288,384]{1,0:T(8,128)(2,1)} custom-call(s32[1]{0:T(128)} %bitcast.13.core_ref, bf16[576,1536]{1,0:T(8,128)(2,1)S(1)} %copy-done, bf16[576,3072]{1,0:T(8,128)(2,1)S(1)} %activate.3.act_ref, bf16[96,4608]{1,0:T(8,128)(2,1)S(1)} %collective-permute-done.17.refs_0_, bf16[96,4608]{1,0:T(8,128)(2,1)S(1)} %collective-permute-done.21.refs_1_, ...), custom_call_target="tpu_custom_call" | custom-call | flops 254803968 | bytes 442368 | tf_op jit(solution)/shard_map/project/pallas_call | solution.py:376
  161.0 0.8 collective-permute-start.23
  161.8 0.7 copy.23.refs_16_
  163.2 0.0 copy-start.1
  163.2 1.5 copy-done.1
  164.7 1.2 copy-done.4
  165.9 1.2 copy-done.6
  167.0 1.2 copy-done.8
  168.2 1.2 copy-done.10
  169.4 0.0 copy-start.24
  169.4 0.0 copy-start.29
  169.5 0.0 copy-start.30
  169.5 0.0 copy-start.32
  169.5 0.0 copy-start.33
  169.5 2.3 %project.13.refs_8_ = bf16[288,384]{1,0:T(8,128)(2,1)S(1)} custom-call(s32[1]{0:T(128)} %bitcast.13.core_ref, bf16[576,1536]{1,0:T(8,128)(2,1)S(1)} %copy-done.1, bf16[576,3072]{1,0:T(8,128)(2,1)S(1)} %activate.3.act_ref, bf16[96,4608]{1,0:T(8,128)(2,1)S(1)} %copy-done.4, bf16[96,4608]{1,0:T(8,128)(2,1)S(1)} %copy-done.8, bf16[96,4608]{1,0:T(8,128)(2,1)S(1)} %copy-done.6, ...), custom_call_target="tpu_custom_call" | custom-call | flops 254803968 | bytes 442368 | tf_op jit(solution)/shard_map/project/pallas_call | solution.py:376
  171.9 0.1 collective-permute-done.23.refs_9_
  172.1 5.3 %finish.1 = (bf16[3,96,3072]{2,1,0:T(8,128)(2,1)}, f32[2,64,96]{2,1,0:T(8,128)}) custom-call(s32[1]{0:T(128)} %bitcast.tile_ref, s32[16]{0:T(128)S(1)} %copy-done.33, f32[1]{0:T(128)S(6)} %copy.27.step_ref, bf16[288,384]{1,0:T(8,128)(2,1)S(1)} %copy-done.13, bf16[288,384]{1,0:T(8,128)(2,1)S(1)} %copy-done.26, bf16[288,768]{1,0:T(8,128)(2,1)S(1)} %copy-done.15, ...), custom_call_target="tpu_custom_call" | custom-call | flops 141557760 | bytes 8847360 | tf_op jit(solution)/shard_map/finish/pallas_call | solution.py:444
  (73 shorter events, 0.2 us)
Async XLA Ops:
  3.4 41.9 %collective-permute-start.1 = (bf16[192,4608]{1,0:T(8,128)(2,1)}, bf16[192,4608]{1,0:T(8,128)(2,1)}, u32[]{:S(2)}, u32[]{:S(2)}) collective-permute-start(bf16[192,4608]{1,0:T(8,128)(2,1)} %pad_maximum_fusion.refs_0_), channel_id=1, source_target_pairs={{0,4},{2,6},{4,12},{6,14},{12,20},{14,22},{20,28},{22,30},{28,24},... | collective-permute-start | bytes 5308424 | tf_op jit(solution)/shard_map/ppermute | solution.py:481
  6.4 40.4 %collective-permute-start.2 = (bf16[192,4608]{1,0:T(8,128)(2,1)}, bf16[192,4608]{1,0:T(8,128)(2,1)}, u32[]{:S(2)}, u32[]{:S(2)}) collective-permute-start(bf16[192,4608]{1,0:T(8,128)(2,1)} %pad_maximum_fusion.refs_0_), channel_id=1, source_target_pairs={{0,8},{2,10},{4,0},{6,2},{12,4},{14,6},{20,12},{22,14},{28,20},{30... | collective-permute-start | bytes 5308424 | tf_op jit(solution)/shard_map/ppermute | solution.py:481
  6.4 40.3 %collective-permute-start.3 = (bf16[192,4608]{1,0:T(8,128)(2,1)}, bf16[192,4608]{1,0:T(8,128)(2,1)}, u32[]{:S(2)}, u32[]{:S(2)}) collective-permute-start(bf16[192,4608]{1,0:T(8,128)(2,1)} %pad_maximum_fusion.refs_0_), channel_id=1, source_target_pairs={{0,2},{2,0},{4,6},{6,4},{8,10},{10,8},{12,14},{14,12},{16,18},{18,... | collective-permute-start | bytes 5308424 | tf_op jit(solution)/shard_map/ppermute | solution.py:485
  10.0 60.5 %collective-permute-start = (bf16[3,3,96,1536]{3,2,1,0:T(8,128)(2,1)}, bf16[3,3,96,1536]{3,2,1,0:T(8,128)(2,1)}, u32[]{:S(2)}, u32[]{:S(2)}) collective-permute-start(bf16[3,3,96,1536]{3,2,1,0:T(8,128)(2,1)} %dynamic-slice_bitcast_fusion), channel_id=1, source_target_pairs={{0,1},{1,0},{2,3},{3,2},{4,5},{5,4},{6,7},{7,6},{8,9},{9,8},{10,11... | collective-permute-start | bytes 7962632 | tf_op jit(solution)/shard_map/ppermute | solution.py:523
  15.9 2.0 %copy-start.2 = (bf16[1,3,96,6144]{3,2,1,0:T(8,128)(2,1)S(1)}, bf16[1,3,96,6144]{3,2,1,0:T(8,128)(2,1)}, u32[]{:S(2)}) copy-start(bf16[1,3,96,6144]{3,2,1,0:T(8,128)(2,1)} %param.20) | copy-start | bytes 10616836
  46.7 39.5 %collective-permute-start.4 = (bf16[192,4608]{1,0:T(8,128)(2,1)}, bf16[192,4608]{1,0:T(8,128)(2,1)}, u32[]{:S(2)}, u32[]{:S(2)}) collective-permute-start(bf16[192,4608]{1,0:T(8,128)(2,1)} %collective-permute-done.1.refs_0_), channel_id=1, source_target_pairs={{0,4},{2,6},{4,12},{6,14},{12,20},{14,22},{20,28},{22,30},{28,24},... | collective-permute-start | bytes 5308424 | tf_op jit(solution)/shard_map/ppermute | solution.py:481
  48.3 39.2 %collective-permute-start.5 = (bf16[192,4608]{1,0:T(8,128)(2,1)}, bf16[192,4608]{1,0:T(8,128)(2,1)}, u32[]{:S(2)}, u32[]{:S(2)}) collective-permute-start(bf16[192,4608]{1,0:T(8,128)(2,1)} %collective-permute-done.2.refs_2_), channel_id=1, source_target_pairs={{0,8},{2,10},{4,0},{6,2},{12,4},{14,6},{20,12},{22,14},{28,20},{30... | collective-permute-start | bytes 5308424 | tf_op jit(solution)/shard_map/ppermute | solution.py:481
  48.8 38.7 %collective-permute-start.6 = (bf16[192,4608]{1,0:T(8,128)(2,1)}, bf16[192,4608]{1,0:T(8,128)(2,1)}, u32[]{:S(2)}, u32[]{:S(2)}) collective-permute-start(bf16[192,4608]{1,0:T(8,128)(2,1)} %collective-permute-done.1.refs_0_), channel_id=1, source_target_pairs={{0,2},{2,0},{4,6},{6,4},{8,10},{10,8},{12,14},{14,12},{16,18},{18,... | collective-permute-start | bytes 5308424 | tf_op jit(solution)/shard_map/ppermute | solution.py:485
  48.8 38.7 %collective-permute-start.7 = (bf16[192,4608]{1,0:T(8,128)(2,1)}, bf16[192,4608]{1,0:T(8,128)(2,1)}, u32[]{:S(2)}, u32[]{:S(2)}) collective-permute-start(bf16[192,4608]{1,0:T(8,128)(2,1)} %collective-permute-done.2.refs_2_), channel_id=1, source_target_pairs={{0,2},{2,0},{4,6},{6,4},{8,10},{10,8},{12,14},{14,12},{16,18},{18,... | collective-permute-start | bytes 5308424 | tf_op jit(solution)/shard_map/ppermute | solution.py:485
  70.5 40.7 %collective-permute-start.10 = (bf16[3,96,3072]{2,1,0:T(8,128)(2,1)}, bf16[3,96,3072]{2,1,0:T(8,128)(2,1)}, u32[]{:S(2)}, u32[]{:S(2)}) collective-permute-start(bf16[3,96,3072]{2,1,0:T(8,128)(2,1)} %dynamic-slice_bitcast_fusion.1), channel_id=1, source_target_pairs={{0,1},{1,0},{2,3},{3,2},{4,5},{5,4},{6,7},{7,6},{8,9},{9,8},{10,11... | collective-permute-start | bytes 5308424 | tf_op jit(solution)/shard_map/ppermute | solution.py:537
  87.5 38.5 %collective-permute-start.8 = (bf16[192,4608]{1,0:T(8,128)(2,1)}, bf16[192,4608]{1,0:T(8,128)(2,1)}, u32[]{:S(2)}, u32[]{:S(2)}) collective-permute-start(bf16[192,4608]{1,0:T(8,128)(2,1)} %collective-permute-done.4.refs_0_), channel_id=1, source_target_pairs={{0,4},{2,6},{4,12},{6,14},{12,20},{14,22},{20,28},{22,30},{28,24},... | collective-permute-start | bytes 5308424 | tf_op jit(solution)/shard_map/ppermute | solution.py:481
  89.1 38.0 %collective-permute-start.9 = (bf16[192,4608]{1,0:T(8,128)(2,1)}, bf16[192,4608]{1,0:T(8,128)(2,1)}, u32[]{:S(2)}, u32[]{:S(2)}) collective-permute-start(bf16[192,4608]{1,0:T(8,128)(2,1)} %collective-permute-done.5.refs_2_), channel_id=1, source_target_pairs={{0,8},{2,10},{4,0},{6,2},{12,4},{14,6},{20,12},{22,14},{28,20},{30... | collective-permute-start | bytes 5308424 | tf_op jit(solution)/shard_map/ppermute | solution.py:481
  89.6 42.1 %collective-permute-start.12 = (bf16[192,4608]{1,0:T(8,128)(2,1)}, bf16[192,4608]{1,0:T(8,128)(2,1)}, u32[]{:S(2)}, u32[]{:S(2)}) collective-permute-start(bf16[192,4608]{1,0:T(8,128)(2,1)} %collective-permute-done.4.refs_0_), channel_id=1, source_target_pairs={{0,2},{2,0},{4,6},{6,4},{8,10},{10,8},{12,14},{14,12},{16,18},{18,... | collective-permute-start | bytes 5308424 | tf_op jit(solution)/shard_map/ppermute | solution.py:485
  89.6 43.7 %collective-permute-start.13 = (bf16[192,4608]{1,0:T(8,128)(2,1)}, bf16[192,4608]{1,0:T(8,128)(2,1)}, u32[]{:S(2)}, u32[]{:S(2)}) collective-permute-start(bf16[192,4608]{1,0:T(8,128)(2,1)} %collective-permute-done.5.refs_2_), channel_id=1, source_target_pairs={{0,2},{2,0},{4,6},{6,4},{8,10},{10,8},{12,14},{14,12},{16,18},{18,... | collective-permute-start | bytes 5308424 | tf_op jit(solution)/shard_map/ppermute | solution.py:485
  99.3 14.8 %copy-start = (bf16[576,1536]{1,0:T(8,128)(2,1)S(1)}, bf16[576,1536]{1,0:T(8,128)(2,1)}, u32[]{:S(2)}) copy-start(bf16[576,1536]{1,0:T(8,128)(2,1)} %attend.3.attn_ref) | copy-start | bytes 5308420
  117.8 8.2 %collective-permute-start.11 = (bf16[288,384]{1,0:T(8,128)(2,1)S(1)}, bf16[288,384]{1,0:T(8,128)(2,1)S(1)}, u32[]{:S(2)}, u32[]{:S(2)}) collective-permute-start(bf16[288,384]{1,0:T(8,128)(2,1)S(1)} %project.7), channel_id=1, source_target_pairs={{0,1},{1,0},{2,3},{3,2},{4,5},{5,4},{6,7},{7,6},{8,9},{9,8},{10,11... | collective-permute-start | bytes 663560 | tf_op jit(solution)/shard_map/ppermute | solution.py:556
  126.0 5.6 %copy-start.14 = (bf16[288,768]{1,0:T(8,128)(2,1)}, bf16[288,768]{1,0:T(8,128)(2,1)S(1)}, u32[]{:S(2)}) copy-start(bf16[288,768]{1,0:T(8,128)(2,1)S(1)} %get-tuple-element.99.refs_2_) | copy-start | bytes 1327108
  126.0 5.6 %copy-start.25 = (bf16[288,384]{1,0:T(8,128)(2,1)}, bf16[288,384]{1,0:T(8,128)(2,1)S(1)}, u32[]{:S(2)}) copy-start(bf16[288,384]{1,0:T(8,128)(2,1)S(1)} %collective-permute-done.11.refs_1_) | copy-start | bytes 663556
  127.1 14.4 %collective-permute-start.15 = (bf16[192,4608]{1,0:T(8,128)(2,1)}, bf16[192,4608]{1,0:T(8,128)(2,1)S(1)}, u32[]{:S(2)}, u32[]{:S(2)}) collective-permute-start(bf16[192,4608]{1,0:T(8,128)(2,1)} %collective-permute-done.8.refs_0_), channel_id=1, source_target_pairs={{0,2},{2,0},{4,6},{6,4},{8,10},{10,8},{12,14},{14,12},{16,18},{18,... | collective-permute-start | bytes 5308424 | tf_op jit(solution)/shard_map/ppermute | solution.py:485
  127.1 14.4 %collective-permute-start.16 = (bf16[192,4608]{1,0:T(8,128)(2,1)}, bf16[192,4608]{1,0:T(8,128)(2,1)S(1)}, u32[]{:S(2)}, u32[]{:S(2)}) collective-permute-start(bf16[192,4608]{1,0:T(8,128)(2,1)} %collective-permute-done.9.refs_2_), channel_id=1, source_target_pairs={{0,2},{2,0},{4,6},{6,4},{8,10},{10,8},{12,14},{14,12},{16,18},{18,... | collective-permute-start | bytes 5308424 | tf_op jit(solution)/shard_map/ppermute | solution.py:485
  127.6 13.4 %collective-permute-start.14 = (bf16[288,768]{1,0:T(8,128)(2,1)S(1)}, bf16[288,768]{1,0:T(8,128)(2,1)S(1)}, u32[]{:S(2)}, u32[]{:S(2)}) collective-permute-start(bf16[288,768]{1,0:T(8,128)(2,1)S(1)} %get-tuple-element.87), channel_id=1, source_target_pairs={{0,1},{1,0},{2,3},{3,2},{4,5},{5,4},{6,7},{7,6},{8,9},{9,8},{10,11... | collective-permute-start | bytes 1327112 | tf_op jit(solution)/shard_map/ppermute | solution.py:552
  131.6 21.8 %collective-permute-start.17 = (bf16[96,4608]{1,0:T(8,128)(2,1)S(1)}, bf16[96,4608]{1,0:T(8,128)(2,1)S(1)}, u32[]{:S(2)}, u32[]{:S(2)}) collective-permute-start(bf16[96,4608]{1,0:T(8,128)(2,1)S(1)} %slice.6), channel_id=1, source_target_pairs={{0,4},{2,6},{4,12},{6,14},{12,20},{14,22},{20,28},{22,30},{28,24},... | collective-permute-start | bytes 2654216 | tf_op jit(solution)/shard_map/ppermute | solution.py:481
  133.2 21.0 %collective-permute-start.18 = (bf16[96,4608]{1,0:T(8,128)(2,1)S(1)}, bf16[96,4608]{1,0:T(8,128)(2,1)S(1)}, u32[]{:S(2)}, u32[]{:S(2)}) collective-permute-start(bf16[96,4608]{1,0:T(8,128)(2,1)S(1)} %slice.7), channel_id=1, source_target_pairs={{0,8},{2,10},{4,0},{6,2},{12,4},{14,6},{20,12},{22,14},{28,20},{30... | collective-permute-start | bytes 2654216 | tf_op jit(solution)/shard_map/ppermute | solution.py:481
  140.2 0.8 copy-start.18
  141.0 7.3 %copy-start.16 = (bf16[288,768]{1,0:T(8,128)(2,1)}, bf16[288,768]{1,0:T(8,128)(2,1)S(1)}, u32[]{:S(2)}) copy-start(bf16[288,768]{1,0:T(8,128)(2,1)S(1)} %collective-permute-done.14.refs_3_) | copy-start | bytes 1327108
  141.0 12.4 %collective-permute-start.19 = (bf16[288,768]{1,0:T(8,128)(2,1)S(1)}, bf16[288,768]{1,0:T(8,128)(2,1)S(1)}, u32[]{:S(2)}, u32[]{:S(2)}) collective-permute-start(bf16[288,768]{1,0:T(8,128)(2,1)S(1)} %get-tuple-element.89), channel_id=1, source_target_pairs={{0,1},{1,0},{2,3},{3,2},{4,5},{5,4},{6,7},{7,6},{8,9},{9,8},{10,11... | collective-permute-start | bytes 1327112 | tf_op jit(solution)/shard_map/ppermute | solution.py:552
  148.3 0.8 copy-start.22
  152.7 0.7 copy-start.12
  153.4 7.6 %copy-start.20 = (bf16[288,768]{1,0:T(8,128)(2,1)}, bf16[288,768]{1,0:T(8,128)(2,1)S(1)}, u32[]{:S(2)}) copy-start(bf16[288,768]{1,0:T(8,128)(2,1)S(1)} %collective-permute-done.19.refs_5_) | copy-start | bytes 1327108
  153.4 7.6 %copy-start.3 = (bf16[96,4608]{1,0:T(8,128)(2,1)}, bf16[96,4608]{1,0:T(8,128)(2,1)S(1)}, u32[]{:S(2)}) copy-start(bf16[96,4608]{1,0:T(8,128)(2,1)S(1)} %collective-permute-done.17.refs_0_) | copy-start | bytes 2654212
  154.2 6.7 %copy-start.5 = (bf16[96,4608]{1,0:T(8,128)(2,1)}, bf16[96,4608]{1,0:T(8,128)(2,1)S(1)}, u32[]{:S(2)}) copy-start(bf16[96,4608]{1,0:T(8,128)(2,1)S(1)} %collective-permute-done.18.refs_2_) | copy-start | bytes 2654212
  154.2 7.6 %copy-start.34 = (f32[64]{0:T(128)S(1)}, f32[64]{0:T(128)}, u32[]{:S(2)}) copy-start(f32[64]{0:T(128)} %param.32) | copy-start | bytes 772
  154.2 2.4 %collective-permute-start.21 = (bf16[96,4608]{1,0:T(8,128)(2,1)S(1)}, bf16[96,4608]{1,0:T(8,128)(2,1)S(1)}, u32[]{:S(2)}, u32[]{:S(2)}) collective-permute-start(bf16[96,4608]{1,0:T(8,128)(2,1)S(1)} %collective-permute-done.17.refs_0_), channel_id=1, source_target_pairs={{0,2},{2,0},{4,6},{6,4},{8,10},{10,8},{12,14},{14,12},{16,18},{18,... | collective-permute-start | bytes 2654216 | tf_op jit(solution)/shard_map/ppermute | solution.py:485
  154.2 3.7 %collective-permute-start.22 = (bf16[96,4608]{1,0:T(8,128)(2,1)S(1)}, bf16[96,4608]{1,0:T(8,128)(2,1)S(1)}, u32[]{:S(2)}, u32[]{:S(2)}) collective-permute-start(bf16[96,4608]{1,0:T(8,128)(2,1)S(1)} %collective-permute-done.18.refs_2_), channel_id=1, source_target_pairs={{0,2},{2,0},{4,6},{6,4},{8,10},{10,8},{12,14},{14,12},{16,18},{18,... | collective-permute-start | bytes 2654216 | tf_op jit(solution)/shard_map/ppermute | solution.py:485
  154.8 17.1 %collective-permute-start.20 = (bf16[288,768]{1,0:T(8,128)(2,1)}, bf16[288,768]{1,0:T(8,128)(2,1)}, u32[]{:S(2)}, u32[]{:S(2)}) collective-permute-start(bf16[288,768]{1,0:T(8,128)(2,1)} %get-tuple-element.94), channel_id=1, source_target_pairs={{0,1},{1,0},{2,3},{3,2},{4,5},{5,4},{6,7},{7,6},{8,9},{9,8},{10,11... | collective-permute-start | bytes 1327112 | tf_op jit(solution)/shard_map/ppermute | solution.py:552
  156.7 4.3 %copy-start.7 = (bf16[96,4608]{1,0:T(8,128)(2,1)}, bf16[96,4608]{1,0:T(8,128)(2,1)S(1)}, u32[]{:S(2)}) copy-start(bf16[96,4608]{1,0:T(8,128)(2,1)S(1)} %collective-permute-done.21.refs_1_) | copy-start | bytes 2654212
  157.9 3.1 %copy-start.9 = (bf16[96,4608]{1,0:T(8,128)(2,1)}, bf16[96,4608]{1,0:T(8,128)(2,1)S(1)}, u32[]{:S(2)}) copy-start(bf16[96,4608]{1,0:T(8,128)(2,1)S(1)} %collective-permute-done.22.refs_3_) | copy-start | bytes 2654212
  161.0 10.9 %collective-permute-start.23 = (bf16[288,384]{1,0:T(8,128)(2,1)}, bf16[288,384]{1,0:T(8,128)(2,1)}, u32[]{:S(2)}, u32[]{:S(2)}) collective-permute-start(bf16[288,384]{1,0:T(8,128)(2,1)} %project.12), channel_id=1, source_target_pairs={{0,1},{1,0},{2,3},{3,2},{4,5},{5,4},{6,7},{7,6},{8,9},{9,8},{10,11... | collective-permute-start | bytes 663560 | tf_op jit(solution)/shard_map/ppermute | solution.py:572
  163.2 1.5 copy-start.1
  164.7 1.2 copy-start.4
  165.9 1.2 copy-start.6
  167.0 1.2 copy-start.8
  168.2 1.2 copy-start.10
  169.4 2.6 %copy-start.11 = (bf16[1,3,96,3072]{3,2,1,0:T(8,128)(2,1)S(1)}, bf16[1,3,96,3072]{3,2,1,0:T(8,128)(2,1)}, u32[]{:S(2)}) copy-start(bf16[1,3,96,3072]{3,2,1,0:T(8,128)(2,1)} %param.21) | copy-start | bytes 5308420
  169.4 2.6 %copy-start.13 = (bf16[288,384]{1,0:T(8,128)(2,1)S(1)}, bf16[288,384]{1,0:T(8,128)(2,1)}, u32[]{:S(2)}) copy-start(bf16[288,384]{1,0:T(8,128)(2,1)} %copy-done.12) | copy-start | bytes 663556
  169.4 2.6 %copy-start.15 = (bf16[288,768]{1,0:T(8,128)(2,1)S(1)}, bf16[288,768]{1,0:T(8,128)(2,1)}, u32[]{:S(2)}) copy-start(bf16[288,768]{1,0:T(8,128)(2,1)} %copy-done.14) | copy-start | bytes 1327108
  169.4 2.6 %copy-start.17 = (bf16[288,768]{1,0:T(8,128)(2,1)S(1)}, bf16[288,768]{1,0:T(8,128)(2,1)}, u32[]{:S(2)}) copy-start(bf16[288,768]{1,0:T(8,128)(2,1)} %copy-done.16) | copy-start | bytes 1327108
  169.4 2.6 %copy-start.19 = (bf16[288,768]{1,0:T(8,128)(2,1)S(1)}, bf16[288,768]{1,0:T(8,128)(2,1)}, u32[]{:S(2)}) copy-start(bf16[288,768]{1,0:T(8,128)(2,1)} %copy-done.18) | copy-start | bytes 1327108
  169.4 2.6 %copy-start.21 = (bf16[288,768]{1,0:T(8,128)(2,1)S(1)}, bf16[288,768]{1,0:T(8,128)(2,1)}, u32[]{:S(2)}) copy-start(bf16[288,768]{1,0:T(8,128)(2,1)} %copy-done.20) | copy-start | bytes 1327108
  169.4 2.6 %copy-start.23 = (bf16[288,768]{1,0:T(8,128)(2,1)S(1)}, bf16[288,768]{1,0:T(8,128)(2,1)}, u32[]{:S(2)}) copy-start(bf16[288,768]{1,0:T(8,128)(2,1)} %copy-done.22) | copy-start | bytes 1327108
  169.4 2.6 %copy-start.24 = (bf16[3072,64]{0,1:T(8,128)(2,1)S(1)}, bf16[3072,64]{0,1:T(8,128)(2,1)}, u32[]{:S(2)}) copy-start(bf16[3072,64]{0,1:T(8,128)(2,1)} %param.31) | copy-start | bytes 1179652
  169.4 2.6 %copy-start.26 = (bf16[288,384]{1,0:T(8,128)(2,1)S(1)}, bf16[288,384]{1,0:T(8,128)(2,1)}, u32[]{:S(2)}) copy-start(bf16[288,384]{1,0:T(8,128)(2,1)} %copy-done.25) | copy-start | bytes 663556
  169.4 2.6 %copy-start.27 = (f32[64,1]{1,0:T(8,128)S(1)}, f32[64,1]{1,0:T(8,128)}, u32[]{:S(2)}) copy-start(f32[64,1]{1,0:T(8,128)} %copy.23.refs_16_) | copy-start | bytes 772
  169.4 2.6 %copy-start.28 = (f32[1,2,96,64]{2,3,1,0:T(8,128)S(1)}, f32[1,2,96,64]{2,3,1,0:T(8,128)}, u32[]{:S(2)}) copy-start(f32[1,2,96,64]{2,3,1,0:T(8,128)} %param.33) | copy-start | bytes 147460
  169.4 2.6 %copy-start.29 = (f32[3072]{0:T(1024)S(1)}, f32[3072]{0:T(1024)}, u32[]{:S(2)}) copy-start(f32[3072]{0:T(1024)} %param.27) | copy-start | bytes 36868
  169.5 2.6 %copy-start.30 = (f32[1,3072]{1,0:T(1,128)S(1)}, f32[1,3072]{1,0:T(1,128)}, u32[]{:S(2)}) copy-start(f32[1,3072]{1,0:T(1,128)} %refs_12_.1) | copy-start | bytes 36868
  169.5 2.6 %copy-start.31 = (f32[1,3072]{1,0:T(1,128)S(1)}, f32[1,3072]{1,0:T(1,128)}, u32[]{:S(2)}) copy-start(f32[1,3072]{1,0:T(1,128)} %refs_13_.1) | copy-start | bytes 36868
  169.5 2.6 %copy-start.32 = (f32[1,3072]{1,0:T(1,128)S(1)}, f32[1,3072]{1,0:T(1,128)}, u32[]{:S(2)}) copy-start(f32[1,3072]{1,0:T(1,128)} %refs_14_.1) | copy-start | bytes 36868
  169.5 2.6 %copy-start.33 = (s32[16]{0:T(128)S(1)}, s32[16]{0:T(128)}, u32[]{:S(2)}) copy-start(s32[16]{0:T(128)} %constant.41.clone.place_ref) | copy-start | bytes 196
